TPU v7x, 32 devices: a whole 2x2x4 slice. The times are simulated.
32 devices in a mesh: dp: 8 (over z, x), fsdp: 4 (over y, core).
Axes of the slice: x: 2, y: 2, z: 4, core: 2. Of those that a mesh axis runs over, the one named last changes fastest.
Arguments:
- inputs: float32 [8192, 768], P(('dp', 'fsdp')), may hold values from -6 to 6
- lengths: int32 [32, 2], P(('dp', 'fsdp')), may hold values from 0 to 256, as said below
- in_projection: bfloat16 [2, 768, 2304], P(None, 'dp', 'fsdp'), may hold values from -0.21875 to 0.21875
- out_projection: bfloat16 [2, 768, 768], P(None, 'dp', 'fsdp'), may hold values from -0.21875 to 0.21875
- up_weight: bfloat16 [2, 768, 3072], P(None, 'dp', 'fsdp'), may hold values from -0.21875 to 0.21875
- down_weight: bfloat16 [2, 3072, 768], P(None, 'dp', 'fsdp'), may hold values from -0.109375 to 0.109375
- norm_gains: bfloat16 [2, 3, 768], P(None, None, 'dp'), may hold values from 0.5 to 1.5
- biases: bfloat16 [2, 7, 768], P(None, None, 'dp'), may hold values from -3 to 3
- hidden_gains: bfloat16 [2, 1, 3072], P(None, None, 'dp'), may hold values from 0.5 to 1.5
- hidden_biases: bfloat16 [2, 2, 3072], P(None, None, 'dp'), may hold values from -3 to 3
- cotangent: float32 [8192, 768], P(('dp', 'fsdp')), may hold values from -6 to 6
Outputs:
- outputs: float32 [8192, 768], P(('dp', 'fsdp'))
- input_gradient: float32 [8192, 768], P(('dp', 'fsdp'))
- in_projection_gradient: float32 [2, 768, 2304], P(None, 'dp', 'fsdp')
- out_projection_gradient: float32 [2, 768, 768], P(None, 'dp', 'fsdp')
- up_weight_gradient: float32 [2, 768, 3072], P(None, 'dp', 'fsdp')
- down_weight_gradient: float32 [2, 3072, 768], P(None, 'dp', 'fsdp')
- norm_gains_gradient: float32 [2, 3, 768], P(None, None, 'dp')
- biases_gradient: float32 [2, 7, 768], P(None, None, 'dp')
- hidden_gains_gradient: float32 [2, 1, 3072], P(None, None, 'dp')
- hidden_biases_gradient: float32 [2, 2, 3072], P(None, None, 'dp')
Inputs may be any that keep to these rules, and one draw needn't show every extreme that they name: Row r lists the lengths of the 2 sequences packed in order from the first of device r's 256 token slots (devices in the order dp then fsdp); the slots after them are padding. A row sums to at most 256 and to at least 126. 0 marks an empty sequence slot; a nonempty sequence has 64 tokens or more; in every draw some device holds one sequence of 256 tokens.
All inputs are finite; a program needn't handle non-finite values.
Results may differ from a plain program's by a relative error of at most 0.018.
Values may be sent and summed in bfloat16 or wider, within the bound.
No kernel may reach another device: no remote copies, remote signals or barrier semaphores. Data moves between devices by JAX's collectives and lax.ppermute only.
A program may use at most 192 MiB of HBM per device.

v0:
```python
import math

import jax
import jax.numpy as jnp
from jax import lax
from jax.sharding import PartitionSpec as P

HEADS = 12
HEAD_DIM = 64
LAYERS = 2
SEQS_DEV = 2


epsilon = 1e-05
block_limit = 512


def segments(lengths, count_rows):
    ends = jnp.cumsum(lengths, axis=-1)
    places = jnp.arange(count_rows, dtype=jnp.int32)
    return jnp.sum((places[:, None] >= ends[0][None, :]).astype(jnp.int32), axis=1)


def layer_norm(values, gain_row, shift_row):
    mean_value = jnp.mean(values, axis=-1, keepdims=True)
    centred = values - mean_value
    variance = jnp.mean(centred * centred, axis=-1, keepdims=True)
    inv_root = lax.rsqrt(variance + epsilon)
    normed = centred * inv_root
    return (normed * gain_row + shift_row, normed, inv_root)


def norm_backward(upstream, gain_row, normed, inv_root):
    scaled = upstream * gain_row
    inner_sum = (
        scaled
        - jnp.mean(scaled, axis=-1, keepdims=True)
        - normed * jnp.mean(scaled * normed, axis=-1, keepdims=True)
    )
    return (inv_root * inner_sum, jnp.sum(upstream * normed, axis=0), jnp.sum(upstream, axis=0))


def gelu_value(values):
    return 0.5 * values * (1.0 + lax.erf(values * (1.0 / math.sqrt(2.0))))


def gelu_slope(values):
    cumulative = 0.5 * (1.0 + lax.erf(values * (1.0 / math.sqrt(2.0))))
    density = jnp.exp(-0.5 * values * values) * (1.0 / math.sqrt(2.0 * math.pi))
    return cumulative + values * density


def attend_forward(query_rows, key_rows, value_rows, segment_ids):
    count_rows = query_rows.shape[0]
    split_shape = (count_rows, HEADS, HEAD_DIM)
    query_heads = query_rows.reshape(split_shape)
    key_heads = key_rows.reshape(split_shape)
    value_heads = value_rows.reshape(split_shape)
    block_rows = min(count_rows, block_limit)
    block_count = count_rows // block_rows
    score_scale = 1.0 / math.sqrt(HEAD_DIM)

    def one_block(block_index):
        scores = (
            jnp.einsum("qhd,khd->hqk", query_heads, key_heads, preferred_element_type=jnp.float32)
            * score_scale
        )
        same_doc = segment_ids[:, None] == segment_ids[None, :]
        scores = jnp.where(same_doc[None], scores, -1e30)
        row_max = jnp.max(scores, axis=-1, keepdims=True)
        exponent = jnp.exp(scores - row_max)
        row_total = jnp.sum(exponent, axis=-1, keepdims=True)
        weights = (exponent / row_total).astype(jnp.bfloat16)
        mixed_block = jnp.einsum(
            "hqk,khd->qhd", weights, value_heads, preferred_element_type=jnp.float32
        )
        return (mixed_block, (row_max + jnp.log(row_total))[..., 0])

    mixed_blocks, log_totals = lax.map(one_block, jnp.arange(block_count))
    return (mixed_blocks.reshape(count_rows, HEADS * HEAD_DIM), log_totals)


def attend_backward(query_rows, key_rows, value_rows, segment_ids, log_totals, mixed_grad):
    count_rows = query_rows.shape[0]
    split_shape = (count_rows, HEADS, HEAD_DIM)
    query_heads = query_rows.reshape(split_shape)
    key_heads = key_rows.reshape(split_shape)
    value_heads = value_rows.reshape(split_shape)
    grad_heads = mixed_grad.reshape(split_shape)
    block_rows = min(count_rows, block_limit)
    block_count = count_rows // block_rows
    score_scale = 1.0 / math.sqrt(HEAD_DIM)

    def one_block(carry, block_index):
        key_grad, value_grad = carry
        scores = (
            jnp.einsum("qhd,khd->hqk", query_heads, key_heads, preferred_element_type=jnp.float32)
            * score_scale
        )
        same_doc = segment_ids[:, None] == segment_ids[None, :]
        scores = jnp.where(same_doc[None], scores, -1e30)
        prob_rows = jnp.exp(scores - log_totals[block_index][..., None])
        value_grad = value_grad + jnp.einsum(
            "hqk,qhd->khd",
            prob_rows.astype(jnp.bfloat16),
            grad_heads,
            preferred_element_type=jnp.float32,
        )
        grad_probs = jnp.einsum(
            "qhd,khd->hqk", grad_heads, value_heads, preferred_element_type=jnp.float32
        )
        inner_sum = jnp.sum(prob_rows * grad_probs, axis=-1, keepdims=True)
        grad_scores = (prob_rows * (grad_probs - inner_sum)).astype(jnp.bfloat16)
        query_grad = (
            jnp.einsum("hqk,khd->qhd", grad_scores, key_heads, preferred_element_type=jnp.float32)
            * score_scale
        )
        key_grad = (
            key_grad
            + jnp.einsum(
                "hqk,qhd->khd", grad_scores, query_heads, preferred_element_type=jnp.float32
            )
            * score_scale
        )
        return ((key_grad, value_grad), query_grad)

    zero_heads = jnp.zeros(split_shape, jnp.float32)
    (key_grad, value_grad), query_grad = lax.scan(
        one_block, (zero_heads, zero_heads), jnp.arange(block_count)
    )
    flat_shape = (count_rows, HEADS * HEAD_DIM)
    return (
        query_grad.reshape(flat_shape),
        key_grad.reshape(flat_shape),
        value_grad.reshape(flat_shape),
    )


def fetch_forward(
    layer_index,
    in_projection,
    out_projection,
    up_weight,
    down_weight,
    norm_gains,
    biases,
    hidden_gains,
    hidden_biases,
):
    inner_parts = (
        lax.all_gather(in_projection[layer_index], "fsdp", axis=1, tiled=True),
        lax.all_gather(out_projection[layer_index], "fsdp", axis=1, tiled=True),
        lax.all_gather(up_weight[layer_index], "fsdp", axis=1, tiled=True),
        lax.all_gather(down_weight[layer_index], "fsdp", axis=1, tiled=True),
    )
    return (
        lax.all_gather(inner_parts[0], "dp", axis=0, tiled=True),
        lax.all_gather(inner_parts[1], "dp", axis=0, tiled=True),
        lax.all_gather(inner_parts[2], "dp", axis=0, tiled=True),
        lax.all_gather(inner_parts[3], "dp", axis=0, tiled=True),
        lax.all_gather(norm_gains[layer_index], "dp", axis=1, tiled=True),
        lax.all_gather(biases[layer_index], "dp", axis=1, tiled=True),
        lax.all_gather(hidden_gains[layer_index], "dp", axis=1, tiled=True),
        lax.all_gather(hidden_biases[layer_index], "dp", axis=1, tiled=True),
    )


def fetch_backward(
    layer_index,
    in_projection,
    out_projection,
    up_weight,
    down_weight,
    norm_gains,
    biases,
    hidden_gains,
    hidden_biases,
):
    inner_parts = (
        lax.all_gather(in_projection[layer_index], "fsdp", axis=1, tiled=True),
        lax.all_gather(out_projection[layer_index], "fsdp", axis=1, tiled=True),
        lax.all_gather(up_weight[layer_index], "fsdp", axis=1, tiled=True),
        lax.all_gather(down_weight[layer_index], "fsdp", axis=1, tiled=True),
    )
    return (
        lax.all_gather(inner_parts[0], "dp", axis=0, tiled=True),
        lax.all_gather(inner_parts[1], "dp", axis=0, tiled=True),
        lax.all_gather(inner_parts[2], "dp", axis=0, tiled=True),
        lax.all_gather(inner_parts[3], "dp", axis=0, tiled=True),
        lax.all_gather(norm_gains[layer_index], "dp", axis=1, tiled=True),
        lax.all_gather(biases[layer_index], "dp", axis=1, tiled=True),
        lax.all_gather(hidden_gains[layer_index], "dp", axis=1, tiled=True),
        lax.all_gather(hidden_biases[layer_index], "dp", axis=1, tiled=True),
    )


def layer_forward(stream, fetched, segment_ids):
    in_full, out_full, up_full, down_full, gain_rows, shift_rows, hidden_gain, hidden_shift = (
        fetched
    )
    gain_rows = gain_rows.astype(jnp.float32)
    shift_rows = shift_rows.astype(jnp.float32)
    hidden_gain = hidden_gain.astype(jnp.float32)
    hidden_shift = hidden_shift.astype(jnp.float32)
    model_width = stream.shape[1]
    normed_one, unit_one, inv_one = layer_norm(stream, gain_rows[0], shift_rows[0])
    attn_input = normed_one.astype(jnp.bfloat16)
    projected = jnp.dot(attn_input, in_full, preferred_element_type=jnp.float32)
    query_rows = (projected[:, 0:model_width] + shift_rows[1]).astype(jnp.bfloat16)
    key_rows = projected[:, model_width : 2 * model_width].astype(jnp.bfloat16)
    value_rows = (projected[:, 2 * model_width : 3 * model_width] + shift_rows[2]).astype(
        jnp.bfloat16
    )
    attn_mixed, log_totals = attend_forward(query_rows, key_rows, value_rows, segment_ids)
    normed_two, unit_two, inv_two = layer_norm(attn_mixed, gain_rows[1], shift_rows[3])
    mixed_input = normed_two.astype(jnp.bfloat16)
    middle = stream + (
        jnp.dot(mixed_input, out_full, preferred_element_type=jnp.float32) + shift_rows[4]
    )
    normed_three, unit_three, inv_three = layer_norm(middle, gain_rows[2], shift_rows[5])
    ffn_input = normed_three.astype(jnp.bfloat16)
    hidden_pre = jnp.dot(ffn_input, up_full, preferred_element_type=jnp.float32) + hidden_shift[0]
    normed_four, unit_four, inv_four = layer_norm(
        gelu_value(hidden_pre), hidden_gain[0], hidden_shift[1]
    )
    ffn_hidden = normed_four.astype(jnp.bfloat16)
    result = middle + (
        jnp.dot(ffn_hidden, down_full, preferred_element_type=jnp.float32) + shift_rows[6]
    )
    saved_values = (
        attn_input,
        query_rows,
        key_rows,
        value_rows,
        log_totals,
        unit_one,
        inv_one,
        unit_two,
        inv_two,
        mixed_input,
        unit_three,
        inv_three,
        ffn_input,
        hidden_pre,
        unit_four,
        inv_four,
        ffn_hidden,
    )
    return (result, saved_values)


def layer_backward(stream_grad, fetched, saved_values, segment_ids):
    in_full, out_full, up_full, down_full, gain_rows, shift_rows, hidden_gain, hidden_shift = (
        fetched
    )
    gain_rows = gain_rows.astype(jnp.float32)
    hidden_gain = hidden_gain.astype(jnp.float32)
    (
        attn_input,
        query_rows,
        key_rows,
        value_rows,
        log_totals,
        unit_one,
        inv_one,
        unit_two,
        inv_two,
        mixed_input,
        unit_three,
        inv_three,
        ffn_input,
        hidden_pre,
        unit_four,
        inv_four,
        ffn_hidden,
    ) = saved_values
    model_width = stream_grad.shape[1]
    branch_two = stream_grad.astype(jnp.bfloat16)
    down_bias_grad = jnp.sum(branch_two, axis=0, dtype=jnp.float32)
    down_grad = jnp.einsum("tf,td->fd", ffn_hidden, branch_two, preferred_element_type=jnp.float32)
    hidden_grad = jnp.einsum("td,fd->tf", branch_two, down_full, preferred_element_type=jnp.float32)
    act_grad, hidden_gain_grad, hidden_shift_grad = norm_backward(
        hidden_grad, hidden_gain[0], unit_four, inv_four
    )
    pre_grad = (act_grad * gelu_slope(hidden_pre)).astype(jnp.bfloat16)
    up_bias_grad = jnp.sum(pre_grad, axis=0, dtype=jnp.float32)
    up_grad = jnp.einsum("td,tf->df", ffn_input, pre_grad, preferred_element_type=jnp.float32)
    ffn_in_grad = jnp.einsum("tf,df->td", pre_grad, up_full, preferred_element_type=jnp.float32)
    middle_part, gain_three, shift_three = norm_backward(
        ffn_in_grad, gain_rows[2], unit_three, inv_three
    )
    middle_grad = stream_grad + middle_part
    branch_one = middle_grad.astype(jnp.bfloat16)
    out_bias_grad = jnp.sum(branch_one, axis=0, dtype=jnp.float32)
    out_grad = jnp.einsum("te,td->ed", mixed_input, branch_one, preferred_element_type=jnp.float32)
    mixed_in_grad = jnp.einsum(
        "td,ed->te", branch_one, out_full, preferred_element_type=jnp.float32
    )
    mixed_grad, gain_two, shift_two = norm_backward(mixed_in_grad, gain_rows[1], unit_two, inv_two)
    query_grad, key_grad, value_grad = attend_backward(
        query_rows, key_rows, value_rows, segment_ids, log_totals, mixed_grad.astype(jnp.bfloat16)
    )
    projected_grad = jnp.concatenate(
        [
            query_grad.astype(jnp.bfloat16),
            key_grad.astype(jnp.bfloat16),
            value_grad.astype(jnp.bfloat16),
        ],
        axis=1,
    )
    query_bias_grad = jnp.sum(projected_grad[:, 0:model_width], axis=0, dtype=jnp.float32)
    value_bias_grad = jnp.sum(
        projected_grad[:, 2 * model_width : 3 * model_width], axis=0, dtype=jnp.float32
    )
    in_grad = jnp.einsum(
        "te,tp->ep", attn_input, projected_grad, preferred_element_type=jnp.float32
    )
    attn_in_grad = jnp.einsum(
        "tp,ep->te", projected_grad, in_full, preferred_element_type=jnp.float32
    )
    stream_part, gain_one, shift_one = norm_backward(attn_in_grad, gain_rows[0], unit_one, inv_one)
    input_grad = middle_grad + stream_part
    gradients = (
        in_grad,
        out_grad,
        up_grad,
        down_grad,
        jnp.stack([gain_one, gain_two, gain_three]),
        jnp.stack(
            [
                shift_one,
                query_bias_grad,
                value_bias_grad,
                shift_two,
                out_bias_grad,
                shift_three,
                down_bias_grad,
            ]
        ),
        jnp.stack([hidden_gain_grad]),
        jnp.stack([up_bias_grad, hidden_shift_grad]),
    )
    return (input_grad, gradients)


def reduce_each(gradients):
    outer_parts = (
        lax.psum_scatter(
            gradients[0].astype(jnp.bfloat16), "dp", scatter_dimension=0, tiled=True
        ).astype(jnp.float32),
        lax.psum_scatter(
            gradients[1].astype(jnp.bfloat16), "dp", scatter_dimension=0, tiled=True
        ).astype(jnp.float32),
        lax.psum_scatter(
            gradients[2].astype(jnp.bfloat16), "dp", scatter_dimension=0, tiled=True
        ).astype(jnp.float32),
        lax.psum_scatter(
            gradients[3].astype(jnp.bfloat16), "dp", scatter_dimension=0, tiled=True
        ).astype(jnp.float32),
        lax.psum_scatter(
            gradients[4].astype(jnp.bfloat16), "dp", scatter_dimension=1, tiled=True
        ).astype(jnp.float32),
        lax.psum_scatter(
            gradients[5].astype(jnp.bfloat16), "dp", scatter_dimension=1, tiled=True
        ).astype(jnp.float32),
        lax.psum_scatter(
            gradients[6].astype(jnp.bfloat16), "dp", scatter_dimension=1, tiled=True
        ).astype(jnp.float32),
        lax.psum_scatter(
            gradients[7].astype(jnp.bfloat16), "dp", scatter_dimension=1, tiled=True
        ).astype(jnp.float32),
    )
    inner_parts = (
        lax.psum_scatter(
            outer_parts[0].astype(jnp.bfloat16), "fsdp", scatter_dimension=1, tiled=True
        ).astype(jnp.float32),
        lax.psum_scatter(
            outer_parts[1].astype(jnp.bfloat16), "fsdp", scatter_dimension=1, tiled=True
        ).astype(jnp.float32),
        lax.psum_scatter(
            outer_parts[2].astype(jnp.bfloat16), "fsdp", scatter_dimension=1, tiled=True
        ).astype(jnp.float32),
        lax.psum_scatter(
            outer_parts[3].astype(jnp.bfloat16), "fsdp", scatter_dimension=1, tiled=True
        ).astype(jnp.float32),
    )
    vector_parts = lax.psum(
        (outer_parts[4], outer_parts[5], outer_parts[6], outer_parts[7]), "fsdp"
    )
    return tuple(inner_parts) + tuple(vector_parts)


def shards(
    inputs,
    lengths,
    in_projection,
    out_projection,
    up_weight,
    down_weight,
    norm_gains,
    biases,
    hidden_gains,
    hidden_biases,
    cotangent,
):
    count_rows = inputs.shape[0]
    segment_ids = segments(lengths, count_rows)
    valid_rows = (segment_ids < SEQS_DEV).astype(jnp.float32)[:, None]
    weight_args = (
        in_projection,
        out_projection,
        up_weight,
        down_weight,
        norm_gains,
        biases,
        hidden_gains,
        hidden_biases,
    )
    stream = inputs
    saved_layers = []
    fetched_layers = []
    for layer_index in range(LAYERS):
        fetched = fetch_forward(layer_index, *weight_args)
        stream, saved_values = layer_forward(stream, fetched, segment_ids)
        saved_layers.append(saved_values)
        fetched_layers.append(fetched)
    outputs = stream * valid_rows
    stream_grad = cotangent * valid_rows
    layer_grads = [None] * LAYERS
    for layer_index in reversed(range(LAYERS)):
        fetched = fetch_backward(layer_index, *weight_args)
        stream_grad, gradients = layer_backward(
            stream_grad, fetched, saved_layers[layer_index], segment_ids
        )
        gradients = reduce_each(gradients)
        layer_grads[layer_index] = gradients
    stacked = tuple((jnp.stack([entry[member] for entry in layer_grads]) for member in range(8)))
    return (
        outputs,
        stream_grad,
        stacked[0],
        stacked[1],
        stacked[2],
        stacked[3],
        stacked[4],
        stacked[5],
        stacked[6],
        stacked[7],
    )


def solution(mesh):
    placed = (
        P(("dp", "fsdp"), None),
        P(("dp", "fsdp"), None),
        P(None, "dp", "fsdp"),
        P(None, "dp", "fsdp"),
        P(None, "dp", "fsdp"),
        P(None, "dp", "fsdp"),
        P(None, None, "dp"),
        P(None, None, "dp"),
        P(None, None, "dp"),
        P(None, None, "dp"),
        P(("dp", "fsdp"), None),
    )
    return jax.shard_map(
        shards,
        mesh=mesh,
        in_specs=placed,
        out_specs=(
            P(("dp", "fsdp"), None),
            P(("dp", "fsdp"), None),
            P(None, "dp", "fsdp"),
            P(None, "dp", "fsdp"),
            P(None, "dp", "fsdp"),
            P(None, "dp", "fsdp"),
            P(None, None, "dp"),
            P(None, None, "dp"),
            P(None, None, "dp"),
            P(None, None, "dp"),
        ),
        check_vma=False,
    )
```

profile of v0, /device:TPU:0, one launch (start us, length us, event | category | flops | bytes accessed | tf_op | source)
XLA Modules:
  0.0 2014.6 jit_solution(6786383253257632922)
XLA Ops:
  86.3 26.3 %all-gather.20 = bf16[1,2,3072]{2,1,0:T(2,128)(2,1)S(1)} all-gather(bf16[1,2,384]{2,1,0:T(2,128)(2,1)S(1)} %get-tuple-element.256), channel_id=22, replica_groups=mesh['dp'=8,'fsdp'=4] {'dp'}, dimensions={2}, use_global_device_ids=true | all-gather | bytes 13824 | tf_op jit(solution)/shard_map/all_gather | solution.py:164
  112.6 26.0 %all-gather.21 = bf16[1,1,3072]{2,0,1:T(2,128)(2,1)S(1)} all-gather(bf16[1,1,384]{2,0,1:T(2,128)(2,1)S(1)} %get-tuple-element.258), channel_id=23, replica_groups=mesh['dp'=8,'fsdp'=4] {'dp'}, dimensions={2}, use_global_device_ids=true | all-gather | bytes 6912 | tf_op jit(solution)/shard_map/all_gather | solution.py:163
  138.6 26.4 %all-gather.8 = bf16[1,2,3072]{2,1,0:T(2,128)(2,1)S(1)} all-gather(bf16[1,2,384]{2,1,0:T(2,128)(2,1)S(1)} %get-tuple-element.257), channel_id=10, replica_groups=mesh['dp'=8,'fsdp'=4] {'dp'}, dimensions={2}, use_global_device_ids=true | all-gather | bytes 13824 | tf_op jit(solution)/shard_map/all_gather | solution.py:164
  165.0 26.5 %all-gather.9 = bf16[1,1,3072]{2,0,1:T(2,128)(2,1)S(1)} all-gather(bf16[1,1,384]{2,0,1:T(2,128)(2,1)S(1)} %get-tuple-element.259), channel_id=11, replica_groups=mesh['dp'=8,'fsdp'=4] {'dp'}, dimensions={2}, use_global_device_ids=true | all-gather | bytes 6912 | tf_op jit(solution)/shard_map/all_gather | solution.py:163
  193.8 32.0 %all-gather = bf16[1,3,768]{1,0,2:T(2,128)(2,1)S(1)} all-gather(bf16[1,3,96]{1,0,2:T(2,128)(2,1)S(1)} %copy.200), channel_id=2, replica_groups=mesh['dp'=8,'fsdp'=4] {'dp'}, dimensions={2}, use_global_device_ids=true | all-gather | bytes 5184 | tf_op jit(solution)/shard_map/all_gather | solution.py:161
  233.9 32.4 %all-gather.1 = bf16[1,7,768]{1,0,2:T(2,128)(2,1)S(1)} all-gather(bf16[1,7,96]{1,0,2:T(2,128)(2,1)S(1)} %copy.201), channel_id=3, replica_groups=mesh['dp'=8,'fsdp'=4] {'dp'}, dimensions={2}, use_global_device_ids=true | all-gather | bytes 12096 | tf_op jit(solution)/shard_map/all_gather | solution.py:162
  283.8 32.5 %all-gather.12 = bf16[1,3,768]{1,0,2:T(2,128)(2,1)S(1)} all-gather(bf16[1,3,96]{1,0,2:T(2,128)(2,1)S(1)} %copy.204), channel_id=14, replica_groups=mesh['dp'=8,'fsdp'=4] {'dp'}, dimensions={2}, use_global_device_ids=true | all-gather | bytes 5184 | tf_op jit(solution)/shard_map/all_gather | solution.py:161
  324.9 32.7 %all-gather.13 = bf16[1,7,768]{1,0,2:T(2,128)(2,1)S(1)} all-gather(bf16[1,7,96]{1,0,2:T(2,128)(2,1)S(1)} %copy.205), channel_id=15, replica_groups=mesh['dp'=8,'fsdp'=4] {'dp'}, dimensions={2}, use_global_device_ids=true | all-gather | bytes 12096 | tf_op jit(solution)/shard_map/all_gather | solution.py:162
  428.1 70.7 %all-gather.45.cloned.1.call-done = bf16[1,768,3072]{2,1,0:T(8,128)(2,1)} async-done(((bf16[1,96,3072]{2,1,0:T(8,128)(2,1)}), bf16[1,768,3072]{2,1,0:T(8,128)(2,1)}) %all-gather.45.cloned.1.call-update) | async-done | bytes 4718608 | tf_op jit(solution)/shard_map/all_gather | solution.py:159
  508.3 71.8 %all-gather.47.cloned.1.call-done = bf16[1,3072,768]{1,2,0:T(8,128)(2,1)} async-done(((bf16[1,384,768]{1,2,0:T(8,128)(2,1)}), bf16[1,3072,768]{1,2,0:T(8,128)(2,1)}) %all-gather.47.cloned.1.call-update) | async-done | bytes 4718608 | tf_op jit(solution)/shard_map/all_gather | solution.py:160
  700.3 40.8 %reduce-scatter.57.cloned.1.call-done = bf16[96,768]{1,0:T(8,128)(2,1)} async-done(((bf16[768,768]{1,0:T(8,128)(2,1)}), bf16[96,768]{1,0:T(8,128)(2,1)}) %reduce-scatter.57.cloned.1.call-update) | async-done | bytes 147472 | tf_op jit(solution)/shard_map/reduce_scatter | solution.py:351
  743.0 80.0 %reduce-scatter.55.cloned.1.call-done = bf16[96,2304]{1,0:T(8,128)(2,1)} async-done(((bf16[768,2304]{1,0:T(8,128)(2,1)}), bf16[96,2304]{1,0:T(8,128)(2,1)}) %reduce-scatter.55.cloned.1.call-update) | async-done | bytes 442384 | tf_op jit(solution)/shard_map/reduce_scatter | solution.py:348
  825.2 79.8 %reduce-scatter.53.cloned.1.call-done = bf16[96,2304]{1,0:T(8,128)(2,1)} async-done(((bf16[768,2304]{1,0:T(8,128)(2,1)}), bf16[96,2304]{1,0:T(8,128)(2,1)}) %reduce-scatter.53.cloned.1.call-update) | async-done | bytes 442384 | tf_op jit(solution)/shard_map/reduce_scatter | solution.py:348
  907.2 96.4 %reduce-scatter.71.cloned.1.call-done = bf16[384,768]{1,0:T(8,128)(2,1)} async-done(((bf16[3072,768]{1,0:T(8,128)(2,1)}), bf16[384,768]{1,0:T(8,128)(2,1)}) %reduce-scatter.71.cloned.1.call-update) | async-done | bytes 589840 | tf_op jit(solution)/shard_map/reduce_scatter | solution.py:357
  1005.9 96.5 %reduce-scatter.69.cloned.1.call-done = bf16[384,768]{1,0:T(8,128)(2,1)} async-done(((bf16[3072,768]{1,0:T(8,128)(2,1)}), bf16[384,768]{1,0:T(8,128)(2,1)}) %reduce-scatter.69.cloned.1.call-update) | async-done | bytes 589840 | tf_op jit(solution)/shard_map/reduce_scatter | solution.py:357
  1112.3 54.0 %reduce-scatter.87.cloned.1.call-done = bf16[96,3]{1,0:T(8,128)(2,1)} async-done(((bf16[768,3]{1,0:T(8,128)(2,1)}), bf16[96,3]{1,0:T(8,128)(2,1)}) %reduce-scatter.87.cloned.1.call-update) | async-done | bytes 592
  1167.1 97.2 %reduce-scatter.65.cloned.1.call-done = bf16[96,3072]{1,0:T(8,128)(2,1)} async-done(((bf16[768,3072]{1,0:T(8,128)(2,1)}), bf16[96,3072]{1,0:T(8,128)(2,1)}) %reduce-scatter.65.cloned.1.call-update) | async-done | bytes 589840 | tf_op jit(solution)/shard_map/reduce_scatter | solution.py:354
  1264.4 63.9 %reduce-scatter.85.cloned.1.call-done = bf16[96,3]{1,0:T(8,128)(2,1)} async-done(((bf16[768,3]{1,0:T(8,128)(2,1)}), bf16[96,3]{1,0:T(8,128)(2,1)}) %reduce-scatter.85.cloned.1.call-update) | async-done | bytes 592
  1329.1 63.8 %reduce-scatter.95.cloned.1.call-done = bf16[384,1]{1,0:T(8,128)(2,1)} async-done(((bf16[3072,1]{1,0:T(8,128)(2,1)}), bf16[384,1]{1,0:T(8,128)(2,1)}) %reduce-scatter.95.cloned.1.call-update) | async-done | bytes 784
  1393.9 64.1 %reduce-scatter.93.cloned.1.call-done = bf16[384,1]{1,0:T(8,128)(2,1)} async-done(((bf16[3072,1]{1,0:T(8,128)(2,1)}), bf16[384,1]{1,0:T(8,128)(2,1)}) %reduce-scatter.93.cloned.1.call-update) | async-done | bytes 784
  1459.0 62.1 %reduce-scatter.91.cloned.1.call-done = bf16[96,7]{1,0:T(8,128)(2,1)} async-done(((bf16[768,7]{1,0:T(8,128)(2,1)}), bf16[96,7]{1,0:T(8,128)(2,1)}) %reduce-scatter.91.cloned.1.call-update) | async-done | bytes 1360
  1521.9 62.6 %reduce-scatter.89.cloned.1.call-done = bf16[96,7]{1,0:T(8,128)(2,1)} async-done(((bf16[768,7]{1,0:T(8,128)(2,1)}), bf16[96,7]{1,0:T(8,128)(2,1)}) %reduce-scatter.89.cloned.1.call-update) | async-done | bytes 1360
  1585.4 64.1 %reduce-scatter.99.cloned.1.call-done = bf16[384,2]{1,0:T(8,128)(2,1)} async-done(((bf16[3072,2]{1,0:T(8,128)(2,1)}), bf16[384,2]{1,0:T(8,128)(2,1)}) %reduce-scatter.99.cloned.1.call-update) | async-done | bytes 1552
  1650.4 64.1 %reduce-scatter.97.cloned.1.call-done = bf16[384,2]{1,0:T(8,128)(2,1)} async-done(((bf16[3072,2]{1,0:T(8,128)(2,1)}), bf16[384,2]{1,0:T(8,128)(2,1)}) %reduce-scatter.97.cloned.1.call-update) | async-done | bytes 1552
  1715.4 96.9 %reduce-scatter.61.cloned.1.call-done = bf16[96,3072]{1,0:T(8,128)(2,1)} async-done(((bf16[768,3072]{1,0:T(8,128)(2,1)}), bf16[96,3072]{1,0:T(8,128)(2,1)}) %reduce-scatter.61.cloned.1.call-update) | async-done | bytes 589840 | tf_op jit(solution)/shard_map/reduce_scatter | solution.py:354
  1835.8 21.7 %reduce-scatter.77.cloned.1.call-done = bf16[192,96]{1,0:T(8,128)(2,1)} async-done(((bf16[768,96]{1,0:T(8,128)(2,1)}), bf16[192,96]{1,0:T(8,128)(2,1)}) %reduce-scatter.77.cloned.1.call-update) | async-done | bytes 36880
  1859.1 23.4 %reduce-scatter.75.cloned.1.call-done = bf16[576,96]{1,0:T(8,128)(2,1)} async-done(((bf16[2304,96]{1,0:T(8,128)(2,1)}), bf16[576,96]{1,0:T(8,128)(2,1)}) %reduce-scatter.75.cloned.1.call-update) | async-done | bytes 110608
  1883.5 24.1 %reduce-scatter.73.cloned.1.call-done = bf16[576,96]{1,0:T(8,128)(2,1)} async-done(((bf16[2304,96]{1,0:T(8,128)(2,1)}), bf16[576,96]{1,0:T(8,128)(2,1)}) %reduce-scatter.73.cloned.1.call-update) | async-done | bytes 110608
  1909.5 22.7 %reduce-scatter.83.cloned.1.call-done = bf16[192,384]{1,0:T(8,128)(2,1)} async-done(((bf16[768,384]{1,0:T(8,128)(2,1)}), bf16[192,384]{1,0:T(8,128)(2,1)}) %reduce-scatter.83.cloned.1.call-update) | async-done | bytes 147472
  1933.3 23.4 %reduce-scatter.81.cloned.1.call-done = bf16[192,384]{1,0:T(8,128)(2,1)} async-done(((bf16[768,384]{1,0:T(8,128)(2,1)}), bf16[192,384]{1,0:T(8,128)(2,1)}) %reduce-scatter.81.cloned.1.call-update) | async-done | bytes 147472
  1959.0 22.4 %reduce-scatter.67.cloned.1.call-done = bf16[96,768]{1,0:T(8,128)(2,1)} async-done(((bf16[96,3072]{1,0:T(8,128)(2,1)}), bf16[96,768]{1,0:T(8,128)(2,1)}) %reduce-scatter.67.cloned.1.call-update) | async-done | bytes 147472 | tf_op jit(solution)/shard_map/reduce_scatter | solution.py:380
  1981.4 24.6 %reduce-scatter.63.cloned.1.call-done = bf16[96,768]{1,0:T(8,128)(2,1)} async-done(((bf16[96,3072]{1,0:T(8,128)(2,1)}), bf16[96,768]{1,0:T(8,128)(2,1)}) %reduce-scatter.63.cloned.1.call-update) | async-done | bytes 147472 | tf_op jit(solution)/shard_map/reduce_scatter | solution.py:380
  (648 shorter events, 371.7 us)
Async XLA Ops:
  7.2 369.7 %all-gather.33.cloned.1.call-start = ((), (), s32[]{:S(2)}) async-start(), calls=%async_computation.34 | async-start | bytes 3981312 | tf_op jit(solution)/shard_map/all_gather | solution.py:157
  23.1 365.4 %all-gather.35.cloned.1.call-start = ((), (), s32[]{:S(2)}) async-start(), calls=%async_computation.35 | async-start | bytes 1327104 | tf_op jit(solution)/shard_map/all_gather | solution.py:158
  30.8 361.3 %all-gather.37.cloned.1.call-start = ((), (), s32[]{:S(2)}) async-start(), calls=%async_computation.36 | async-start | bytes 5308416 | tf_op jit(solution)/shard_map/all_gather | solution.py:159
  39.1 361.8 %all-gather.39.cloned.1.call-start = ((), (), s32[]{:S(2)}) async-start(), calls=%async_computation.37 | async-start | bytes 5308416 | tf_op jit(solution)/shard_map/all_gather | solution.py:160
  47.3 360.1 %all-gather.41.cloned.1.call-start = ((), (), s32[]{:S(2)}) async-start(), calls=%async_computation.38 | async-start | bytes 3981312 | tf_op jit(solution)/shard_map/all_gather | solution.py:157
  60.7 363.8 %all-gather.43.cloned.1.call-start = ((), (), s32[]{:S(2)}) async-start(), calls=%async_computation.39 | async-start | bytes 1327104 | tf_op jit(solution)/shard_map/all_gather | solution.py:158
  68.4 430.4 %all-gather.45.cloned.1.call-start = ((), (), s32[]{:S(2)}) async-start(), calls=%async_computation.40 | async-start | bytes 5308416 | tf_op jit(solution)/shard_map/all_gather | solution.py:159
  76.6 503.5 %all-gather.47.cloned.1.call-start = ((), (), s32[]{:S(2)}) async-start(), calls=%async_computation.41 | async-start | bytes 5308416 | tf_op jit(solution)/shard_map/all_gather | solution.py:160
  84.7 613.8 %reduce-scatter.59.cloned.1.call-start = ((), (), s32[]{:S(2)}) async-start(), calls=%async_computation.27 | async-start | bytes 1327104 | tf_op jit(solution)/shard_map/reduce_scatter | solution.py:351
  612.4 128.8 %reduce-scatter.57.cloned.1.call-start = ((), (), s32[]{:S(2)}) async-start(), calls=%async_computation.26 | async-start | bytes 1327104 | tf_op jit(solution)/shard_map/reduce_scatter | solution.py:351
  634.2 188.8 %reduce-scatter.55.cloned.1.call-start = ((), (), s32[]{:S(2)}) async-start(), calls=%async_computation.25 | async-start | bytes 3981312 | tf_op jit(solution)/shard_map/reduce_scatter | solution.py:348
  638.8 266.2 %reduce-scatter.53.cloned.1.call-start = ((), (), s32[]{:S(2)}) async-start(), calls=%async_computation.24 | async-start | bytes 3981312 | tf_op jit(solution)/shard_map/reduce_scatter | solution.py:348
  655.2 348.4 %reduce-scatter.71.cloned.1.call-start = ((), (), s32[]{:S(2)}) async-start(), calls=%async_computation.33 | async-start | bytes 5308416 | tf_op jit(solution)/shard_map/reduce_scatter | solution.py:357
  661.8 440.5 %reduce-scatter.69.cloned.1.call-start = ((), (), s32[]{:S(2)}) async-start(), calls=%async_computation.32 | async-start | bytes 5308416 | tf_op jit(solution)/shard_map/reduce_scatter | solution.py:357
  668.6 497.8 %reduce-scatter.87.cloned.1.call-start = ((), (), s32[]{:S(2)}) async-start(), calls=%async_computation.49 | async-start | bytes 221184
  670.1 594.2 %reduce-scatter.65.cloned.1.call-start = ((), (), s32[]{:S(2)}) async-start(), calls=%async_computation.30 | async-start | bytes 5308416 | tf_op jit(solution)/shard_map/reduce_scatter | solution.py:354
  675.6 652.6 %reduce-scatter.85.cloned.1.call-start = ((), (), s32[]{:S(2)}) async-start(), calls=%async_computation.48 | async-start | bytes 221184
  683.3 709.6 %reduce-scatter.95.cloned.1.call-start = ((), (), s32[]{:S(2)}) async-start(), calls=%async_computation.53 | async-start | bytes 884736
  685.5 772.5 %reduce-scatter.93.cloned.1.call-start = ((), (), s32[]{:S(2)}) async-start(), calls=%async_computation.52 | async-start | bytes 884736
  687.7 833.4 %reduce-scatter.91.cloned.1.call-start = ((), (), s32[]{:S(2)}) async-start(), calls=%async_computation.51 | async-start | bytes 221184
  688.9 895.6 %reduce-scatter.89.cloned.1.call-start = ((), (), s32[]{:S(2)}) async-start(), calls=%async_computation.50 | async-start | bytes 221184
  690.2 959.2 %reduce-scatter.99.cloned.1.call-start = ((), (), s32[]{:S(2)}) async-start(), calls=%async_computation.55 | async-start | bytes 884736
  691.6 1022.9 %reduce-scatter.97.cloned.1.call-start = ((), (), s32[]{:S(2)}) async-start(), calls=%async_computation.54 | async-start | bytes 884736
  692.9 1119.4 %reduce-scatter.61.cloned.1.call-start = ((), (), s32[]{:S(2)}) async-start(), calls=%async_computation.28 | async-start | bytes 5308416 | tf_op jit(solution)/shard_map/reduce_scatter | solution.py:354
  698.5 1136.4 %reduce-scatter.79.cloned.1.call-start = ((), (), s32[]{:S(2)}) async-start(), calls=%async_computation.45 | async-start | bytes 245760
  700.3 1157.2 %reduce-scatter.77.cloned.1.call-start = ((), (), s32[]{:S(2)}) async-start(), calls=%async_computation.44 | async-start | bytes 245760
  742.9 1139.6 %reduce-scatter.75.cloned.1.call-start = ((), (), s32[]{:S(2)}) async-start(), calls=%async_computation.43 | async-start | bytes 737280
  825.1 1082.5 %reduce-scatter.73.cloned.1.call-start = ((), (), s32[]{:S(2)}) async-start(), calls=%async_computation.42 | async-start | bytes 737280
  907.2 1025.1 %reduce-scatter.83.cloned.1.call-start = ((), (), s32[]{:S(2)}) async-start(), calls=%async_computation.47 | async-start | bytes 737280
  1005.8 950.9 %reduce-scatter.81.cloned.1.call-start = ((), (), s32[]{:S(2)}) async-start(), calls=%async_computation.46 | async-start | bytes 737280
  1104.5 876.9 %reduce-scatter.67.cloned.1.call-start = ((), (), s32[]{:S(2)}) async-start(), calls=%async_computation.31 | async-start | bytes 737280 | tf_op jit(solution)/shard_map/reduce_scatter | solution.py:380
  1264.3 741.7 %reduce-scatter.63.cloned.1.call-start = ((), (), s32[]{:S(2)}) async-start(), calls=%async_computation.29 | async-start | bytes 737280 | tf_op jit(solution)/shard_map/reduce_scatter | solution.py:380
  (174 other events, 4941.5 us)
Sparse Core Ops, SparseCore 0:
  23.2 66.0 all-gather.32
  92.1 39.5 all-gather.34
  133.9 85.0 all-gather.36
  220.8 86.7 all-gather.38
  310.2 65.9 all-gather.40
  378.3 39.6 all-gather.42
  420.1 78.6 all-gather.44
  500.9 79.1 all-gather.46
  612.5 62.2 reduce-scatter.58
  678.1 63.0 reduce-scatter.56
  744.8 78.1 reduce-scatter.54
  826.5 78.4 reduce-scatter.52
  908.7 94.9 reduce-scatter.70
  1007.2 95.1 reduce-scatter.68
  1105.4 60.8 reduce-scatter.86
  1169.8 94.4 reduce-scatter.64
  1267.4 60.8 reduce-scatter.84
  1331.4 61.4 reduce-scatter.94
  1396.6 61.3 reduce-scatter.92
  1461.1 59.9 reduce-scatter.90
  1524.4 60.1 reduce-scatter.88
  1587.8 61.5 reduce-scatter.98
  1653.1 61.3 reduce-scatter.96
  1718.0 94.3 reduce-scatter.60
  1815.4 19.4 reduce-scatter.78
  1837.7 19.7 reduce-scatter.76
  1860.4 22.0 reduce-scatter.74
  1885.6 22.0 reduce-scatter.72
  1910.2 22.0 reduce-scatter.82
  1934.6 22.0 reduce-scatter.80
  1959.3 22.0 reduce-scatter.66
  1983.9 22.0 reduce-scatter.62
where the time goes:
time: 2020 us; the launch traced here: 2010 us
  waiting for transfers between devices  1400 us (69%)
  blocking collectives  315 us (16%)
  local copies, waits for them, and re-layouts  129 us (6%)
  matrix products  120 us (6%)
  other arithmetic  32 us (2%)
    unnamed x46, waiting for transfers between devices  623 us
    reduce_scatter x2, waiting for transfers between devices, reduce_each(): lax.psum_scatter(gradients[2].astype(jnp.bfloat16), 'dp', scatter_dimensi...  194 us
    reduce_scatter x2, waiting for transfers between devices, reduce_each(): lax.psum_scatter(gradients[3].astype(jnp.bfloat16), 'dp', scatter_dimensi...  193 us
    reduce_scatter x2, waiting for transfers between devices, reduce_each(): lax.psum_scatter(gradients[0].astype(jnp.bfloat16), 'dp', scatter_dimensi...  160 us
    all_gather x2, waiting for transfers between devices, fetch_forward(): lax.all_gather(inner_parts[3], 'dp', axis=0, tiled=True)  71.8 us
    all_gather x2, waiting for transfers between devices, fetch_forward(): lax.all_gather(inner_parts[2], 'dp', axis=0, tiled=True)  70.7 us
    all_gather x2, blocking collectives, fetch_forward(): lax.all_gather(biases[layer_index], 'dp', axis=1, tiled=True)  65.1 us
    all_gather x2, blocking collectives, fetch_forward(): lax.all_gather(norm_gains[layer_index], 'dp', axis=1, tiled=True)  64.5 us
  transfers between devices with their start and end apart: 32, of which 25 were waited for; matrix products, arithmetic and copies ran while one was open for 11% of the time, Pallas kernels for 0%

commit v1 on v0

v1 whole, which is shorter than its diff:
```python
import functools
import math

import jax
import jax.numpy as jnp
from jax import lax
from jax.experimental import pallas as pl
from jax.experimental.pallas import tpu as pltpu
from jax.sharding import PartitionSpec as P

HEADS = 12
HD = 64
LAYERS = 2
SEQS = 2
D = 768
FF = 3072
T = 256
EPS = 1e-05
BF = jnp.bfloat16
F32 = jnp.float32
MIB = 1 << 20

ANY = pl.BlockSpec(memory_space=pl.ANY)
SMEM = pl.BlockSpec(memory_space=pltpu.SMEM)
VMEM = pl.BlockSpec(memory_space=pltpu.VMEM)

G1, G2, G3, C1, BQ, BV, C2, BO, C3, B2 = range(10)
VROWS = 16
HROW = 10
G4, B1, C4 = 10, 11, 12

RB = 32


def dot(a, b):
    return jnp.dot(a, b, preferred_element_type=F32)


def dot_nt(a, b):
    return lax.dot_general(a, b, (((1,), (1,)), ((), ())), preferred_element_type=F32)


def unit_lane(u):
    f, j = divmod(u, 9)
    return 512 * f + 64 * j if j < 8 else 2048 + 128 * f


def ln_stats(v):
    m = jnp.mean(v, axis=-1, keepdims=True)
    cen = v - m
    inv = lax.rsqrt(jnp.mean(cen * cen, axis=-1, keepdims=True) + EPS)
    return cen * inv, inv


def ln_back(dn, g, n, inv):
    e = dn * g
    dv = inv * (e - jnp.mean(e, axis=-1, keepdims=True) - n * jnp.mean(e * n, axis=-1, keepdims=True))
    return dv, jnp.sum(dn * n, axis=0, keepdims=True), jnp.sum(dn, axis=0, keepdims=True)


def seg_of(scal, places):
    e0 = scal[0]
    e1 = scal[0] + scal[1]
    return (places >= e0).astype(jnp.int32) + (places >= e1).astype(jnp.int32)


class Plan:
    def __init__(self, fast):
        self.fast = fast

    def load_a(self, scal, pieces, m, dst):
        if not self.fast:
            return [(pieces[0], dst)]
        out = []
        for h, ri, x, f, ref in self._pieces(scal, pieces):
            src = ref.at[ri, :, pl.ds(m * 48, 48)]
            out.append((src.at[:, :, pl.ds(0, 512)], dst.at[:, x, h, :, pl.ds(pl.multiple_of(f * 512, 512), 512)]))
            out.append((src.at[:, :, pl.ds(512, 256)], dst.at[:, x, h, :, pl.ds(pl.multiple_of(2048 + f * 256, 256), 256)]))
        return out

    def load_b(self, scal, pieces, m, dst):
        if not self.fast:
            return [(pieces[1], dst)]
        return [
            (ref.at[ri, :, pl.ds(m * 48, 48)], dst.at[:, x, h, :, pl.ds(pl.multiple_of(f * 768, 768), 768)])
            for h, ri, x, f, ref in self._pieces(scal, pieces)
        ]

    def load_c(self, scal, pieces, m, dst):
        if not self.fast:
            return [(pieces[2], dst)]
        return [
            (
                ref.at[ri, :, pl.ds(m * 48, 48), pl.ds(j * 384, 384)],
                dst.at[:, f, j, h, :, pl.ds(pl.multiple_of(x * 384, 384), 384)],
            )
            for h, ri, x, f, ref in self._pieces(scal, pieces)
            for j in range(2)
        ]

    def _pieces(self, scal, pieces):
        mx, my, mc = scal[3], scal[4], scal[5]
        for h in range(2):
            for bi in range(4):
                ro, rc = bi % 2, bi // 2
                for ri in range(2):
                    rx, ry = (ri, ro) if h == 0 else (ro, ri)
                    x = lax.rem(mx + rx, 2)
                    y = lax.rem(my + ry, 2)
                    c = lax.rem(mc + rc, 2)
                    yield h, ri, x, y * 2 + c, pieces[h * 4 + bi]

    def blocks(self, scal):
        if not self.fast:
            return [(f, 0, 0) for f in range(4)]
        my, mc = scal[4], scal[5]
        return [(lax.rem(my + ry, 2) * 2 + lax.rem(mc + rc, 2), rc, ry) for rc in (1, 0) for ry in (1, 0)]

    def store_ab(self, scal, src, outs, m, f, rc, ry):
        if not self.fast:
            return [(src, outs[0].at[f])]
        res = []
        for rx in range(2):
            x = lax.rem(scal[3] + rx, 2)
            for h in range(2):
                first, second = (rx, ry) if h == 0 else (ry, rx)
                res.append((src.at[:, x, h], outs[rc * 2 + h].at[first, second, :, pl.ds(m * 48, 48)]))
        return res

    def store_c(self, scal, src, outs, m):
        if not self.fast:
            return [(src, outs[1])]
        res = []
        for f, rc, ry in self.blocks(scal):
            for rx in range(2):
                x = lax.rem(scal[3] + rx, 2)
                for h in range(2):
                    first, second = (rx, ry) if h == 0 else (ry, rx)
                    for j in range(2):
                        res.append(
                            (
                                src.at[:, f, j, h, :, pl.ds(pl.multiple_of(x * 384, 384), 384)],
                                outs[rc * 2 + h].at[first, second, :, pl.ds(m * 48, 48), pl.ds(j * 384, 384)],
                            )
                        )
        return res

    def store_vec(self, scal, src, outs):
        res = []
        for _, rc, ry in self.blocks(scal):
            for rx in range(2):
                x = lax.rem(scal[3] + rx, 2)
                res.append((src.at[:, x], outs[rc * 2].at[rx, ry, :, pl.ds(48, 16)]))
        return res


def start(copies, sems, base=0):
    made = [pltpu.make_async_copy(s, d, sems.at[base + i]) for i, (s, d) in enumerate(copies)]
    for c in made:
        c.start()
    return made


def wait(made):
    for c in made:
        c.wait()


def attn_fwd(plan, npieces, m, *refs):
    scal, x_ref, vec_ref, pb_ref = refs[:4]
    pieces = refs[4 : 4 + npieces]
    x1_ref, a1_ref, un_ref, p_ref, o_ref, a2_ref = refs[4 + npieces : 10 + npieces]
    wa, sems = refs[10 + npieces :]
    loads = start(plan.load_a(scal, pieces, m, wa), sems)
    n1, _ = ln_stats(x_ref[...])
    a1 = (n1 * vec_ref[G1 : G1 + 1] + vec_ref[C1 : C1 + 1]).astype(BF)
    a1_ref[...] = a1
    seg_row = seg_of(scal, lax.broadcasted_iota(jnp.int32, (T, T), 1))
    seg_col = seg_of(scal, lax.broadcasted_iota(jnp.int32, (T, T), 0))
    same = seg_row == seg_col
    wait(loads)
    for f in range(4):
        part = dot(a1, wa[:, :, :, :, 512 * f : 512 * f + 512].reshape(D, 512)) + pb_ref[0:1, 512 * f : 512 * f + 512]
        last = dot(a1, wa[:, :, :, :, 2048 + 256 * f : 2176 + 256 * f].reshape(D, 128)) + pb_ref[0:1, 2048 + 128 * f : 2176 + 128 * f]
        for j in range(9):
            u = 9 * f + j
            val = part[:, 64 * j : 64 * j + 64] if j < 8 else last[:, 0:64]
            val = val.astype(BF)
            if u < HEADS:
                val = val * BF(0.125)
            un_ref[u] = val
    for h in range(HEADS):
        s = jnp.where(same, dot_nt(un_ref[h], un_ref[HEADS + h]), -1e30)
        ex = jnp.exp(s - jnp.max(s, axis=-1, keepdims=True))
        p = ex * (1.0 / jnp.sum(ex, axis=-1, keepdims=True))
        p_ref[h] = p
        o_ref[:, 64 * h : 64 * h + 64] = dot(p.astype(BF), un_ref[2 * HEADS + h])
    n2, _ = ln_stats(o_ref[...])
    a2 = (n2 * vec_ref[G2 : G2 + 1] + vec_ref[C2 : C2 + 1]).astype(BF)
    a2_ref[...] = a2
    z = [dot(a2, wa[:, :, :, :, 2048 + 256 * f : 2304 + 256 * f].reshape(D, 256))[:, 64:] for f in range(4)]
    x1_ref[...] = x_ref[...] + (jnp.concatenate(z, axis=1) + vec_ref[BO : BO + 1])


def ff_fwd(plan, npieces, mb, mc, last, *refs):
    scal, x1_ref, vec_ref, hid_ref = refs[:4]
    pieces = refs[4 : 4 + npieces]
    x2_ref, a3_ref, sl_ref, n4_ref, a4_ref = refs[4 + npieces : 9 + npieces]
    wb, wc, sems = refs[9 + npieces :]
    load_b = start(plan.load_b(scal, pieces, mb, wb), sems)
    load_c = start(plan.load_c(scal, pieces, mc, wc), sems, len(load_b))
    n3, _ = ln_stats(x1_ref[...])
    a3 = (n3 * vec_ref[G3 : G3 + 1] + vec_ref[C3 : C3 + 1]).astype(BF)
    a3_ref[...] = a3
    wait(load_b)
    for f in range(4):
        cols = slice(768 * f, 768 * f + 768)
        n4_ref[:, cols] = dot(a3, wb[:, :, :, :, cols].reshape(D, 768)) + hid_ref[B1 : B1 + 1, cols]

    def rows_step(i, carry):
        rows = pl.ds(i * RB, RB)
        total = jnp.zeros((RB, 1), F32)
        for f in range(4):
            cols = slice(768 * f, 768 * f + 768)
            u = n4_ref[rows, cols]
            phi_c = 0.5 * (1.0 + lax.erf(u * (1.0 / math.sqrt(2.0))))
            r = u * phi_c
            sl_ref[rows, cols] = phi_c + u * (jnp.exp(-0.5 * u * u) * (1.0 / math.sqrt(2.0 * math.pi)))
            n4_ref[rows, cols] = r
            total += jnp.sum(r, axis=-1, keepdims=True)
        mean = total * (1.0 / FF)
        total = jnp.zeros((RB, 1), F32)
        for f in range(4):
            cols = slice(768 * f, 768 * f + 768)
            cen = n4_ref[rows, cols] - mean
            total += jnp.sum(cen * cen, axis=-1, keepdims=True)
        inv = lax.rsqrt(total * (1.0 / FF) + EPS)
        for f in range(4):
            cols = slice(768 * f, 768 * f + 768)
            n4 = (n4_ref[rows, cols] - mean) * inv
            n4_ref[rows, cols] = n4
            a4_ref[rows, cols] = (n4 * hid_ref[G4 : G4 + 1, cols] + hid_ref[C4 : C4 + 1, cols]).astype(BF)
            sl_ref[rows, cols] = sl_ref[rows, cols] * inv
        return carry

    lax.fori_loop(0, T // RB, rows_step, 0)
    wait(load_c)
    acc = dot_nt(a4_ref[:, 0:768], wc[0].reshape(D, 768))
    for z in range(1, 4):
        acc += dot_nt(a4_ref[:, 768 * z : 768 * z + 768], wc[z].reshape(D, 768))
    x2 = x1_ref[...] + (acc + vec_ref[B2 : B2 + 1])
    if last:
        seg = seg_of(scal, lax.broadcasted_iota(jnp.int32, (T, 1), 0))
        x2 = x2 * (seg < SEQS).astype(F32)
    x2_ref[...] = x2


def ff_bwd(plan, npieces, nouts, mb, mc, last, *refs):
    scal, dy_ref, x1_ref, a3_ref, sl_ref, n4_ref, a4_ref, vec_ref, hid_ref = refs[:9]
    pieces = refs[9 : 9 + npieces]
    dx1_ref, gv_ref, gh_ref = refs[9 + npieces : 12 + npieces]
    outs = refs[12 + npieces : 12 + npieces + nouts]
    wb, wc, gb, gc, da4, du_ref, sems = refs[12 + npieces + nouts :]
    load_c = start(plan.load_c(scal, pieces, mc, wc), sems)
    load_b = start(plan.load_b(scal, pieces, mb, wb), sems, len(load_c))
    base = len(load_c) + len(load_b)
    dy = dy_ref[...]
    if last:
        seg = seg_of(scal, lax.broadcasted_iota(jnp.int32, (T, 1), 0))
        dy = dy * (seg < SEQS).astype(F32)
    dz2 = dy.astype(BF)
    gv_ref[...] = jnp.zeros_like(gv_ref)
    gh_ref[...] = jnp.zeros_like(gh_ref)
    gv_ref[B2 : B2 + 1] = jnp.sum(dz2.astype(F32), axis=0, keepdims=True)
    dz2t = dz2.T
    wait(load_c)
    for z in range(4):
        cols = slice(768 * z, 768 * z + 768)
        da4[:, cols] = dot(dz2, wc[z].reshape(D, 768))
        gc[z] = dot(dz2t, a4_ref[:, cols]).astype(BF).reshape(4, 2, 2, 48, 768)
    saves = start(plan.store_c(scal, gc, outs, mc), sems, base)
    base += len(saves)

    def rows_step(i, carry):
        rows = pl.ds(i * RB, RB)
        s1 = jnp.zeros((RB, 1), F32)
        s2 = jnp.zeros((RB, 1), F32)
        for z in range(4):
            cols = slice(768 * z, 768 * z + 768)
            da = da4[rows, cols]
            n4 = n4_ref[rows, cols]
            dn = da * n4
            e = da * hid_ref[G4 : G4 + 1, cols]
            da4[rows, cols] = e
            s1 += jnp.sum(e, axis=-1, keepdims=True)
            s2 += jnp.sum(e * n4, axis=-1, keepdims=True)
            gh_ref[G4 : G4 + 1, cols] += jnp.sum(dn, axis=0, keepdims=True)
            gh_ref[C4 : C4 + 1, cols] += jnp.sum(da, axis=0, keepdims=True)
        s1 = s1 * (1.0 / FF)
        s2 = s2 * (1.0 / FF)
        for z in range(4):
            cols = slice(768 * z, 768 * z + 768)
            du = (sl_ref[rows, cols] * (da4[rows, cols] - s1 - n4_ref[rows, cols] * s2)).astype(BF)
            du_ref[rows, cols] = du
            gh_ref[B1 : B1 + 1, cols] += jnp.sum(du.astype(F32), axis=0, keepdims=True)
        return carry

    lax.fori_loop(0, T // RB, rows_step, 0)
    a3t = a3_ref[...].T
    wait(load_b)
    da3 = jnp.zeros((T, D), F32)
    for i, (f, rc, ry) in enumerate(plan.blocks(scal)):
        cols = pl.ds(pl.multiple_of(f * 768, 768), 768)
        du = du_ref[:, cols]
        gb[i] = dot(a3t, du).astype(BF).reshape(4, 2, 2, 48, 768)
        more = start(plan.store_ab(scal, gb.at[i], outs, mb, f, rc, ry), sems, base)
        base += len(more)
        saves += more
        da3 += dot_nt(du, wb[:, :, :, :, cols].reshape(D, 768))
    n3, inv3 = ln_stats(x1_ref[...])
    part, dg3, dc3 = ln_back(da3, vec_ref[G3 : G3 + 1], n3, inv3)
    gv_ref[G3 : G3 + 1] = dg3
    gv_ref[C3 : C3 + 1] = dc3
    dx1_ref[...] = dy + part
    wait(saves)


def attn_bwd(plan, npieces, nouts, m, fold, *refs):
    scal, dx1_ref, x_ref, a1_ref, un_ref, p_ref, o_ref, a2_ref, vec_ref = refs[:9]
    pos = 9
    others = refs[pos : pos + (5 if fold else 0)]
    pos += len(others)
    pieces = refs[pos : pos + npieces]
    pos += npieces
    dx_ref, gv_ref = refs[pos : pos + 2]
    outs = refs[pos + 2 : pos + 2 + nouts]
    scratch = refs[pos + 2 + nouts :]
    wa, ga, dpm, dzp, do_ref = scratch[:5]
    vblk = scratch[5] if fold else None
    sems = scratch[-1]
    loads = start(plan.load_a(scal, pieces, m, wa), sems)
    base = len(loads)
    dx1 = dx1_ref[...]
    dz = dx1.astype(BF)
    gv_ref[...] = jnp.zeros_like(gv_ref)
    gv_ref[BO : BO + 1] = jnp.sum(dz.astype(F32), axis=0, keepdims=True)
    dzp[...] = jnp.concatenate(
        [jnp.concatenate([jnp.zeros((T, 64), BF), dz[:, 192 * f : 192 * f + 192]], axis=1) for f in range(4)], axis=1
    )
    n2, inv2 = ln_stats(o_ref[...])
    wait(loads)
    da2 = dot_nt(dzp[...], wa[:, :, :, :, 2048:3072].reshape(D, 1024))
    do, dg2, dc2 = ln_back(da2, vec_ref[G2 : G2 + 1], n2, inv2)
    gv_ref[G2 : G2 + 1] = dg2
    gv_ref[C2 : C2 + 1] = dc2
    do = do.astype(BF)
    for f in range(4):
        dpm[:, 2048 + 256 * f : 2304 + 256 * f] = jnp.zeros((T, 256), BF)
    for h in range(HEADS):
        doh = do[:, 64 * h : 64 * h + 64]
        p = p_ref[h]
        q, k, v = un_ref[h], un_ref[HEADS + h], un_ref[2 * HEADS + h]
        dv = dot(p.astype(BF).T, doh)
        dp = dot_nt(doh, v)
        delta = jnp.sum(p * dp, axis=-1, keepdims=True)
        ds = (p * (dp - delta)).astype(BF)
        dq = dot(ds, k) * 0.125
        dk = dot(ds.T, q)
        for which, grad in ((0, dq), (1, dk), (2, dv)):
            u = which * HEADS + h
            f, j = divmod(u, 9)
            lane = 512 * f + 64 * j if j < 8 else 2048 + 256 * f
            grad = grad.astype(BF)
            dpm[:, lane : lane + 64] = grad
            if which != 1:
                row = BQ if which == 0 else BV
                gv_ref[row : row + 1, 64 * h : 64 * h + 64] = jnp.sum(grad.astype(F32), axis=0, keepdims=True)
    a1t = a1_ref[...].T
    a2t = a2_ref[...].T
    saves = []
    for i, (f, rc, ry) in enumerate(plan.blocks(scal)):
        main = dpm[:, pl.ds(pl.multiple_of(f * 512, 512), 512)]
        tail = dpm[:, pl.ds(pl.multiple_of(2048 + f * 256, 256), 256)]
        ga[i, :, :, :, :, 0:512] = dot(a1t, main).astype(BF).reshape(4, 2, 2, 48, 512)
        ga[i, :, :, :, :, 512:768] = (
            (dot(a1t, tail) + dot(a2t, dzp[:, pl.ds(pl.multiple_of(f * 256, 256), 256)])).astype(BF).reshape(4, 2, 2, 48, 256)
        )
        more = start(plan.store_ab(scal, ga.at[i], outs, m, f, rc, ry), sems, base)
        base += len(more)
        saves += more
    da1 = dot_nt(dpm[...], wa[...].reshape(D, FF))
    n1, inv1 = ln_stats(x_ref[...])
    part, dg1, dc1 = ln_back(da1, vec_ref[G1 : G1 + 1], n1, inv1)
    gv_ref[G1 : G1 + 1] = dg1
    gv_ref[C1 : C1 + 1] = dc1
    dx_ref[...] = dx1 + part
    if fold:
        va0, vb1, va1, gh0, gh1 = (r[...] for r in others)
        v0 = gv_ref[...] + va0
        v1 = vb1 + va1
        for d in range(8):
            c96 = slice(96 * d, 96 * d + 96)
            c384 = slice(384 * d, 384 * d + 384)
            low = jnp.concatenate([v0[:, c96], v1[:, c96], jnp.zeros((VROWS, 576), F32)], axis=1)
            vblk[d // 2, d % 2] = (low + jnp.concatenate([gh0[:, c384], gh1[:, c384]], axis=1)).astype(BF)
        more = start(plan.store_vec(scal, vblk, outs), sems, base)
        saves += more
    wait(saves)


def params(mib):
    return pltpu.CompilerParams(vmem_limit_bytes=mib * MIB)


def cost(flops, nbytes):
    return pl.CostEstimate(flops=int(flops), bytes_accessed=int(nbytes), transcendentals=0)


WA = pltpu.VMEM((4, 2, 2, 48, FF), BF)
WC = pltpu.VMEM((4, 4, 2, 2, 48, D), BF)
S = jax.ShapeDtypeStruct
WBYTES = D * FF * 2


def call_attn_fwd(plan, scal, x, vec, pbias, pieces, m):
    n = len(pieces)
    return pl.pallas_call(
        functools.partial(attn_fwd, plan, n, m),
        out_shape=(S((T, D), F32), S((T, D), BF), S((36, T, HD), BF), S((HEADS, T, T), F32), S((T, D), F32), S((T, D), BF)),
        in_specs=[SMEM, VMEM, VMEM, VMEM] + [ANY] * n,
        out_specs=[VMEM] * 6,
        scratch_shapes=[WA, pltpu.SemaphoreType.DMA((32,))],
        compiler_params=params(40),
        cost_estimate=cost(2 * T * D * FF * 6, WBYTES + 8e6),
        name="attn_fwd",
    )(scal, x, vec, pbias, *pieces)


def call_ff_fwd(plan, scal, x1, vec, hid, pieces, mb, mc, last):
    n = len(pieces)
    return pl.pallas_call(
        functools.partial(ff_fwd, plan, n, mb, mc, last),
        out_shape=(S((T, D), F32), S((T, D), BF), S((T, FF), F32), S((T, FF), F32), S((T, FF), BF)),
        in_specs=[SMEM, VMEM, VMEM, VMEM] + [ANY] * n,
        out_specs=[VMEM] * 5,
        scratch_shapes=[WA, WC, pltpu.SemaphoreType.DMA((48,))],
        compiler_params=params(40),
        cost_estimate=cost(2 * T * D * FF * 6, 2 * WBYTES + 8e6),
        name="ff_fwd",
    )(scal, x1, vec, hid, *pieces)


def grad_shapes(plan, n, extra=0):
    if not plan.fast:
        shapes = [S((4, 4, 2, 2, 48, D), BF)] * n
        return shapes
    return [S((2, 2, 4, n * 48 + e, D), BF) for e in (extra, 0, extra, 0)]


def call_ff_bwd(plan, scal, dy, x1, a3, sl, n4, a4, vec, hid, pieces, mb, mc, last):
    n = len(pieces)
    g = grad_shapes(plan, 2)
    res = pl.pallas_call(
        functools.partial(ff_bwd, plan, n, len(g), mb, mc, last),
        out_shape=(S((T, D), F32), S((VROWS, D), F32), S((VROWS, FF), F32), *g),
        in_specs=[SMEM] + [VMEM] * 8 + [ANY] * n,
        out_specs=[VMEM] * 3 + [ANY] * len(g),
        scratch_shapes=[
            WA,
            WC,
            WC,
            WC,
            pltpu.VMEM((T, FF), F32),
            pltpu.VMEM((T, FF), BF),
            pltpu.SemaphoreType.DMA((112,)),
        ],
        compiler_params=params(50),
        cost_estimate=cost(2 * T * D * FF * 8, 4 * WBYTES + 8e6),
        name="ff_bwd",
    )(scal, dy, x1, a3, sl, n4, a4, vec, hid, *pieces)
    return res[:3], res[3:]


def call_attn_bwd(plan, scal, dx1, x, a1, un, p, o, a2, vec, pieces, m, others):
    n = len(pieces)
    fold = len(others) > 0
    g = grad_shapes(plan, 1, 16 if fold else 0)
    vblk = [pltpu.VMEM((4, 2, VROWS, D), BF)] if fold else []
    res = pl.pallas_call(
        functools.partial(attn_bwd, plan, n, len(g), m, fold),
        out_shape=(S((T, D), F32), S((VROWS, D), F32), *g),
        in_specs=[SMEM] + [VMEM] * (8 + len(others)) + [ANY] * n,
        out_specs=[VMEM] * 2 + [ANY] * len(g),
        scratch_shapes=[
            WA,
            WC,
            pltpu.VMEM((T, FF), BF),
            pltpu.VMEM((T, 1024), BF),
            pltpu.VMEM((T, D), BF),
            *vblk,
            pltpu.SemaphoreType.DMA((64,)),
        ],
        compiler_params=params(40),
        cost_estimate=cost(2 * T * D * FF * 8, 2 * WBYTES + 8e6),
        name="attn_bwd",
    )(scal, dx1, x, a1, un, p, o, a2, vec, *others, *pieces)
    return res[:2], res[2:]


def shift(n, k):
    return [(i, (i + k) % n) for i in range(n)]


class Ring:
    def __init__(self, dp, fsdp):
        self.X = fsdp // 2
        self.Z = dp // self.X
        self.dp, self.fsdp = dp, fsdp

    def z(self, v, k):
        return lax.ppermute(v, "dp", [(z * self.X + x, (z + k) % self.Z * self.X + x) for z in range(self.Z) for x in range(self.X)])

    def x(self, v):
        return lax.ppermute(v, "dp", [(i, i ^ 1) for i in range(self.dp)])

    def y(self, v):
        return lax.ppermute(v, "fsdp", [(i, i ^ 2) for i in range(self.fsdp)])

    def c(self, v):
        return lax.ppermute(v, "fsdp", [(i, i ^ 1) for i in range(self.fsdp)])


def zcat_kernel(r1, r2, scal, p0, p1, p2, p3, o1, o2, sems):
    copies = []
    for k, ref in enumerate((p0, p1, p2, p3)):
        z = lax.rem(scal[2] + 4 - k, 4)
        copies.append((ref.at[pl.ds(0, r1)], o1.at[z]))
        copies.append((ref.at[pl.ds(r1, r2)], o2.at[z]))
    wait(start(copies, sems))


def zcat(scal, parts, r1, r2):
    return pl.pallas_call(
        functools.partial(zcat_kernel, r1, r2),
        out_shape=(S((4, r1, D), BF), S((4, r2, D), BF)),
        in_specs=[SMEM] + [ANY] * 4,
        out_specs=[ANY] * 2,
        scratch_shapes=[pltpu.SemaphoreType.DMA((8,))],
        cost_estimate=cost(0, 8 * (r1 + r2) * D * 4),
        name="zcat",
    )(scal, *parts)


def gather_chunk(ring, scal, pack, r1):
    r2 = pack.shape[0] - r1
    parts = [pack] + [ring.z(pack, k) for k in (1, 2, 3)]
    h1, h2 = zcat(scal, parts, r1, r2)
    x1 = ring.x(h1)
    y2 = ring.y(h2)
    h1 = jnp.stack([h1, x1])
    h2 = jnp.stack([h2, y2])
    y1 = ring.y(h1)
    x2 = ring.x(h2)
    return [h1, y1, ring.c(h1), ring.c(y1), h2, x2, ring.c(h2), ring.c(x2)]


def add(a, b):
    return (a.astype(F32) + b.astype(F32)).astype(BF)


def scatter_chunk(ring, zme, grads):
    k0, k1, s0, s1 = grads
    r0, r1 = ring.c(s0), ring.c(s1)
    x0 = ring.x(add(k0[1], r0[1]))
    y1 = ring.y(add(k1[1], r1[1]))
    a0 = add(k0[0], r0[0])
    a1 = add(k1[0], r1[0])
    y0 = ring.y(add(a0[1], x0[1]))
    x1 = ring.x(add(a1[1], y1[1]))
    b0 = add(a0[0], x0[0])
    b1 = add(a1[0], y1[0])

    def at(k):
        z = lax.rem(zme + k, 4)
        pick = lambda v: lax.dynamic_index_in_dim(v, z, 0, keepdims=False)
        return jnp.concatenate([add(pick(b0), pick(y0)), add(pick(b1), pick(x1))], axis=0)

    total = at(0).astype(F32)
    for k in (1, 2, 3):
        total = total + ring.z(at(k), k).astype(F32)
    return total


def unpack_vec(rows):
    rows = rows.astype(F32)
    vecs, hids = [], []
    for l in range(LAYERS):
        v = rows[:, :, 96 * l : 96 * l + 96].transpose(1, 0, 2).reshape(VROWS, D)
        h = rows[:, :, 384 * l : 384 * l + 384].transpose(1, 0, 2).reshape(VROWS, FF)
        vecs.append(v)
        hids.append(h)
    return vecs, hids


def proj_bias(vec):
    full = jnp.concatenate([vec[BQ], jnp.zeros((D,), F32), vec[BV]]).reshape(4, 9 * HD)
    return jnp.concatenate(
        [full[:, :512].reshape(2048), jnp.pad(full[:, 512:], ((0, 0), (0, 64))).reshape(512)]
    ).reshape(1, 2560)


def run_layers(plan, scal, inputs, cotangent, vecs, hids, pieces, after):
    pb = [proj_bias(v) for v in vecs]
    x = inputs
    kept = []
    for l in range(LAYERS):
        pa, ma, pbc, mb, mc = pieces[l]
        x1, a1, un, p, o, a2 = call_attn_fwd(plan, scal, x, vecs[l], pb[l], pa, ma)
        x2, a3, sl, n4, a4 = call_ff_fwd(plan, scal, x1, vecs[l], hids[l], pbc, mb, mc, l == LAYERS - 1)
        kept.append((x, x1, a1, un, p, o, a2, a3, sl, n4, a4))
        x = x2
    outputs = x
    dy = cotangent
    vec_grads = {}
    for l in reversed(range(LAYERS)):
        pa, ma, pbc, mb, mc = pieces[l]
        x, x1, a1, un, p, o, a2, a3, sl, n4, a4 = kept[l]
        (dx1, gva, gh), gbc = call_ff_bwd(plan, scal, dy, x1, a3, sl, n4, a4, vecs[l], hids[l], pbc, mb, mc, l == LAYERS - 1)
        after(l, "bc", gbc)
        others = (gva, *vec_grads[1][:2], gh, vec_grads[1][2]) if plan.fast and l == 0 else ()
        (dy, gvb), ga = call_attn_bwd(plan, scal, dx1, x, a1, un, p, o, a2, vecs[l], pa, ma, others)
        after(l, "a", ga)
        vec_grads[l] = (gva, gvb, gh)
    return outputs, dy, vec_grads


def fast_shards(ring, inputs, lengths, in_projection, out_projection, up_weight, down_weight, norm_gains, biases, hidden_gains, hidden_biases, cotangent):
    plan = Plan(True)
    dpi, fi = lax.axis_index("dp"), lax.axis_index("fsdp")
    zme = dpi // ring.X
    place = jnp.stack([zme, dpi % ring.X, fi // 2, fi % 2]).astype(jnp.int32)
    scal = jnp.concatenate([lengths[0], place, jnp.zeros((2,), jnp.int32)])

    own_vec = jnp.concatenate([norm_gains, biases], axis=1)
    own_hid = jnp.concatenate([hidden_gains, hidden_biases], axis=1)
    vec_rows = jnp.concatenate(
        [
            jnp.pad(jnp.concatenate([own_vec[0], own_vec[1]], axis=1), ((0, 0), (0, 576))),
            jnp.concatenate([own_hid[0], own_hid[1]], axis=1),
            jnp.zeros((3, D), BF),
        ],
        axis=0,
    )
    pack_a = [jnp.concatenate([in_projection[l], out_projection[l]], axis=1) for l in range(LAYERS)]
    pack_c = []
    for l in range(LAYERS):
        t = down_weight[l].T
        pack_c.append(jnp.concatenate([t[:96], t[96:]], axis=1))
    pack_bc = []
    for l in range(LAYERS):
        b, c = up_weight[l], pack_c[l]
        pack_bc.append(jnp.concatenate([b[:48], c[:48], b[48:], c[48:]], axis=0))
    first = jnp.concatenate([pack_a[0][:48], vec_rows, pack_a[0][48:]], axis=0)
    pieces = []
    for l in range(LAYERS):
        got_a = gather_chunk(ring, scal, first if l == 0 else pack_a[l], 64 if l == 0 else 48)
        got_bc = gather_chunk(ring, scal, pack_bc[l], 96)
        pieces.append((got_a, 0, got_bc, 0, 1))
        if l == 0:
            rows = got_a[0][:, :, 48:64]
            xme = dpi % ring.X
            rows = jnp.where(xme == 0, rows, rows[::-1]).transpose(1, 0, 2, 3).reshape(8, VROWS, D)
            vecs, hids = unpack_vec(rows)
    sums = {}

    def after(l, name, grads):
        sums[l, name] = scatter_chunk(ring, zme, grads)

    outputs, input_gradient, _ = run_layers(plan, scal, inputs, cotangent, vecs, hids, pieces, after)
    a = [sums[0, "a"], sums[1, "a"]]
    vrows = a[0][48:64]
    a[0] = jnp.concatenate([a[0][:48], a[0][64:]], axis=0)
    bc = [sums[l, "bc"] for l in range(LAYERS)]
    b = [jnp.concatenate([v[:48], v[96:144]], axis=0) for v in bc]
    c = [jnp.concatenate([v[48:96], v[144:]], axis=0) for v in bc]
    c = [jnp.concatenate([v[:, :384], v[:, 384:]], axis=0).T for v in c]
    gv = jnp.stack([vrows[:10, :96], vrows[:10, 96:192]])
    gh = jnp.stack([vrows[10:13, :384], vrows[10:13, 384:]])
    return (
        outputs,
        input_gradient,
        jnp.stack([v[:, :576] for v in a]),
        jnp.stack([v[:, 576:] for v in a]),
        jnp.stack(b),
        jnp.stack(c),
        gv[:, :3],
        gv[:, 3:],
        gh[:, :1],
        gh[:, 1:],
    )


def whole_shards(inputs, lengths, in_projection, out_projection, up_weight, down_weight, norm_gains, biases, hidden_gains, hidden_biases, cotangent):
    plan = Plan(False)
    scal = jnp.concatenate([lengths[0], jnp.zeros((6,), jnp.int32)])

    def full(w):
        return lax.all_gather(lax.all_gather(w, "fsdp", axis=1, tiled=True), "dp", axis=0, tiled=True)

    def rows(v, width):
        return jnp.pad(lax.all_gather(v, "dp", axis=1, tiled=True).astype(F32), ((0, VROWS - v.shape[0]), (0, 0)))

    vecs, hids, pieces = [], [], []
    for l in range(LAYERS):
        qkv = full(in_projection[l]).reshape(D, 4, 9 * HD)
        out = full(out_projection[l]).reshape(D, 4, 192)
        a = jnp.concatenate([qkv[:, :, :512].reshape(D, 2048), jnp.concatenate([qkv[:, :, 512:], out], axis=2).reshape(D, 1024)], axis=1)
        b = full(up_weight[l])
        c = full(down_weight[l]).reshape(4, D, D).transpose(0, 2, 1)
        shape = (4, 2, 2, 48, FF)
        got = [a.reshape(shape), b.reshape(shape), c.reshape(4, 4, 2, 2, 48, D)]
        pieces.append((got, 0, got, 0, 0))
        vecs.append(rows(jnp.concatenate([norm_gains[l], biases[l]], axis=0), D))
        hid = rows(jnp.concatenate([hidden_gains[l], hidden_biases[l]], axis=0), FF)
        hids.append(jnp.roll(hid, HROW, axis=0))
    grads = {}

    def after(l, name, got):
        grads[l, name] = got

    outputs, input_gradient, vec_grads = run_layers(plan, scal, inputs, cotangent, vecs, hids, pieces, after)

    def scatter(g):
        g = lax.psum_scatter(g.astype(BF), "dp", scatter_dimension=0, tiled=True)
        return lax.psum_scatter(g, "fsdp", scatter_dimension=1, tiled=True).astype(F32)

    def scatter_rows(v):
        v = lax.psum_scatter(v.astype(BF), "dp", scatter_dimension=1, tiled=True).astype(F32)
        return lax.psum(v, "fsdp")

    res = []
    for l in range(LAYERS):
        gb, gc = grads[l, "bc"]
        (ga,) = grads[l, "a"]
        ga = ga.reshape(4, D, D).transpose(1, 0, 2)
        gva, gvb, gh = vec_grads[l]
        gv = scatter_rows((gva + gvb)[:10])
        gh = scatter_rows(gh[HROW : HROW + 3])
        res.append(
            (
                scatter(ga[:, :, :576].reshape(D, 3 * D)),
                scatter(ga[:, :, 576:].reshape(D, D)),
                scatter(gb.reshape(4, D, D).transpose(1, 0, 2).reshape(D, FF)),
                scatter(gc.reshape(4, D, D).transpose(0, 2, 1).reshape(FF, D)),
                gv[:3],
                gv[3:],
                gh[:1],
                gh[1:],
            )
        )
    return (outputs, input_gradient, *(jnp.stack([r[i] for r in res]) for i in range(8)))


def solution(mesh):
    dp, fsdp = mesh.shape["dp"], mesh.shape["fsdp"]
    both = P(("dp", "fsdp"), None)
    mat = P(None, "dp", "fsdp")
    row = P(None, None, "dp")
    ring = Ring(dp, fsdp)
    shards = functools.partial(fast_shards, ring) if (dp, fsdp) == (8, 4) else whole_shards
    return jax.shard_map(
        shards,
        mesh=mesh,
        in_specs=(both, both, mat, mat, mat, mat, row, row, row, row, both),
        out_specs=(both, both, mat, mat, mat, mat, row, row, row, row),
        check_vma=False,
    )
```

time: 2020 us -> 625 us (0.31)
  waiting for transfers between devices: 1400 us -> 175 us
  blocking collectives: 315 us -> 0 us
  Pallas kernels: 0 us -> 223 us
  starting transfers between devices: 1.54 us -> 123 us
  matrix products: 120 us -> 0 us
  local copies, waits for them, and re-layouts: 129 us -> 60.7 us
    reduce_scatter x10 -> x0, waiting for transfers between devices: 635 us -> none  [the longest x2 194 us: reduce_each(): lax.psum_scatter(gradients[2].astype(jnp.bfloat16), 'dp', scatter_dimensi...]
    unnamed x46 -> x0, waiting for transfers between devices: 623 us -> none
    all_gather x16 -> x0, blocking collectives: 304 us -> none  [the longest x2 65.1 us: fetch_forward(): lax.all_gather(biases[layer_index], 'dp', axis=1, tiled=True)]
    pallas_call x0 -> x12, Pallas kernels: none -> 223 us  [the longest x4 118 us: zcat(): pl.pallas_call(functools.partial(zcat_kernel, r1, r2), out_shape=(S((4, r...]
    ppermute x0 -> x80, waiting for transfers between devices: none -> 175 us  [the longest x16 87.6 us: y(): return lax.ppermute(v, 'fsdp', [(i, i ^ 2) for i in range(self.fsdp)])]
    all_gather x8 -> x0, waiting for transfers between devices: 143 us -> none  [the longest x2 71.8 us: fetch_forward(): lax.all_gather(inner_parts[3], 'dp', axis=0, tiled=True)]
    ppermute x0 -> x80, starting transfers between devices: none -> 123 us  [the longest x24 82.4 us: z(): lax.ppermute(v, 'dp', [(z * self.X + x, (z + k) % self.Z * self.X + x) fo...]
    dot_general x36 -> x0, matrix products: 120 us -> none  [the longest x2 12.3 us: layer_forward(): jnp.dot(ffn_input, up_full, preferred_element_type=jnp.float32)]
  transfers between devices with their start and end apart: 32 -> 80, of which waited for: 25 -> 26; matrix products, arithmetic and copies ran while one was open for 11% -> 9% of each run, Pallas kernels for 0% -> 29%
where the time goes in v1:
time: 625 us; the launch traced here: 618 us
  Pallas kernels  223 us (36%)
  waiting for transfers between devices  175 us (28%)
  starting transfers between devices  123 us (20%)
  local copies, waits for them, and re-layouts  60.7 us (10%)
  other arithmetic  33.8 us (5%)
    pallas_call x4, Pallas kernels, zcat(): pl.pallas_call(functools.partial(zcat_kernel, r1, r2), out_shape=(S((4, r...  118 us
    ppermute x16, waiting for transfers between devices, y(): return lax.ppermute(v, 'fsdp', [(i, i ^ 2) for i in range(self.fsdp)])  87.6 us
    ppermute x24, starting transfers between devices, z(): lax.ppermute(v, 'dp', [(z * self.X + x, (z + k) % self.Z * self.X + x) fo...  82.4 us
    ppermute x16, waiting for transfers between devices, x(): return lax.ppermute(v, 'dp', [(i, i ^ 1) for i in range(self.dp)])  43.6 us
    ppermute x24, waiting for transfers between devices, z(): lax.ppermute(v, 'dp', [(z * self.X + x, (z + k) % self.Z * self.X + x) fo...  43.3 us
    unnamed x230, local copies, waits for them, and re-layouts  43.2 us
    pallas_call x2, Pallas kernels, call_ff_bwd(): pl.pallas_call(functools.partial(ff_bwd, plan, n, len(g), mb, mc, last),...  33.8 us
    pallas_call x2, Pallas kernels, call_attn_bwd(): pl.pallas_call(functools.partial(attn_bwd, plan, n, len(g), m, fold), out...  33.5 us
  transfers between devices with their start and end apart: 80, of which 26 were waited for; matrix products, arithmetic and copies ran while one was open for 9% of the time, Pallas kernels for 29%

profile of v1, /device:TPU:0, one launch (start us, length us, event | category | flops | bytes accessed | tf_op | source)
XLA Modules:
  0.0 618.1 jit_solution(4584586213901079515)
XLA Ops:
  13.1 6.8 %collective-permute-start.1 = (bf16[112,768]{1,0:T(8,128)(2,1)S(1)}, bf16[112,768]{1,0:T(8,128)(2,1)S(1)}, u32[]{:S(2)}, u32[]{:S(2)}) collective-permute-start(bf16[112,768]{1,0:T(8,128)(2,1)S(1)} %concatenate.123.p0), channel_id=1, source_target_pairs={{0,16},{4,20},{8,24},{12,28},{16,0},{20,4},{24,8},{28,12},{1,17},{... | collective-permute-start | bytes 516104 | tf_op jit(solution)/shard_map/ppermute | solution.py:521
  24.0 18.3 %collective-permute-start.2 = (bf16[112,768]{1,0:T(8,128)(2,1)S(1)}, bf16[112,768]{1,0:T(8,128)(2,1)S(1)}, u32[]{:S(2)}, u32[]{:S(2)}) collective-permute-start(bf16[112,768]{1,0:T(8,128)(2,1)S(1)} %concatenate.123.p0), channel_id=1, source_target_pairs={{0,24},{4,28},{8,0},{12,4},{16,8},{20,12},{24,16},{28,20},{1,25},{... | collective-permute-start | bytes 516104 | tf_op jit(solution)/shard_map/ppermute | solution.py:521
  45.0 9.8 %collective-permute-start.33 = (bf16[192,768]{1,0:T(8,128)(2,1)S(1)}, bf16[192,768]{1,0:T(8,128)(2,1)S(1)}, u32[]{:S(2)}, u32[]{:S(2)}) collective-permute-start(bf16[192,768]{1,0:T(8,128)(2,1)S(1)} %fusion.39.p0), channel_id=1, source_target_pairs={{0,8},{4,12},{8,16},{12,20},{16,24},{20,28},{24,0},{28,4},{1,9},{5... | collective-permute-start | bytes 884744 | tf_op jit(solution)/shard_map/ppermute | solution.py:521
  58.2 15.3 %collective-permute-start.35 = (bf16[192,768]{1,0:T(8,128)(2,1)S(1)}, bf16[192,768]{1,0:T(8,128)(2,1)S(1)}, u32[]{:S(2)}, u32[]{:S(2)}) collective-permute-start(bf16[192,768]{1,0:T(8,128)(2,1)S(1)} %fusion.39.p0), channel_id=1, source_target_pairs={{0,24},{4,28},{8,0},{12,4},{16,8},{20,12},{24,16},{28,20},{1,25},{... | collective-permute-start | bytes 884744 | tf_op jit(solution)/shard_map/ppermute | solution.py:521
  74.1 19.7 %zcat.6 = (bf16[4,48,768]{2,1,0:T(8,128)(2,1)}, bf16[4,48,768]{2,1,0:T(8,128)(2,1)}) custom-call(s32[8]{0:T(128)} %concatenate.117.scal.refs_0_, bf16[96,768]{1,0:T(8,128)(2,1)} %copy-done.79, bf16[96,768]{1,0:T(8,128)(2,1)} %copy-done.103, bf16[96,768]{1,0:T(8,128)(2,1)} %copy-done.104, bf16[96,768]{1,0:T(8,128)(2,1)} %copy-done.105), custom_call_target="tpu_custom_call" | custom-call | bytes 2359296 | tf_op jit(solution)/shard_map/zcat/pallas_call | solution.py:543
  95.4 37.6 %zcat.5 = (bf16[4,96,768]{2,1,0:T(8,128)(2,1)}, bf16[4,96,768]{2,1,0:T(8,128)(2,1)}) custom-call(s32[8]{0:T(128)} %concatenate.117.scal.refs_0_, bf16[192,768]{1,0:T(8,128)(2,1)} %copy-done.77, bf16[192,768]{1,0:T(8,128)(2,1)} %copy-done.93, bf16[192,768]{1,0:T(8,128)(2,1)} %copy-done.95, bf16[192,768]{1,0:T(8,128)(2,1)} %copy-done.96), custom_call_target="tpu_custom_call" | custom-call | bytes 4718592 | tf_op jit(solution)/shard_map/zcat/pallas_call | solution.py:543
  136.3 22.7 %zcat.4 = (bf16[4,64,768]{2,1,0:T(8,128)(2,1)}, bf16[4,48,768]{2,1,0:T(8,128)(2,1)}) custom-call(s32[8]{0:T(128)} %concatenate.117.scal.refs_0_, bf16[112,768]{1,0:T(8,128)(2,1)} %copy-done.78, bf16[112,768]{1,0:T(8,128)(2,1)} %copy-done.100, bf16[112,768]{1,0:T(8,128)(2,1)} %copy-done.101, bf16[112,768]{1,0:T(8,128)(2,1)} %copy-done.102), custom_call_target="tpu_custom_call" | custom-call | bytes 2752512 | tf_op jit(solution)/shard_map/zcat/pallas_call | solution.py:543
  162.1 37.6 %zcat.7 = (bf16[4,96,768]{2,1,0:T(8,128)(2,1)}, bf16[4,96,768]{2,1,0:T(8,128)(2,1)}) custom-call(s32[8]{0:T(128)} %concatenate.117.scal.refs_0_, bf16[192,768]{1,0:T(8,128)(2,1)} %copy-done.76, bf16[192,768]{1,0:T(8,128)(2,1)} %copy-done.91, bf16[192,768]{1,0:T(8,128)(2,1)} %copy-done.92, bf16[192,768]{1,0:T(8,128)(2,1)} %copy-done.94), custom_call_target="tpu_custom_call" | custom-call | bytes 4718592 | tf_op jit(solution)/shard_map/zcat/pallas_call | solution.py:543
  213.5 12.6 %collective-permute-done.26.refs_5_.refs_10_ = bf16[2,4,48,768]{3,2,1,0:T(8,128)(2,1)} collective-permute-done((bf16[2,4,48,768]{3,2,1,0:T(8,128)(2,1)S(1)}, bf16[2,4,48,768]{3,2,1,0:T(8,128)(2,1)}, u32[]{:S(2)}, u32[]{:S(2)}) %collective-permute-start.26) | collective-permute-done | bytes 589856 | tf_op jit(solution)/shard_map/ppermute | solution.py:527
  253.0 7.2 %collective-permute-done.15.refs_5_.refs_10_ = bf16[2,4,96,768]{3,2,1,0:T(8,128)(2,1)} collective-permute-done((bf16[2,4,96,768]{3,2,1,0:T(8,128)(2,1)S(1)}, bf16[2,4,96,768]{3,2,1,0:T(8,128)(2,1)}, u32[]{:S(2)}, u32[]{:S(2)}) %collective-permute-start.15) | collective-permute-done | bytes 1179680 | tf_op jit(solution)/shard_map/ppermute | solution.py:527
  285.7 7.1 %attn_fwd.2 = (f32[256,768]{1,0:T(8,128)S(1)}, bf16[256,768]{1,0:T(8,128)(2,1)S(1)}, bf16[36,256,64]{2,1,0:T(8,128)(2,1)S(1)}, f32[12,256,256]{2,1,0:T(8,128)S(1...) custom-call(s32[8]{0:T(128)S(1)} %copy-done.15, f32[256,768]{1,0:T(8,128)S(1)} %copy-done.21, ...), custom_call_target="tpu_custom_call" | custom-call | flops 7247757312 | bytes 12718592 | tf_op jit(solution)/shard_map/attn_fwd/pallas_call | solution.py:427
  300.7 11.0 %ff_fwd.2 = (f32[256,768]{1,0:T(8,128)S(1)}, bf16[256,768]{1,0:T(8,128)(2,1)S(1)}, f32[256,3072]{1,0:T(8,128)}, f32[256,3072]{1,0:T(8,128)}, bf16[256,3072]{1,0:T(8,128)(2,1)S(1)}) custom-call(s32[8]{0:T(128)S(1)} %copy-done.15, f32[256,768]{1,0:T(8,128)S(1)} %copy-done.50, f32[16,768]{1,0:T(8,128)S(1)} %copy-done.13, f32[16,3072]{1,0:T(8,128)S(1)} %bitcast.378, ...), custom_call_target="tpu_custom_call" | custom-call | flops 7247757312 | bytes 17437184 | tf_op jit(solution)/shard_map/ff_fwd/pallas_call | solution.py:441
  317.6 6.9 %attn_fwd.3 = (f32[256,768]{1,0:T(8,128)S(1)}, bf16[256,768]{1,0:T(8,128)(2,1)S(1)}, bf16[36,256,64]{2,1,0:T(8,128)(2,1)S(1)}, f32[12,256,256]{2,1,0:T(8,128)S(1...) custom-call(s32[8]{0:T(128)S(1)} %copy-done.15, f32[256,768]{1,0:T(8,128)S(1)} %copy-done.53, ...), custom_call_target="tpu_custom_call" | custom-call | flops 7247757312 | bytes 12718592 | tf_op jit(solution)/shard_map/attn_fwd/pallas_call | solution.py:427
  328.3 13.2 %ff_fwd.3 = (f32[256,768]{1,0:T(8,128)}, bf16[256,768]{1,0:T(8,128)(2,1)S(1)}, f32[256,3072]{1,0:T(8,128)}, f32[256,3072]{1,0:T(8,128)}, bf16[256,3072]{1,0:T(8,128)(2,1)S(1)}) custom-call(s32[8]{0:T(128)S(1)} %copy-done.15, f32[256,768]{1,0:T(8,128)S(1)} %get-tuple-element.73.refs_1_.refs_2_, f32[16,768]{1,0:T(8,128)S(1)} %copy-done.14, ...), custom_call_target="tpu_custom_call" | custom-call | flops 7247757312 | bytes 17437184 | tf_op jit(solution)/shard_map/ff_fwd/pallas_call | solution.py:441
  342.8 17.0 %ff_bwd.2 = (f32[256,768]{1,0:T(8,128)S(1)}, f32[16,768]{1,0:T(8,128)S(1)}, f32[16,3072]{1,0:T(8,128)S(1)}, bf16[2,2,4,96,768]{4,3,2,1,0:T(8,128)(2,1)}, bf16[2,...) custom-call(s32[8]{0:T(128)S(1)} %copy-done.15, ...), custom_call_target="tpu_custom_call" | custom-call | flops 9663676416 | bytes 26874368 | tf_op jit(solution)/shard_map/ff_bwd/pallas_call | solution.py:463
  362.0 16.1 %attn_bwd.2 = (f32[256,768]{1,0:T(8,128)S(1)}, f32[16,768]{1,0:T(8,128)S(1)}, bf16[2,2,4,48,768]{4,3,2,1,0:T(8,128)(2,1)S(1)}, bf16[2,2,4,48,768]{4,3,2,1,0:T(8,...) custom-call(s32[8]{0:T(128)S(1)} %copy-done.15, ...), custom_call_target="tpu_custom_call" | custom-call | flops 9663676416 | bytes 17437184 | tf_op jit(solution)/shard_map/attn_bwd/pallas_call | solution.py:489
  379.3 16.8 %ff_bwd.3 = (f32[256,768]{1,0:T(8,128)S(1)}, f32[16,768]{1,0:T(8,128)S(1)}, f32[16,3072]{1,0:T(8,128)S(1)}, bf16[2,2,4,96,768]{4,3,2,1,0:T(8,128)(2,1)}, bf16[2,...) custom-call(s32[8]{0:T(128)S(1)} %copy-done.15, ...), custom_call_target="tpu_custom_call" | custom-call | flops 9663676416 | bytes 26874368 | tf_op jit(solution)/shard_map/ff_bwd/pallas_call | solution.py:463
  399.0 17.4 %attn_bwd.3 = (f32[256,768]{1,0:T(8,128)}, f32[16,768]{1,0:T(8,128)}, bf16[2,2,4,64,768]{4,3,2,1,0:T(8,128)(2,1)S(1)}, bf16[2,2,4,48,768]{4,3,2,1,0:T(8,128)(2,1...) custom-call(s32[8]{0:T(128)S(1)} %copy-done.15, ...), custom_call_target="tpu_custom_call" | custom-call | flops 9663676416 | bytes 17437184 | tf_op jit(solution)/shard_map/attn_bwd/pallas_call | solution.py:489
  426.8 9.1 %collective-permute-done.57 = bf16[2,4,48,768]{3,2,1,0:T(8,128)(2,1)} collective-permute-done((bf16[2,4,48,768]{3,2,1,0:T(8,128)(2,1)}, bf16[2,4,48,768]{3,2,1,0:T(8,128)(2,1)}, u32[]{:S(2)}, u32[]{:S(2)}) %collective-permute-start.57) | collective-permute-done | bytes 589856 | tf_op jit(solution)/shard_map/ppermute | solution.py:527
  441.1 6.9 %collective-permute-done.48 = bf16[2,4,48,768]{3,2,1,0:T(8,128)(2,1)} collective-permute-done((bf16[2,4,48,768]{3,2,1,0:T(8,128)(2,1)}, bf16[2,4,48,768]{3,2,1,0:T(8,128)(2,1)}, u32[]{:S(2)}, u32[]{:S(2)}) %collective-permute-start.48) | collective-permute-done | bytes 589856 | tf_op jit(solution)/shard_map/ppermute | solution.py:527
  449.9 6.7 %collective-permute-done.55 = bf16[4,48,768]{2,1,0:T(8,128)(2,1)S(1)} collective-permute-done((bf16[4,48,768]{2,1,0:T(8,128)(2,1)S(1)}, bf16[4,48,768]{2,1,0:T(8,128)(2,1)S(1)}, u32[]{:S(2)}, u32[]{:S(2)}) %collective-permute-start.55) | collective-permute-done | bytes 294944 | tf_op jit(solution)/shard_map/ppermute | solution.py:527
  458.9 5.5 collective-permute-done.49
  466.9 6.7 %collective-permute-done.60 = bf16[96,768]{1,0:T(8,128)(2,1)S(1)} collective-permute-done((bf16[96,768]{1,0:T(8,128)(2,1)S(1)}, bf16[96,768]{1,0:T(8,128)(2,1)S(1)}, u32[]{:S(2)}, u32[]{:S(2)}) %collective-permute-start.60) | collective-permute-done | bytes 147488 | tf_op jit(solution)/shard_map/ppermute | solution.py:521
  475.7 17.2 %collective-permute-done.45 = bf16[2,4,64,768]{3,2,1,0:T(8,128)(2,1)S(1)} collective-permute-done((bf16[2,4,64,768]{3,2,1,0:T(8,128)(2,1)S(1)}, bf16[2,4,64,768]{3,2,1,0:T(8,128)(2,1)S(1)}, u32[]{:S(2)}, u32[]{:S(2)}) %collective-permute-start.45) | collective-permute-done | bytes 786464 | tf_op jit(solution)/shard_map/ppermute | solution.py:524
  499.4 5.8 collective-permute-done.46
  512.8 5.0 collective-permute-done.51
  523.7 6.8 %collective-permute-done.75 = bf16[2,4,96,768]{3,2,1,0:T(8,128)(2,1)S(1)} collective-permute-done((bf16[2,4,96,768]{3,2,1,0:T(8,128)(2,1)S(1)}, bf16[2,4,96,768]{3,2,1,0:T(8,128)(2,1)S(1)}, u32[]{:S(2)}, u32[]{:S(2)}) %collective-permute-start.75) | collective-permute-done | bytes 1179680 | tf_op jit(solution)/shard_map/ppermute | solution.py:527
  533.3 22.5 %collective-permute-done.66 = bf16[2,4,96,768]{3,2,1,0:T(8,128)(2,1)S(1)} collective-permute-done((bf16[2,4,96,768]{3,2,1,0:T(8,128)(2,1)S(1)}, bf16[2,4,96,768]{3,2,1,0:T(8,128)(2,1)S(1)}, u32[]{:S(2)}, u32[]{:S(2)}) %collective-permute-start.66) | collective-permute-done | bytes 1179680 | tf_op jit(solution)/shard_map/ppermute | solution.py:527
  558.5 5.3 collective-permute-done.76
  579.6 11.4 %collective-permute-start.68 = (bf16[192,768]{1,0:T(8,128)(2,1)S(1)}, bf16[192,768]{1,0:T(8,128)(2,1)S(1)}, u32[]{:S(2)}, u32[]{:S(2)}) collective-permute-start(bf16[192,768]{1,0:T(8,128)(2,1)S(1)} %pad_maximum_fusion.13), channel_id=1, source_target_pairs={{0,8},{4,12},{8,16},{12,20},{16,24},{20,28},{24,0},{28,4},{1,9},{5... | collective-permute-start | bytes 884744 | tf_op jit(solution)/shard_map/ppermute | solution.py:521
  591.0 16.4 %collective-permute-done.78 = bf16[192,768]{1,0:T(8,128)(2,1)S(1)} collective-permute-done((bf16[192,768]{1,0:T(8,128)(2,1)S(1)}, bf16[192,768]{1,0:T(8,128)(2,1)S(1)}, u32[]{:S(2)}, u32[]{:S(2)}) %collective-permute-start.78) | collective-permute-done | bytes 294944 | tf_op jit(solution)/shard_map/ppermute | solution.py:521
  607.6 8.0 %collective-permute-done.69 = bf16[192,768]{1,0:T(8,128)(2,1)S(1)} collective-permute-done((bf16[192,768]{1,0:T(8,128)(2,1)S(1)}, bf16[192,768]{1,0:T(8,128)(2,1)S(1)}, u32[]{:S(2)}, u32[]{:S(2)}) %collective-permute-start.69) | collective-permute-done | bytes 294944 | tf_op jit(solution)/shard_map/ppermute | solution.py:521
  (487 shorter events, 189.0 us)
Async XLA Ops:
  12.9 41.9 %collective-permute-start.11 = (bf16[192,768]{1,0:T(8,128)(2,1)S(1)}, bf16[192,768]{1,0:T(8,128)(2,1)S(1)}, u32[]{:S(2)}, u32[]{:S(2)}) collective-permute-start(bf16[192,768]{1,0:T(8,128)(2,1)S(1)} %fusion.37.p0), channel_id=1, source_target_pairs={{0,8},{4,12},{8,16},{12,20},{16,24},{20,28},{24,0},{28,4},{1,9},{5... | collective-permute-start | bytes 884744 | tf_op jit(solution)/shard_map/ppermute | solution.py:521
  19.8 38.3 %collective-permute-start.12 = (bf16[192,768]{1,0:T(8,128)(2,1)S(1)}, bf16[192,768]{1,0:T(8,128)(2,1)S(1)}, u32[]{:S(2)}, u32[]{:S(2)}) collective-permute-start(bf16[192,768]{1,0:T(8,128)(2,1)S(1)} %fusion.37.p0), channel_id=1, source_target_pairs={{0,16},{4,20},{8,24},{12,28},{16,0},{20,4},{24,8},{28,12},{1,17},{... | collective-permute-start | bytes 884744 | tf_op jit(solution)/shard_map/ppermute | solution.py:521
  19.9 73.9 %collective-permute-start.13 = (bf16[192,768]{1,0:T(8,128)(2,1)S(1)}, bf16[192,768]{1,0:T(8,128)(2,1)S(1)}, u32[]{:S(2)}, u32[]{:S(2)}) collective-permute-start(bf16[192,768]{1,0:T(8,128)(2,1)S(1)} %fusion.37.p0), channel_id=1, source_target_pairs={{0,24},{4,28},{8,0},{12,4},{16,8},{20,12},{24,16},{28,20},{1,25},{... | collective-permute-start | bytes 884744 | tf_op jit(solution)/shard_map/ppermute | solution.py:521
  24.0 109.0 %collective-permute-start.2 = (bf16[112,768]{1,0:T(8,128)(2,1)S(1)}, bf16[112,768]{1,0:T(8,128)(2,1)S(1)}, u32[]{:S(2)}, u32[]{:S(2)}) collective-permute-start(bf16[112,768]{1,0:T(8,128)(2,1)S(1)} %concatenate.123.p0), channel_id=1, source_target_pairs={{0,24},{4,28},{8,0},{12,4},{16,8},{20,12},{24,16},{28,20},{1,25},{... | collective-permute-start | bytes 516104 | tf_op jit(solution)/shard_map/ppermute | solution.py:521
  45.0 89.3 %collective-permute-start.33 = (bf16[192,768]{1,0:T(8,128)(2,1)S(1)}, bf16[192,768]{1,0:T(8,128)(2,1)S(1)}, u32[]{:S(2)}, u32[]{:S(2)}) collective-permute-start(bf16[192,768]{1,0:T(8,128)(2,1)S(1)} %fusion.39.p0), channel_id=1, source_target_pairs={{0,8},{4,12},{8,16},{12,20},{16,24},{20,28},{24,0},{28,4},{1,9},{5... | collective-permute-start | bytes 884744 | tf_op jit(solution)/shard_map/ppermute | solution.py:521
  54.8 81.0 %collective-permute-start.34 = (bf16[192,768]{1,0:T(8,128)(2,1)S(1)}, bf16[192,768]{1,0:T(8,128)(2,1)S(1)}, u32[]{:S(2)}, u32[]{:S(2)}) collective-permute-start(bf16[192,768]{1,0:T(8,128)(2,1)S(1)} %fusion.39.p0), channel_id=1, source_target_pairs={{0,16},{4,20},{8,24},{12,28},{16,0},{20,4},{24,8},{28,12},{1,17},{... | collective-permute-start | bytes 884744 | tf_op jit(solution)/shard_map/ppermute | solution.py:521
  58.2 100.9 %collective-permute-start.35 = (bf16[192,768]{1,0:T(8,128)(2,1)S(1)}, bf16[192,768]{1,0:T(8,128)(2,1)S(1)}, u32[]{:S(2)}, u32[]{:S(2)}) collective-permute-start(bf16[192,768]{1,0:T(8,128)(2,1)S(1)} %fusion.39.p0), channel_id=1, source_target_pairs={{0,24},{4,28},{8,0},{12,4},{16,8},{20,12},{24,16},{28,20},{1,25},{... | collective-permute-start | bytes 884744 | tf_op jit(solution)/shard_map/ppermute | solution.py:521
  93.8 66.7 %collective-permute-start.25 = (bf16[4,48,768]{2,1,0:T(8,128)(2,1)}, bf16[4,48,768]{2,1,0:T(8,128)(2,1)}, u32[]{:S(2)}, u32[]{:S(2)}) collective-permute-start(bf16[4,48,768]{2,1,0:T(8,128)(2,1)} %get-tuple-element.71), channel_id=1, source_target_pairs={{0,4},{4,0},{8,12},{12,8},{16,20},{20,16},{24,28},{28,24},{1,5},{5... | collective-permute-start | bytes 884744 | tf_op jit(solution)/shard_map/ppermute | solution.py:524
  133.7 69.9 %collective-permute-start.14 = (bf16[4,96,768]{2,1,0:T(8,128)(2,1)}, bf16[4,96,768]{2,1,0:T(8,128)(2,1)S(1)}, u32[]{:S(2)}, u32[]{:S(2)}) collective-permute-start(bf16[4,96,768]{2,1,0:T(8,128)(2,1)} %get-tuple-element.68), channel_id=1, source_target_pairs={{0,4},{4,0},{8,12},{12,8},{16,20},{20,16},{24,28},{28,24},{1,5},{5... | collective-permute-start | bytes 1769480 | tf_op jit(solution)/shard_map/ppermute | solution.py:524
  134.3 71.4 %collective-permute-start.18 = (bf16[4,96,768]{2,1,0:T(8,128)(2,1)}, bf16[4,96,768]{2,1,0:T(8,128)(2,1)}, u32[]{:S(2)}, u32[]{:S(2)}) collective-permute-start(bf16[4,96,768]{2,1,0:T(8,128)(2,1)} %get-tuple-element.69), channel_id=1, source_target_pairs={{0,2},{1,3},{2,0},{3,1},{4,6},{5,7},{6,4},{7,5},{8,10},{9,11},{10,... | collective-permute-start | bytes 1769480 | tf_op jit(solution)/shard_map/ppermute | solution.py:527
  135.8 63.8 %collective-permute-start.29 = (bf16[4,48,768]{2,1,0:T(8,128)(2,1)}, bf16[4,48,768]{2,1,0:T(8,128)(2,1)S(1)}, u32[]{:S(2)}, u32[]{:S(2)}) collective-permute-start(bf16[4,48,768]{2,1,0:T(8,128)(2,1)} %get-tuple-element.72), channel_id=1, source_target_pairs={{0,2},{1,3},{2,0},{3,1},{4,6},{5,7},{6,4},{7,5},{8,10},{9,11},{10,... | collective-permute-start | bytes 884744 | tf_op jit(solution)/shard_map/ppermute | solution.py:527
  159.1 43.0 %collective-permute-start.3 = (bf16[4,64,768]{2,1,0:T(8,128)(2,1)}, bf16[4,64,768]{2,1,0:T(8,128)(2,1)S(1)}, u32[]{:S(2)}, u32[]{:S(2)}) collective-permute-start(bf16[4,64,768]{2,1,0:T(8,128)(2,1)} %get-tuple-element.65), channel_id=1, source_target_pairs={{0,4},{4,0},{8,12},{12,8},{16,20},{20,16},{24,28},{28,24},{1,5},{5... | collective-permute-start | bytes 1179656 | tf_op jit(solution)/shard_map/ppermute | solution.py:524
  160.5 40.9 %collective-permute-start.7 = (bf16[4,48,768]{2,1,0:T(8,128)(2,1)}, bf16[4,48,768]{2,1,0:T(8,128)(2,1)}, u32[]{:S(2)}, u32[]{:S(2)}) collective-permute-start(bf16[4,48,768]{2,1,0:T(8,128)(2,1)} %get-tuple-element.66), channel_id=1, source_target_pairs={{0,2},{1,3},{2,0},{3,1},{4,6},{5,7},{6,4},{7,5},{8,10},{9,11},{10,... | collective-permute-start | bytes 884744 | tf_op jit(solution)/shard_map/ppermute | solution.py:527
  252.7 45.7 %collective-permute-start.20 = (bf16[2,4,96,768]{3,2,1,0:T(8,128)(2,1)S(1)}, bf16[2,4,96,768]{3,2,1,0:T(8,128)(2,1)}, u32[]{:S(2)}, u32[]{:S(2)}) collective-permute-start(bf16[2,4,96,768]{3,2,1,0:T(8,128)(2,1)S(1)} %pad_maximum_fusion.1.refs_8_.refs_13_), channel_id=1, source_target_pairs={{0,1},{1,0},{2,3},{3,2},{4,5},{5,4},{6,7},{7,6},{8,9},{9,8},{10,11... | collective-permute-start | bytes 3538952 | tf_op jit(solution)/shard_map/ppermute | solution.py:530
  260.2 38.2 %collective-permute-start.37 = (bf16[2,4,96,768]{3,2,1,0:T(8,128)(2,1)S(1)}, bf16[2,4,96,768]{3,2,1,0:T(8,128)(2,1)}, u32[]{:S(2)}, u32[]{:S(2)}) collective-permute-start(bf16[2,4,96,768]{3,2,1,0:T(8,128)(2,1)S(1)} %pad_maximum_fusion.2.refs_4_.refs_9_), channel_id=1, source_target_pairs={{0,2},{1,3},{2,0},{3,1},{4,6},{5,7},{6,4},{7,5},{8,10},{9,11},{10,... | collective-permute-start | bytes 3538952 | tf_op jit(solution)/shard_map/ppermute | solution.py:527
  260.7 38.2 %collective-permute-start.41 = (bf16[2,4,96,768]{3,2,1,0:T(8,128)(2,1)}, bf16[2,4,96,768]{3,2,1,0:T(8,128)(2,1)}, u32[]{:S(2)}, u32[]{:S(2)}) collective-permute-start(bf16[2,4,96,768]{3,2,1,0:T(8,128)(2,1)} %pad_maximum_fusion.3.refs_8_.refs_13_), channel_id=1, source_target_pairs={{0,4},{4,0},{8,12},{12,8},{16,20},{20,16},{24,28},{28,24},{1,5},{5... | collective-permute-start | bytes 3538952 | tf_op jit(solution)/shard_map/ppermute | solution.py:524
  265.8 33.2 %collective-permute-start.17 = (bf16[2,4,96,768]{3,2,1,0:T(8,128)(2,1)}, bf16[2,4,96,768]{3,2,1,0:T(8,128)(2,1)}, u32[]{:S(2)}, u32[]{:S(2)}) collective-permute-start(bf16[2,4,96,768]{3,2,1,0:T(8,128)(2,1)} %collective-permute-done.15.refs_5_.refs_10_), channel_id=1, source_target_pairs={{0,1},{1,0},{2,3},{3,2},{4,5},{5,4},{6,7},{7,6},{8,9},{9,8},{10,11... | collective-permute-start | bytes 3538952 | tf_op jit(solution)/shard_map/ppermute | solution.py:530
  378.8 38.3 %collective-permute-start.56 = (bf16[2,2,4,48,768]{4,3,2,1,0:T(8,128)(2,1)S(1)}, bf16[2,2,4,48,768]{4,3,2,1,0:T(8,128)(2,1)}, u32[]{:S(2)}, u32[]{:S(2)}) collective-permute-start(bf16[2,2,4,48,768]{4,3,2,1,0:T(8,128)(2,1)S(1)} %get-tuple-element.111), channel_id=1, source_target_pairs={{0,1},{1,0},{2,3},{3,2},{4,5},{5,4},{6,7},{7,6},{8,9},{9,8},{10,11... | collective-permute-start | bytes 3538952 | tf_op jit(solution)/shard_map/ppermute | solution.py:530
  379.2 40.7 %collective-permute-start.53 = (bf16[2,2,4,48,768]{4,3,2,1,0:T(8,128)(2,1)S(1)}, bf16[2,2,4,48,768]{4,3,2,1,0:T(8,128)(2,1)}, u32[]{:S(2)}, u32[]{:S(2)}) collective-permute-start(bf16[2,2,4,48,768]{4,3,2,1,0:T(8,128)(2,1)S(1)} %get-tuple-element.109), channel_id=1, source_target_pairs={{0,1},{1,0},{2,3},{3,2},{4,5},{5,4},{6,7},{7,6},{8,9},{9,8},{10,11... | collective-permute-start | bytes 3538952 | tf_op jit(solution)/shard_map/ppermute | solution.py:530
  417.0 41.5 %collective-permute-start.44 = (bf16[2,2,4,64,768]{4,3,2,1,0:T(8,128)(2,1)}, bf16[2,2,4,64,768]{4,3,2,1,0:T(8,128)(2,1)}, u32[]{:S(2)}, u32[]{:S(2)}) collective-permute-start(bf16[2,2,4,64,768]{4,3,2,1,0:T(8,128)(2,1)} %get-tuple-element.105), channel_id=1, source_target_pairs={{0,1},{1,0},{2,3},{3,2},{4,5},{5,4},{6,7},{7,6},{8,9},{9,8},{10,11... | collective-permute-start | bytes 4718600 | tf_op jit(solution)/shard_map/ppermute | solution.py:530
  426.8 66.8 %collective-permute-start.74 = (bf16[2,2,4,96,768]{4,3,2,1,0:T(8,128)(2,1)}, bf16[2,2,4,96,768]{4,3,2,1,0:T(8,128)(2,1)S(1)}, u32[]{:S(2)}, u32[]{:S(2)}) collective-permute-start(bf16[2,2,4,96,768]{4,3,2,1,0:T(8,128)(2,1)} %get-tuple-element.119), channel_id=1, source_target_pairs={{0,1},{1,0},{2,3},{3,2},{4,5},{5,4},{6,7},{7,6},{8,9},{9,8},{10,11... | collective-permute-start | bytes 7077896 | tf_op jit(solution)/shard_map/ppermute | solution.py:530
  435.9 60.1 %collective-permute-start.71 = (bf16[2,2,4,96,768]{4,3,2,1,0:T(8,128)(2,1)}, bf16[2,2,4,96,768]{4,3,2,1,0:T(8,128)(2,1)S(1)}, u32[]{:S(2)}, u32[]{:S(2)}) collective-permute-start(bf16[2,2,4,96,768]{4,3,2,1,0:T(8,128)(2,1)} %get-tuple-element.117), channel_id=1, source_target_pairs={{0,1},{1,0},{2,3},{3,2},{4,5},{5,4},{6,7},{7,6},{8,9},{9,8},{10,11... | collective-permute-start | bytes 7077896 | tf_op jit(solution)/shard_map/ppermute | solution.py:530
  449.8 48.9 %collective-permute-start.65 = (bf16[2,2,4,96,768]{4,3,2,1,0:T(8,128)(2,1)S(1)}, bf16[2,2,4,96,768]{4,3,2,1,0:T(8,128)(2,1)S(1)}, u32[]{:S(2)}, u32[]{:S(2)}) collective-permute-start(bf16[2,2,4,96,768]{4,3,2,1,0:T(8,128)(2,1)S(1)} %copy-done.109), channel_id=1, source_target_pairs={{0,1},{1,0},{2,3},{3,2},{4,5},{5,4},{6,7},{7,6},{8,9},{9,8},{10,11... | collective-permute-start | bytes 7077896 | tf_op jit(solution)/shard_map/ppermute | solution.py:530
  495.3 35.2 %collective-permute-start.75 = (bf16[2,4,96,768]{3,2,1,0:T(8,128)(2,1)S(1)}, bf16[2,4,96,768]{3,2,1,0:T(8,128)(2,1)S(1)}, u32[]{:S(2)}, u32[]{:S(2)}) collective-permute-start(bf16[2,4,96,768]{3,2,1,0:T(8,128)(2,1)S(1)} %get-tuple-element.151), channel_id=1, source_target_pairs={{0,2},{1,3},{2,0},{3,1},{4,6},{5,7},{6,4},{7,5},{8,10},{9,11},{10,... | collective-permute-start | bytes 3538952 | tf_op jit(solution)/shard_map/ppermute | solution.py:527
  496.9 35.6 %collective-permute-start.72 = (bf16[2,4,96,768]{3,2,1,0:T(8,128)(2,1)S(1)}, bf16[2,4,96,768]{3,2,1,0:T(8,128)(2,1)S(1)}, u32[]{:S(2)}, u32[]{:S(2)}) collective-permute-start(bf16[2,4,96,768]{3,2,1,0:T(8,128)(2,1)S(1)} %get-tuple-element.149), channel_id=1, source_target_pairs={{0,4},{4,0},{8,12},{12,8},{16,20},{20,16},{24,28},{28,24},{1,5},{5... | collective-permute-start | bytes 3538952 | tf_op jit(solution)/shard_map/ppermute | solution.py:524
  512.5 43.3 %collective-permute-start.66 = (bf16[2,4,96,768]{3,2,1,0:T(8,128)(2,1)S(1)}, bf16[2,4,96,768]{3,2,1,0:T(8,128)(2,1)S(1)}, u32[]{:S(2)}, u32[]{:S(2)}) collective-permute-start(bf16[2,4,96,768]{3,2,1,0:T(8,128)(2,1)S(1)} %get-tuple-element.147), channel_id=1, source_target_pairs={{0,2},{1,3},{2,0},{3,1},{4,6},{5,7},{6,4},{7,5},{8,10},{9,11},{10,... | collective-permute-start | bytes 3538952 | tf_op jit(solution)/shard_map/ppermute | solution.py:527
  517.9 39.9 %collective-permute-start.63 = (bf16[2,4,96,768]{3,2,1,0:T(8,128)(2,1)S(1)}, bf16[2,4,96,768]{3,2,1,0:T(8,128)(2,1)S(1)}, u32[]{:S(2)}, u32[]{:S(2)}) collective-permute-start(bf16[2,4,96,768]{3,2,1,0:T(8,128)(2,1)S(1)} %get-tuple-element.145), channel_id=1, source_target_pairs={{0,4},{4,0},{8,12},{12,8},{16,20},{20,16},{24,28},{28,24},{1,5},{5... | collective-permute-start | bytes 3538952 | tf_op jit(solution)/shard_map/ppermute | solution.py:524
  532.8 35.6 %collective-permute-start.73 = (bf16[4,96,768]{2,1,0:T(8,128)(2,1)S(1)}, bf16[4,96,768]{2,1,0:T(8,128)(2,1)S(1)}, u32[]{:S(2)}, u32[]{:S(2)}) collective-permute-start(bf16[4,96,768]{2,1,0:T(8,128)(2,1)S(1)} %get-tuple-element.159), channel_id=1, source_target_pairs={{0,2},{1,3},{2,0},{3,1},{4,6},{5,7},{6,4},{7,5},{8,10},{9,11},{10,... | collective-permute-start | bytes 1769480 | tf_op jit(solution)/shard_map/ppermute | solution.py:527
  568.7 38.7 %collective-permute-start.78 = (bf16[192,768]{1,0:T(8,128)(2,1)S(1)}, bf16[192,768]{1,0:T(8,128)(2,1)S(1)}, u32[]{:S(2)}, u32[]{:S(2)}) collective-permute-start(bf16[192,768]{1,0:T(8,128)(2,1)S(1)} %pad_maximum_fusion.17), channel_id=1, source_target_pairs={{0,16},{4,20},{8,24},{12,28},{16,0},{20,4},{24,8},{28,12},{1,17},{... | collective-permute-start | bytes 884744 | tf_op jit(solution)/shard_map/ppermute | solution.py:521
  568.8 38.6 %collective-permute-start.77 = (bf16[192,768]{1,0:T(8,128)(2,1)S(1)}, bf16[192,768]{1,0:T(8,128)(2,1)S(1)}, u32[]{:S(2)}, u32[]{:S(2)}) collective-permute-start(bf16[192,768]{1,0:T(8,128)(2,1)S(1)} %pad_maximum_fusion.16), channel_id=1, source_target_pairs={{0,8},{4,12},{8,16},{12,20},{16,24},{20,28},{24,0},{28,4},{1,9},{5... | collective-permute-start | bytes 884744 | tf_op jit(solution)/shard_map/ppermute | solution.py:521
  579.3 36.4 %collective-permute-start.69 = (bf16[192,768]{1,0:T(8,128)(2,1)S(1)}, bf16[192,768]{1,0:T(8,128)(2,1)S(1)}, u32[]{:S(2)}, u32[]{:S(2)}) collective-permute-start(bf16[192,768]{1,0:T(8,128)(2,1)S(1)} %pad_maximum_fusion.14), channel_id=1, source_target_pairs={{0,16},{4,20},{8,24},{12,28},{16,0},{20,4},{24,8},{28,12},{1,17},{... | collective-permute-start | bytes 884744 | tf_op jit(solution)/shard_map/ppermute | solution.py:521
  579.6 36.1 %collective-permute-start.68 = (bf16[192,768]{1,0:T(8,128)(2,1)S(1)}, bf16[192,768]{1,0:T(8,128)(2,1)S(1)}, u32[]{:S(2)}, u32[]{:S(2)}) collective-permute-start(bf16[192,768]{1,0:T(8,128)(2,1)S(1)} %pad_maximum_fusion.13), channel_id=1, source_target_pairs={{0,8},{4,12},{8,16},{12,20},{16,24},{20,28},{24,0},{28,4},{1,9},{5... | collective-permute-start | bytes 884744 | tf_op jit(solution)/shard_map/ppermute | solution.py:521
  (158 other events, 2646.0 us)

commit v2 on v1

--- a/solution.py
+++ b/solution.py
@@ -20,7 +20,7 @@
 F32 = jnp.float32
 MIB = 1 << 20
 
-ANY = pl.BlockSpec(memory_space=pl.ANY)
+ANY = pl.BlockSpec(memory_space=pltpu.HBM)
 SMEM = pl.BlockSpec(memory_space=pltpu.SMEM)
 VMEM = pl.BlockSpec(memory_space=pltpu.VMEM)
 
@@ -89,6 +89,7 @@
     def load_c(self, scal, pieces, m, dst):
         if not self.fast:
             return [(pieces[2], dst)]
+        pieces = pieces[-8:]
         return [
             (
                 ref.at[ri, :, pl.ds(m * 48, 48), pl.ds(j * 384, 384)],
@@ -110,6 +111,7 @@
                     c = lax.rem(mc + rc, 2)
                     yield h, ri, x, y * 2 + c, pieces[h * 4 + bi]
 
+
     def blocks(self, scal):
         if not self.fast:
             return [(f, 0, 0) for f in range(4)]
@@ -124,7 +126,7 @@
             x = lax.rem(scal[3] + rx, 2)
             for h in range(2):
                 first, second = (rx, ry) if h == 0 else (ry, rx)
-                res.append((src.at[:, x, h], outs[rc * 2 + h].at[first, second, :, pl.ds(m * 48, 48)]))
+                res.append((src.at[:, x, h], outs[rc].at[h, first, second, :, pl.ds(m * 48, 48)]))
         return res
 
     def store_c(self, scal, src, outs, m):
@@ -140,7 +142,7 @@
                         res.append(
                             (
                                 src.at[:, f, j, h, :, pl.ds(pl.multiple_of(x * 384, 384), 384)],
-                                outs[rc * 2 + h].at[first, second, :, pl.ds(m * 48, 48), pl.ds(j * 384, 384)],
+                                outs[rc].at[h, first, second, :, pl.ds(m * 48, 48), pl.ds(j * 384, 384)],
                             )
                         )
         return res
@@ -150,8 +152,21 @@
         for _, rc, ry in self.blocks(scal):
             for rx in range(2):
                 x = lax.rem(scal[3] + rx, 2)
-                res.append((src.at[:, x], outs[rc * 2].at[rx, ry, :, pl.ds(48, 16)]))
+                for h in range(2):
+                    first, second = (rx, ry) if h == 0 else (ry, rx)
+                    res.append((src.at[h, :, x], outs[rc].at[h, first, second, :, pl.ds(48, 16)]))
         return res
+
+
+def flat(pieces):
+    arrays, finds = [], []
+    for piece in pieces:
+        array, index = piece if isinstance(piece, tuple) else (piece, None)
+        place = next((i for i, v in enumerate(arrays) if v is array), len(arrays))
+        if place == len(arrays):
+            arrays.append(array)
+        finds.append((place, index))
+    return arrays, lambda refs: [refs[i] if j is None else refs[i].at[j] for i, j in finds]
 
 
 def start(copies, sems, base=0):
@@ -166,9 +181,9 @@
         c.wait()
 
 
-def attn_fwd(plan, npieces, m, *refs):
+def attn_fwd(plan, npieces, find, m, *refs):
     scal, x_ref, vec_ref, pb_ref = refs[:4]
-    pieces = refs[4 : 4 + npieces]
+    pieces = find(refs[4 : 4 + npieces])
     x1_ref, a1_ref, un_ref, p_ref, o_ref, a2_ref = refs[4 + npieces : 10 + npieces]
     wa, sems = refs[10 + npieces :]
     loads = start(plan.load_a(scal, pieces, m, wa), sems)
@@ -202,9 +217,9 @@
     x1_ref[...] = x_ref[...] + (jnp.concatenate(z, axis=1) + vec_ref[BO : BO + 1])
 
 
-def ff_fwd(plan, npieces, mb, mc, last, *refs):
+def ff_fwd(plan, npieces, find, mb, mc, last, *refs):
     scal, x1_ref, vec_ref, hid_ref = refs[:4]
-    pieces = refs[4 : 4 + npieces]
+    pieces = find(refs[4 : 4 + npieces])
     x2_ref, a3_ref, sl_ref, n4_ref, a4_ref = refs[4 + npieces : 9 + npieces]
     wb, wc, sems = refs[9 + npieces :]
     load_b = start(plan.load_b(scal, pieces, mb, wb), sems)
@@ -255,9 +270,9 @@
     x2_ref[...] = x2
 
 
-def ff_bwd(plan, npieces, nouts, mb, mc, last, *refs):
+def ff_bwd(plan, npieces, find, nouts, mb, mc, last, *refs):
     scal, dy_ref, x1_ref, a3_ref, sl_ref, n4_ref, a4_ref, vec_ref, hid_ref = refs[:9]
-    pieces = refs[9 : 9 + npieces]
+    pieces = find(refs[9 : 9 + npieces])
     dx1_ref, gv_ref, gh_ref = refs[9 + npieces : 12 + npieces]
     outs = refs[12 + npieces : 12 + npieces + nouts]
     wb, wc, gb, gc, da4, du_ref, sems = refs[12 + npieces + nouts :]
@@ -278,7 +293,7 @@
         cols = slice(768 * z, 768 * z + 768)
         da4[:, cols] = dot(dz2, wc[z].reshape(D, 768))
         gc[z] = dot(dz2t, a4_ref[:, cols]).astype(BF).reshape(4, 2, 2, 48, 768)
-    saves = start(plan.store_c(scal, gc, outs, mc), sems, base)
+    saves = start(plan.store_c(scal, gc, outs, 1), sems, base)
     base += len(saves)
 
     def rows_step(i, carry):
@@ -313,7 +328,7 @@
         cols = pl.ds(pl.multiple_of(f * 768, 768), 768)
         du = du_ref[:, cols]
         gb[i] = dot(a3t, du).astype(BF).reshape(4, 2, 2, 48, 768)
-        more = start(plan.store_ab(scal, gb.at[i], outs, mb, f, rc, ry), sems, base)
+        more = start(plan.store_ab(scal, gb.at[i], outs, 0, f, rc, ry), sems, base)
         base += len(more)
         saves += more
         da3 += dot_nt(du, wb[:, :, :, :, cols].reshape(D, 768))
@@ -325,12 +340,12 @@
     wait(saves)
 
 
-def attn_bwd(plan, npieces, nouts, m, fold, *refs):
+def attn_bwd(plan, npieces, find, nouts, m, fold, *refs):
     scal, dx1_ref, x_ref, a1_ref, un_ref, p_ref, o_ref, a2_ref, vec_ref = refs[:9]
     pos = 9
     others = refs[pos : pos + (5 if fold else 0)]
     pos += len(others)
-    pieces = refs[pos : pos + npieces]
+    pieces = find(refs[pos : pos + npieces])
     pos += npieces
     dx_ref, gv_ref = refs[pos : pos + 2]
     outs = refs[pos + 2 : pos + 2 + nouts]
@@ -402,18 +417,54 @@
             c96 = slice(96 * d, 96 * d + 96)
             c384 = slice(384 * d, 384 * d + 384)
             low = jnp.concatenate([v0[:, c96], v1[:, c96], jnp.zeros((VROWS, 576), F32)], axis=1)
-            vblk[d // 2, d % 2] = (low + jnp.concatenate([gh0[:, c384], gh1[:, c384]], axis=1)).astype(BF)
+            vblk[0, d // 2, d % 2] = low.astype(BF)
+            vblk[1, d // 2, d % 2] = jnp.concatenate([gh0[:, c384], gh1[:, c384]], axis=1).astype(BF)
         more = start(plan.store_vec(scal, vblk, outs), sems, base)
         saves += more
     wait(saves)
 
 
-def params(mib):
-    return pltpu.CompilerParams(vmem_limit_bytes=mib * MIB)
-
-
 def cost(flops, nbytes):
     return pl.CostEstimate(flops=int(flops), bytes_accessed=int(nbytes), transcendentals=0)
+
+
+class Seq:
+    def __init__(self, chained):
+        self.chained = chained
+        self.token = None
+        self.held = []
+        self.carried = []
+
+    def hold(self, *arrays):
+        self.held += arrays
+
+    def carry(self, *arrays):
+        self.carried = list(arrays)
+
+    def __call__(self, kernel, out_shape, in_specs, out_specs, args, scratch=(), mib=24, **options):
+        deps = [self.token] if self.chained and self.token is not None else []
+        deps += self.held
+        carried = self.carried
+        self.held, self.carried = [], []
+        n, k, m, q = len(args), len(deps), len(carried), len(out_shape)
+
+        def body(*refs):
+            first = n + k + m
+            kernel(*refs[:n], *refs[first : first + q], *refs[first + q + m :])
+
+        res = pl.pallas_call(
+            body,
+            out_shape=tuple(out_shape) + tuple(S(v.shape, v.dtype) for v in carried),
+            in_specs=list(in_specs) + [ANY] * (k + m),
+            out_specs=tuple(out_specs) + (ANY,) * m,
+            scratch_shapes=list(scratch),
+            input_output_aliases={n + k + i: q + i for i in range(m)},
+            compiler_params=pltpu.CompilerParams(vmem_limit_bytes=mib * MIB),
+            **options,
+        )(*args, *deps, *carried)
+        self.token = res[0]
+        self.carried = list(res[q:])
+        return res[:q]
 
 
 WA = pltpu.VMEM((4, 2, 2, 48, FF), BF)
@@ -422,88 +473,79 @@
 WBYTES = D * FF * 2
 
 
-def call_attn_fwd(plan, scal, x, vec, pbias, pieces, m):
+def call_attn_fwd(seq, plan, scal, x, vec, pbias, pieces, m):
+    pieces, find = flat(pieces)
     n = len(pieces)
-    return pl.pallas_call(
-        functools.partial(attn_fwd, plan, n, m),
-        out_shape=(S((T, D), F32), S((T, D), BF), S((36, T, HD), BF), S((HEADS, T, T), F32), S((T, D), F32), S((T, D), BF)),
-        in_specs=[SMEM, VMEM, VMEM, VMEM] + [ANY] * n,
-        out_specs=[VMEM] * 6,
-        scratch_shapes=[WA, pltpu.SemaphoreType.DMA((32,))],
-        compiler_params=params(40),
+    return seq(
+        functools.partial(attn_fwd, plan, n, find, m),
+        (S((T, D), F32), S((T, D), BF), S((36, T, HD), BF), S((HEADS, T, T), F32), S((T, D), F32), S((T, D), BF)),
+        [SMEM, VMEM, VMEM, VMEM] + [ANY] * n,
+        [VMEM] * 6,
+        (scal, x, vec, pbias, *pieces),
+        [WA, pltpu.SemaphoreType.DMA((32,))],
         cost_estimate=cost(2 * T * D * FF * 6, WBYTES + 8e6),
         name="attn_fwd",
-    )(scal, x, vec, pbias, *pieces)
-
-
-def call_ff_fwd(plan, scal, x1, vec, hid, pieces, mb, mc, last):
+        mib=64,
+    )
+
+
+def call_ff_fwd(seq, plan, scal, x1, vec, hid, pieces, mb, mc, last):
+    pieces, find = flat(pieces)
     n = len(pieces)
-    return pl.pallas_call(
-        functools.partial(ff_fwd, plan, n, mb, mc, last),
-        out_shape=(S((T, D), F32), S((T, D), BF), S((T, FF), F32), S((T, FF), F32), S((T, FF), BF)),
-        in_specs=[SMEM, VMEM, VMEM, VMEM] + [ANY] * n,
-        out_specs=[VMEM] * 5,
-        scratch_shapes=[WA, WC, pltpu.SemaphoreType.DMA((48,))],
-        compiler_params=params(40),
+    return seq(
+        functools.partial(ff_fwd, plan, n, find, mb, mc, last),
+        (S((T, D), F32), S((T, D), BF), S((T, FF), F32), S((T, FF), F32), S((T, FF), BF)),
+        [SMEM, VMEM, VMEM, VMEM] + [ANY] * n,
+        [VMEM] * 5,
+        (scal, x1, vec, hid, *pieces),
+        [WA, WC, pltpu.SemaphoreType.DMA((48,))],
         cost_estimate=cost(2 * T * D * FF * 6, 2 * WBYTES + 8e6),
         name="ff_fwd",
-    )(scal, x1, vec, hid, *pieces)
+        mib=64,
+    )
 
 
 def grad_shapes(plan, n, extra=0):
     if not plan.fast:
-        shapes = [S((4, 4, 2, 2, 48, D), BF)] * n
-        return shapes
-    return [S((2, 2, 4, n * 48 + e, D), BF) for e in (extra, 0, extra, 0)]
-
-
-def call_ff_bwd(plan, scal, dy, x1, a3, sl, n4, a4, vec, hid, pieces, mb, mc, last):
+        return [S((4, 4, 2, 2, 48, D), BF)] * n
+    return [S((2, 2, 2, 4, n * 48 + extra, D), BF)] * 2
+
+
+def call_ff_bwd(seq, plan, scal, dy, x1, a3, sl, n4, a4, vec, hid, pieces, mb, mc, last):
+    pieces, find = flat(pieces)
     n = len(pieces)
     g = grad_shapes(plan, 2)
-    res = pl.pallas_call(
-        functools.partial(ff_bwd, plan, n, len(g), mb, mc, last),
-        out_shape=(S((T, D), F32), S((VROWS, D), F32), S((VROWS, FF), F32), *g),
-        in_specs=[SMEM] + [VMEM] * 8 + [ANY] * n,
-        out_specs=[VMEM] * 3 + [ANY] * len(g),
-        scratch_shapes=[
-            WA,
-            WC,
-            WC,
-            WC,
-            pltpu.VMEM((T, FF), F32),
-            pltpu.VMEM((T, FF), BF),
-            pltpu.SemaphoreType.DMA((112,)),
-        ],
-        compiler_params=params(50),
+    res = seq(
+        functools.partial(ff_bwd, plan, n, find, len(g), mb, mc, last),
+        (S((T, D), F32), S((VROWS, D), F32), S((VROWS, FF), F32), *g),
+        [SMEM] + [VMEM] * 8 + [ANY] * n,
+        [VMEM] * 3 + [ANY] * len(g),
+        (scal, dy, x1, a3, sl, n4, a4, vec, hid, *pieces),
+        [WA, WC, WC, WC, pltpu.VMEM((T, FF), F32), pltpu.VMEM((T, FF), BF), pltpu.SemaphoreType.DMA((112,))],
         cost_estimate=cost(2 * T * D * FF * 8, 4 * WBYTES + 8e6),
         name="ff_bwd",
-    )(scal, dy, x1, a3, sl, n4, a4, vec, hid, *pieces)
+        mib=64,
+    )
     return res[:3], res[3:]
 
 
-def call_attn_bwd(plan, scal, dx1, x, a1, un, p, o, a2, vec, pieces, m, others):
+def call_attn_bwd(seq, plan, scal, dx1, x, a1, un, p, o, a2, vec, pieces, m, others):
+    pieces, find = flat(pieces)
     n = len(pieces)
     fold = len(others) > 0
     g = grad_shapes(plan, 1, 16 if fold else 0)
-    vblk = [pltpu.VMEM((4, 2, VROWS, D), BF)] if fold else []
-    res = pl.pallas_call(
-        functools.partial(attn_bwd, plan, n, len(g), m, fold),
-        out_shape=(S((T, D), F32), S((VROWS, D), F32), *g),
-        in_specs=[SMEM] + [VMEM] * (8 + len(others)) + [ANY] * n,
-        out_specs=[VMEM] * 2 + [ANY] * len(g),
-        scratch_shapes=[
-            WA,
-            WC,
-            pltpu.VMEM((T, FF), BF),
-            pltpu.VMEM((T, 1024), BF),
-            pltpu.VMEM((T, D), BF),
-            *vblk,
-            pltpu.SemaphoreType.DMA((64,)),
-        ],
-        compiler_params=params(40),
+    vblk = [pltpu.VMEM((2, 4, 2, VROWS, D), BF)] if fold else []
+    res = seq(
+        functools.partial(attn_bwd, plan, n, find, len(g), m, fold),
+        (S((T, D), F32), S((VROWS, D), F32), *g),
+        [SMEM] + [VMEM] * (8 + len(others)) + [ANY] * n,
+        [VMEM] * 2 + [ANY] * len(g),
+        (scal, dx1, x, a1, un, p, o, a2, vec, *others, *pieces),
+        [WA, WC, pltpu.VMEM((T, FF), BF), pltpu.VMEM((T, 1024), BF), pltpu.VMEM((T, D), BF), *vblk, pltpu.SemaphoreType.DMA((64,))],
         cost_estimate=cost(2 * T * D * FF * 8, 2 * WBYTES + 8e6),
         name="attn_bwd",
-    )(scal, dx1, x, a1, un, p, o, a2, vec, *others, *pieces)
+        mib=64,
+    )
     return res[:2], res[2:]
 
 
@@ -520,6 +562,9 @@
     def z(self, v, k):
         return lax.ppermute(v, "dp", [(z * self.X + x, (z + k) % self.Z * self.X + x) for z in range(self.Z) for x in range(self.X)])
 
+    def z_xor(self, v, k):
+        return lax.ppermute(v, "dp", [(i, i ^ (k * self.X)) for i in range(self.dp)])
+
     def x(self, v):
         return lax.ppermute(v, "dp", [(i, i ^ 1) for i in range(self.dp)])
 
@@ -530,65 +575,320 @@
         return lax.ppermute(v, "fsdp", [(i, i ^ 1) for i in range(self.fsdp)])
 
 
-def zcat_kernel(r1, r2, scal, p0, p1, p2, p3, o1, o2, sems):
-    copies = []
+def pack_a_kernel(l, wqkv, wo, out):
+    out[...] = jnp.concatenate([wqkv[l], wo[l]], axis=1)
+
+
+def pack_a(seq, l, wqkv, wo):
+    return seq(
+        functools.partial(pack_a_kernel, l),
+        [S((96, D), BF)],
+        [VMEM] * 2,
+        [VMEM],
+        (wqkv, wo),
+        cost_estimate=cost(0, 4 * 96 * D),
+        name="pack_a",
+    )[0]
+
+
+def pack_bc_rows(l, w1, w2, out, first, second):
+    t = w2[l].T
+    for i, at in enumerate((first, second)):
+        out[at : at + 48] = w1[l, 48 * i : 48 * i + 48]
+        for j in range(2):
+            out[at + 48 : at + 96, 384 * j : 384 * j + 384] = t[96 * j + 48 * i : 96 * j + 48 * i + 48]
+
+
+def pack_vec_kernel(w1, w2, ng, bi, hg, hb, out):
+    def column(v, u, w, first):
+        v = jnp.concatenate([v.astype(F32), u.astype(F32)], axis=0)
+        parts = [jnp.zeros((first, w), F32)] if first else []
+        return jnp.concatenate(parts + [v, jnp.zeros((VROWS - first - v.shape[0], w), F32)], axis=0)
+
+    pack_bc_rows(0, w1, w2, out, 0, 112)
+    low = [column(ng[i], bi[i], 96, 0) for i in range(LAYERS)]
+    hid = [column(hg[i], hb[i], 384, HROW) for i in range(LAYERS)]
+    low = jnp.concatenate(low + [jnp.zeros((VROWS, 576), F32)], axis=1)
+    out[96:112] = (low + jnp.concatenate(hid, axis=1)).astype(BF)
+    out[208:224] = jnp.zeros((VROWS, D), BF)
+
+
+def pack_vec(seq, w1, w2, vectors):
+    return seq(
+        pack_vec_kernel,
+        [S((224, D), BF)],
+        [VMEM] * 6,
+        [VMEM],
+        (w1, w2, *vectors),
+        cost_estimate=cost(0, 4 * 224 * D),
+        name="pack_vec",
+    )[0]
+
+
+def pack_all_kernel(l, wqkv, wo, w1, w2, out):
+    a = jnp.concatenate([wqkv[l], wo[l]], axis=1)
+    out[0:48] = a[0:48]
+    out[144:192] = a[48:96]
+    pack_bc_rows(l, w1, w2, out, 48, 192)
+
+
+def pack_all(seq, l, weights):
+    return seq(
+        functools.partial(pack_all_kernel, l),
+        [S((288, D), BF)],
+        [VMEM] * 4,
+        [VMEM],
+        weights,
+        cost_estimate=cost(0, 4 * 288 * D),
+        name="pack_all",
+    )[0]
+
+
+def zcat_kernel(r1, scal, p0, p1, p2, p3, o1, o2):
     for k, ref in enumerate((p0, p1, p2, p3)):
         z = lax.rem(scal[2] + 4 - k, 4)
-        copies.append((ref.at[pl.ds(0, r1)], o1.at[z]))
-        copies.append((ref.at[pl.ds(r1, r2)], o2.at[z]))
-    wait(start(copies, sems))
-
-
-def zcat(scal, parts, r1, r2):
-    return pl.pallas_call(
-        functools.partial(zcat_kernel, r1, r2),
-        out_shape=(S((4, r1, D), BF), S((4, r2, D), BF)),
-        in_specs=[SMEM] + [ANY] * 4,
-        out_specs=[ANY] * 2,
-        scratch_shapes=[pltpu.SemaphoreType.DMA((8,))],
-        cost_estimate=cost(0, 8 * (r1 + r2) * D * 4),
+        o1[z] = ref[0:r1]
+        o2[z] = ref[r1:]
+
+
+def zcat(seq, scal, parts, r1):
+    r2 = parts[0].shape[0] - r1
+    return seq(
+        functools.partial(zcat_kernel, r1),
+        (S((4, r1, D), BF), S((4, r2, D), BF)),
+        [SMEM] + [VMEM] * 4,
+        [VMEM] * 2,
+        (scal, *parts),
+        cost_estimate=cost(0, 8 * (r1 + r2) * D * 2),
         name="zcat",
-    )(scal, *parts)
-
-
-def gather_chunk(ring, scal, pack, r1):
-    r2 = pack.shape[0] - r1
-    parts = [pack] + [ring.z(pack, k) for k in (1, 2, 3)]
-    h1, h2 = zcat(scal, parts, r1, r2)
-    x1 = ring.x(h1)
-    y2 = ring.y(h2)
-    h1 = jnp.stack([h1, x1])
-    h2 = jnp.stack([h2, y2])
-    y1 = ring.y(h1)
-    x2 = ring.x(h2)
-    return [h1, y1, ring.c(h1), ring.c(y1), h2, x2, ring.c(h2), ring.c(x2)]
-
-
-def add(a, b):
-    return (a.astype(F32) + b.astype(F32)).astype(BF)
-
-
-def scatter_chunk(ring, zme, grads):
-    k0, k1, s0, s1 = grads
-    r0, r1 = ring.c(s0), ring.c(s1)
-    x0 = ring.x(add(k0[1], r0[1]))
-    y1 = ring.y(add(k1[1], r1[1]))
-    a0 = add(k0[0], r0[0])
-    a1 = add(k1[0], r1[0])
-    y0 = ring.y(add(a0[1], x0[1]))
-    x1 = ring.x(add(a1[1], y1[1]))
-    b0 = add(a0[0], x0[0])
-    b1 = add(a1[0], y1[0])
-
-    def at(k):
-        z = lax.rem(zme + k, 4)
-        pick = lambda v: lax.dynamic_index_in_dim(v, z, 0, keepdims=False)
-        return jnp.concatenate([add(pick(b0), pick(y0)), add(pick(b1), pick(x1))], axis=0)
-
-    total = at(0).astype(F32)
-    for k in (1, 2, 3):
-        total = total + ring.z(at(k), k).astype(F32)
-    return total
+    )
+
+
+def pile_kernel(first, rows, h1, x1, h2, y2, o1, o2):
+    mine = pl.ds(first, rows)
+    o1[0] = h1[:, mine]
+    o1[1] = x1[:, mine]
+    o2[0] = h2[:, mine]
+    o2[1] = y2[:, mine]
+
+
+def pile(seq, first, rows, parts):
+    return seq(
+        functools.partial(pile_kernel, first, rows),
+        [S((2, 4, rows, D), BF)] * 2,
+        [VMEM] * 4,
+        [VMEM] * 2,
+        parts,
+        cost_estimate=cost(0, 64 * rows * D),
+        name="pile",
+    )
+
+
+def merge_kernel(*refs):
+    for i, ref in enumerate(refs[:-1]):
+        refs[-1][i] = ref[...]
+
+
+def merge(seq, *parts):
+    shape = (len(parts), *parts[0].shape)
+    return seq(merge_kernel, [S(shape, BF)], [VMEM] * len(parts), [VMEM], parts, cost_estimate=cost(0, 4 * math.prod(shape)), name="merge")[0]
+
+
+def total(refs):
+    out = refs[0].astype(F32)
+    for r in refs[1:]:
+        out = out + r.astype(F32)
+    return out
+
+
+class Sums:
+    def __init__(self, scal):
+        self.scal = scal
+        self.arrays = []
+        self.outs = []
+        self.sums = []
+
+    def source(self, array):
+        for i, v in enumerate(self.arrays):
+            if v is array:
+                return i
+        self.arrays.append(array)
+        return len(self.arrays) - 1
+
+    def out(self, *shape):
+        self.outs.append(shape)
+        return len(self.outs) - 1
+
+    def add(self, out, where, sources, rows):
+        self.sums.append((out, where, [(self.source(v), at, deep) for v, at, deep in sources], rows))
+
+    def run(self, seq, name):
+        n, q = len(self.arrays), len(self.outs)
+        copies = sum(len(v[2]) for v in self.sums)
+        sums = self.sums
+
+        def kernel(scal, *refs):
+            arrays, outs = refs[:n], refs[n : n + q]
+            ins, made, sems = refs[n + q : n + q + copies], refs[n + q + copies : -1], refs[-1]
+            pairs = [(arrays[i].at[at(scal)], ins[j]) for j, (i, at, _) in enumerate(v for t in sums for v in t[2])]
+            loads = start(pairs, sems)
+            saves, first = [], 0
+            for t, (out, where, sources, rows) in enumerate(sums):
+                mine = range(first, first + len(sources))
+                first += len(sources)
+                wait([loads[j] for j in mine])
+                made[t][...] = total([ins[j][...].reshape(rows, D) for j in mine]).astype(BF)
+                saves += start([(made[t], outs[out].at[where(scal)])], sems, copies + t)
+            wait(saves)
+
+        scratch = [pltpu.VMEM((4, t[3] // 4, D) if deep else (t[3], D), BF) for t in sums for _, _, deep in t[2]]
+        scratch += [pltpu.VMEM((t[3], D), BF) for t in sums]
+        return seq(
+            kernel,
+            [S((*v, D), BF) for v in self.outs],
+            [SMEM] + [ANY] * n,
+            [ANY] * q,
+            (self.scal, *self.arrays),
+            scratch + [pltpu.SemaphoreType.DMA((copies + len(sums),))],
+            cost_estimate=cost(0, 2 * D * sum(t[3] * (1 + len(t[2])) for t in sums)),
+            name=name,
+            mib=64,
+        )
+
+
+def finish_kernel(scal, *refs):
+    keep_bc, got_bc, keep_a, got_a, last = refs[:5]
+    in_out, out_out, up_out, down_out, vec_out = refs[13:]
+    i = lax.rem(scal[2], 2)
+    upper = total([keep_bc[i], got_bc[i], last[0:192]])
+    a1 = total([keep_a[i], got_a[i], last[192:]])
+    lower = total([r[...] for r in refs[5:9]])
+    rows_a = total([r[...] for r in refs[9:13]])
+    vec_out[0:VROWS] = rows_a[48:64]
+    vec_out[VROWS:] = rows_a[112:128]
+    a0 = jnp.concatenate([rows_a[:48], rows_a[64:112]], axis=0)
+    for l, a, bc in ((0, a0, lower), (1, a1, upper)):
+        in_out[l] = a[:, :576]
+        out_out[l] = a[:, 576:]
+        up_out[l, 0:48] = bc[0:48]
+        up_out[l, 48:96] = bc[96:144]
+        c = jnp.concatenate([bc[48:96], bc[144:192]], axis=0)
+        for j in range(2):
+            down_out[l, :, 96 * j : 96 * j + 96] = c[:, 384 * j : 384 * j + 384].T
+
+
+def finish(seq, scal, parts):
+    return seq(
+        finish_kernel,
+        [S((2, 96, 576), F32), S((2, 96, 192), F32), S((2, 96, D), F32), S((2, 384, 192), F32), S((2 * VROWS, D), F32)],
+        [SMEM] + [VMEM] * len(parts),
+        [VMEM] * 5,
+        (scal, *parts),
+        cost_estimate=cost(0, 8e6),
+        name="finish",
+    )
+
+
+class Gather:
+    def __init__(self, seq, ring, scal):
+        self.seq, self.ring, self.scal = seq, ring, scal
+
+    def z_all(self, pack):
+        self.parts = [pack] + [self.ring.z(pack, k) for k in (1, 2, 3)]
+
+    def xy_first(self):
+        h1, h2 = zcat(self.seq, self.scal, self.parts, self.parts[0].shape[0] // 2)
+        self.both = h1, self.ring.x(h1), h2, self.ring.y(h2)
+
+    def xy_second(self, both, first, rows):
+        self.h1, self.h2 = pile(self.seq, first, rows, both)
+        self.y1, self.x2 = self.ring.y(self.h1), self.ring.x(self.h2)
+
+    def core(self):
+        both = self.ring.c(merge(self.seq, self.h1, self.y1, self.h2, self.x2))
+        self.other = [(both, i) for i in range(4)]
+        return both
+
+    def core_own(self):
+        self.own = self.ring.c(self.h1), self.ring.c(self.h2)
+        return self.own
+
+    def core_got(self):
+        both = self.ring.c(merge(self.seq, self.y1, self.x2))
+        self.other = [self.own[0], (both, 0), self.own[1], (both, 1)]
+        return both
+
+    def pieces(self):
+        return [self.h1, self.y1, *self.other[:2], self.h2, self.x2, *self.other[2:]]
+
+
+def rows_at(first, rows):
+    return lambda scal: (pl.ds(first, rows),)
+
+
+class Scatter:
+    def __init__(self, ring, grads):
+        self.ring = ring
+        self.keep, self.send = grads
+        self.rows = self.keep.shape[4]
+
+    def core(self, send):
+        self.got = self.ring.c(send)
+        return self.got
+
+    def both(self, *index):
+        return [(v, lambda scal: index, True) for v in (self.keep, self.got)]
+
+    def first(self, sums, x, y, at=0):
+        self.at1 = at
+        r = 4 * self.rows
+        for h, out in ((0, x), (1, y)):
+            for s in range(2):
+                sums.add(out, rows_at(at + s * r, r), self.both(h, 1, s), r)
+
+    def second(self, sums, x, y, at=0):
+        self.at2 = at
+        r = 4 * self.rows
+        for h, got, out in ((0, self.x1st, y), (1, self.y1st, x)):
+            sums.add(out, rows_at(at, r), self.both(h, 0, 1) + [(got, rows_at(self.at1 + r, r), False)], r)
+
+    def block(self, sums, out, where, z):
+        n = self.rows
+        for h, a, b in ((0, self.x1st, self.y2nd), (1, self.y1st, self.x2nd)):
+
+            def local(scal, h=h):
+                return (h, 0, 0, z(scal))
+
+            def sent(first):
+                return lambda scal: (pl.ds(pl.multiple_of(first + z(scal) * n, 16), n),)
+
+            sources = [(v, local, False) for v in (self.keep, self.got)]
+            sources += [(a, sent(self.at1), False), (b, sent(self.at2), False)]
+            sums.add(out, where(h * n, n), sources, n)
+
+    def third_pair(self, sums):
+        outs = [sums.out(2, 2 * self.rows) for _ in range(2)]
+        for k in (1, 0):
+            for i in range(2):
+
+                def z(scal, k=k, i=i):
+                    high = scal[2] // 2
+                    return 2 * (1 - high if k else high) + i
+
+                self.block(sums, outs[k], lambda first, n, i=i: lambda scal: (i, pl.ds(first, n)), z)
+        return outs
+
+    def third_direct(self, sums):
+        outs = [sums.out(2 * self.rows) for _ in range(4)]
+        for k in (1, 2, 3, 0):
+            self.block(sums, outs[k], rows_at, lambda scal, k=k: lax.rem(scal[2] + k, 4))
+        return outs
+
+
+def fourth(sums, out, at, keep, got):
+    rows = keep.shape[1]
+    where = lambda scal: (1 - lax.rem(scal[2], 2),)
+    sums.add(out, rows_at(at, rows), [(keep, where, False), (got, where, False)], rows)
 
 
 def unpack_vec(rows):
@@ -609,99 +909,135 @@
     ).reshape(1, 2560)
 
 
-def run_layers(plan, scal, inputs, cotangent, vecs, hids, pieces, after):
-    pb = [proj_bias(v) for v in vecs]
-    x = inputs
-    kept = []
-    for l in range(LAYERS):
-        pa, ma, pbc, mb, mc = pieces[l]
-        x1, a1, un, p, o, a2 = call_attn_fwd(plan, scal, x, vecs[l], pb[l], pa, ma)
-        x2, a3, sl, n4, a4 = call_ff_fwd(plan, scal, x1, vecs[l], hids[l], pbc, mb, mc, l == LAYERS - 1)
-        kept.append((x, x1, a1, un, p, o, a2, a3, sl, n4, a4))
-        x = x2
-    outputs = x
-    dy = cotangent
-    vec_grads = {}
-    for l in reversed(range(LAYERS)):
-        pa, ma, pbc, mb, mc = pieces[l]
-        x, x1, a1, un, p, o, a2, a3, sl, n4, a4 = kept[l]
-        (dx1, gva, gh), gbc = call_ff_bwd(plan, scal, dy, x1, a3, sl, n4, a4, vecs[l], hids[l], pbc, mb, mc, l == LAYERS - 1)
-        after(l, "bc", gbc)
-        others = (gva, *vec_grads[1][:2], gh, vec_grads[1][2]) if plan.fast and l == 0 else ()
-        (dy, gvb), ga = call_attn_bwd(plan, scal, dx1, x, a1, un, p, o, a2, vecs[l], pa, ma, others)
-        after(l, "a", ga)
-        vec_grads[l] = (gva, gvb, gh)
-    return outputs, dy, vec_grads
-
-
 def fast_shards(ring, inputs, lengths, in_projection, out_projection, up_weight, down_weight, norm_gains, biases, hidden_gains, hidden_biases, cotangent):
     plan = Plan(True)
+    seq = Seq(True)
     dpi, fi = lax.axis_index("dp"), lax.axis_index("fsdp")
-    zme = dpi // ring.X
-    place = jnp.stack([zme, dpi % ring.X, fi // 2, fi % 2]).astype(jnp.int32)
+    xme = dpi % ring.X
+    place = jnp.stack([dpi // ring.X, xme, fi // 2, fi % 2]).astype(jnp.int32)
     scal = jnp.concatenate([lengths[0], place, jnp.zeros((2,), jnp.int32)])
 
-    own_vec = jnp.concatenate([norm_gains, biases], axis=1)
-    own_hid = jnp.concatenate([hidden_gains, hidden_biases], axis=1)
-    vec_rows = jnp.concatenate(
-        [
-            jnp.pad(jnp.concatenate([own_vec[0], own_vec[1]], axis=1), ((0, 0), (0, 576))),
-            jnp.concatenate([own_hid[0], own_hid[1]], axis=1),
-            jnp.zeros((3, D), BF),
-        ],
-        axis=0,
-    )
-    pack_a = [jnp.concatenate([in_projection[l], out_projection[l]], axis=1) for l in range(LAYERS)]
-    pack_c = []
-    for l in range(LAYERS):
-        t = down_weight[l].T
-        pack_c.append(jnp.concatenate([t[:96], t[96:]], axis=1))
-    pack_bc = []
-    for l in range(LAYERS):
-        b, c = up_weight[l], pack_c[l]
-        pack_bc.append(jnp.concatenate([b[:48], c[:48], b[48:], c[48:]], axis=0))
-    first = jnp.concatenate([pack_a[0][:48], vec_rows, pack_a[0][48:]], axis=0)
-    pieces = []
-    for l in range(LAYERS):
-        got_a = gather_chunk(ring, scal, first if l == 0 else pack_a[l], 64 if l == 0 else 48)
-        got_bc = gather_chunk(ring, scal, pack_bc[l], 96)
-        pieces.append((got_a, 0, got_bc, 0, 1))
-        if l == 0:
-            rows = got_a[0][:, :, 48:64]
-            xme = dpi % ring.X
-            rows = jnp.where(xme == 0, rows, rows[::-1]).transpose(1, 0, 2, 3).reshape(8, VROWS, D)
-            vecs, hids = unpack_vec(rows)
-    sums = {}
-
-    def after(l, name, grads):
-        sums[l, name] = scatter_chunk(ring, zme, grads)
-
-    outputs, input_gradient, _ = run_layers(plan, scal, inputs, cotangent, vecs, hids, pieces, after)
-    a = [sums[0, "a"], sums[1, "a"]]
-    vrows = a[0][48:64]
-    a[0] = jnp.concatenate([a[0][:48], a[0][64:]], axis=0)
-    bc = [sums[l, "bc"] for l in range(LAYERS)]
-    b = [jnp.concatenate([v[:48], v[96:144]], axis=0) for v in bc]
-    c = [jnp.concatenate([v[48:96], v[144:]], axis=0) for v in bc]
-    c = [jnp.concatenate([v[:, :384], v[:, 384:]], axis=0).T for v in c]
+    a, b, c, d, e = (Gather(seq, ring, scal) for _ in range(5))
+    a.z_all(pack_a(seq, 0, in_projection, out_projection))
+    cd = pack_all(seq, 1, (in_projection, out_projection, up_weight, down_weight))
+    a.xy_first()
+    b.z_all(pack_vec(seq, up_weight, down_weight, (norm_gains, biases, hidden_gains, hidden_biases)))
+    seq.hold(b.parts[1])
+    a.xy_second(a.both, 0, 48)
+    seq.hold(a.y1, a.x2)
+    b.xy_first()
+    c.z_all(cd)
+    seq.hold(a.core(), c.parts[3])
+    b.xy_second(b.both, 0, 112)
+    rows = b.h1[:, :, 96:112]
+    rows = jnp.where(xme == 0, rows, rows[::-1]).transpose(1, 0, 2, 3).reshape(8, VROWS, D)
+    vecs, hids = unpack_vec(rows)
+    pb = [proj_bias(v) for v in vecs]
+    kept = [None, None]
+    x = inputs
+    x1, a1, un, p, o, a2 = call_attn_fwd(seq, plan, scal, x, vecs[0], pb[0], a.pieces(), 0)
+    seq.hold(b.y1, b.x2, *b.core_own())
+    c.xy_first()
+    c.xy_second(c.both, 0, 48)
+    d.xy_second(c.both, 48, 48)
+    e.xy_second(c.both, 96, 48)
+    b.core_got()
+    x2, a3, sl, n4, a4 = call_ff_fwd(seq, plan, scal, x1, vecs[0], hids[0], b.pieces(), 0, 1, False)
+    kept[0] = (x, x1, a1, un, p, o, a2, a3, sl, n4, a4)
+    x = x2
+    seq.hold(d.y1, d.x2)
+    c.core()
+    d.core()
+    x1, a1, un, p, o, a2 = call_attn_fwd(seq, plan, scal, x, vecs[1], pb[1], c.pieces(), 0)
+    e.core_own()
+    e.core_got()
+    outputs, a3, sl, n4, a4 = call_ff_fwd(seq, plan, scal, x1, vecs[1], hids[1], d.pieces() + e.pieces(), 0, 0, True)
+
+    (dx1, gva1, gh1), grads = call_ff_bwd(seq, plan, scal, cotangent, x1, a3, sl, n4, a4, vecs[1], hids[1], d.pieces() + e.pieces(), 0, 0, True)
+    s1 = Scatter(ring, grads)
+    s1.core(s1.send)
+    (dy, gvb1), grads = call_attn_bwd(seq, plan, scal, dx1, x, a1, un, p, o, a2, vecs[1], c.pieces(), 0, ())
+    s2 = Scatter(ring, grads)
+
+    sums = Sums(scal)
+    outs = sums.out(768), sums.out(768)
+    s1.first(sums, *outs)
+    seq.carry(s2.send)
+    u, v = sums.run(seq, "sums_1")
+    s2.core(*seq.carried)
+    s1.x1st, s1.y1st = ring.x(u), ring.y(v)
+
+    x, x1, a1, un, p, o, a2, a3, sl, n4, a4 = kept[0]
+    (dx1, gva0, gh0), grads = call_ff_bwd(seq, plan, scal, dy, x1, a3, sl, n4, a4, vecs[0], hids[0], b.pieces(), 0, 1, False)
+    s3 = Scatter(ring, grads)
+
+    sums = Sums(scal)
+    outs = sums.out(768), sums.out(768)
+    s2.first(sums, *outs)
+    s1.second(sums, *outs, 384)
+    seq.carry(s3.send)
+    u, v = sums.run(seq, "sums_2")
+    s3.core(*seq.carried)
+    s2.x1st, s2.y1st = s1.x2nd, s1.y2nd = ring.x(u), ring.y(v)
+
+    others = (gva0, gva1, gvb1, gh0, gh1)
+    (input_gradient, _), grads = call_attn_bwd(seq, plan, scal, dx1, x, a1, un, p, o, a2, vecs[0], a.pieces(), 0, others)
+    s4 = Scatter(ring, grads)
+
+    sums = Sums(scal)
+    outs = sums.out(960), sums.out(960)
+    s2.second(sums, *outs)
+    s3.first(sums, *outs, 192)
+    s1.third_pair(sums)
+    seq.carry(s4.send)
+    u, v, keep1, send1 = sums.run(seq, "sums_3")
+    s4.core(*seq.carried)
+    s3.x1st, s3.y1st = s2.x2nd, s2.y2nd = ring.x(u), ring.y(v)
+    got1 = ring.z_xor(send1, 2)
+
+    sums = Sums(scal)
+    outs = sums.out(384), sums.out(384)
+    s3.second(sums, *outs)
+    s2.third_pair(sums)
+    seq.hold(got1)
+    u, v, keep2, send2 = sums.run(seq, "sums_4")
+    s3.x2nd, s3.y2nd = ring.x(u), ring.y(v)
+    got2 = ring.z_xor(send2, 2)
+
+    sums = Sums(scal)
+    s3.third_direct(sums)
+    outs = sums.out(512), sums.out(512)
+    s4.first(sums, *outs)
+    seq.hold(got2)
+    *parts3, u, v = sums.run(seq, "sums_5")
+    parts3 = parts3[:1] + [ring.z(parts3[k], k) for k in (1, 2, 3)]
+    s4.x1st, s4.y1st = ring.x(u), ring.y(v)
+
+    sums = Sums(scal)
+    outs = sums.out(256), sums.out(256)
+    s4.second(sums, *outs)
+    seq.hold(*parts3[1:3])
+    u, v = sums.run(seq, "sums_6")
+    s4.x2nd, s4.y2nd = ring.x(u), ring.y(v)
+
+    sums = Sums(scal)
+    s4.third_direct(sums)
+    out = sums.out(288)
+    fourth(sums, out, 0, keep1, got1)
+    fourth(sums, out, 192, keep2, got2)
+    seq.hold(parts3[3])
+    res = sums.run(seq, "sums_7")
+    parts4 = [res[0]] + [ring.z(res[k], k) for k in (1, 2, 3)]
+    last = ring.z_xor(res[4], 1)
+    g_in, g_out, g_up, g_down, vrows = finish(seq, scal, [keep1, got1, keep2, got2, last, *parts3, *parts4])
     gv = jnp.stack([vrows[:10, :96], vrows[:10, 96:192]])
-    gh = jnp.stack([vrows[10:13, :384], vrows[10:13, 384:]])
-    return (
-        outputs,
-        input_gradient,
-        jnp.stack([v[:, :576] for v in a]),
-        jnp.stack([v[:, 576:] for v in a]),
-        jnp.stack(b),
-        jnp.stack(c),
-        gv[:, :3],
-        gv[:, 3:],
-        gh[:, :1],
-        gh[:, 1:],
-    )
+    gh = jnp.stack([vrows[26:29, :384], vrows[26:29, 384:]])
+    return outputs, input_gradient, g_in, g_out, g_up, g_down, gv[:, :3], gv[:, 3:], gh[:, :1], gh[:, 1:]
 
 
 def whole_shards(inputs, lengths, in_projection, out_projection, up_weight, down_weight, norm_gains, biases, hidden_gains, hidden_biases, cotangent):
     plan = Plan(False)
+    seq = Seq(False)
     scal = jnp.concatenate([lengths[0], jnp.zeros((6,), jnp.int32)])
 
     def full(w):
@@ -719,16 +1055,27 @@
         c = full(down_weight[l]).reshape(4, D, D).transpose(0, 2, 1)
         shape = (4, 2, 2, 48, FF)
         got = [a.reshape(shape), b.reshape(shape), c.reshape(4, 4, 2, 2, 48, D)]
-        pieces.append((got, 0, got, 0, 0))
+        pieces.append(got)
         vecs.append(rows(jnp.concatenate([norm_gains[l], biases[l]], axis=0), D))
         hid = rows(jnp.concatenate([hidden_gains[l], hidden_biases[l]], axis=0), FF)
         hids.append(jnp.roll(hid, HROW, axis=0))
-    grads = {}
-
-    def after(l, name, got):
-        grads[l, name] = got
-
-    outputs, input_gradient, vec_grads = run_layers(plan, scal, inputs, cotangent, vecs, hids, pieces, after)
+    pb = [proj_bias(v) for v in vecs]
+    x = inputs
+    kept = []
+    for l in range(LAYERS):
+        x1, a1, un, p, o, a2 = call_attn_fwd(seq, plan, scal, x, vecs[l], pb[l], pieces[l], 0)
+        x2, a3, sl, n4, a4 = call_ff_fwd(seq, plan, scal, x1, vecs[l], hids[l], pieces[l], 0, 0, l == LAYERS - 1)
+        kept.append((x, x1, a1, un, p, o, a2, a3, sl, n4, a4))
+        x = x2
+    outputs = x
+    dy = cotangent
+    layer_grads = [None] * LAYERS
+    for l in reversed(range(LAYERS)):
+        x, x1, a1, un, p, o, a2, a3, sl, n4, a4 = kept[l]
+        last = l == LAYERS - 1
+        (dx1, gva, gh), (gb, gc) = call_ff_bwd(seq, plan, scal, dy, x1, a3, sl, n4, a4, vecs[l], hids[l], pieces[l], 0, 0, last)
+        (dy, gvb), (ga,) = call_attn_bwd(seq, plan, scal, dx1, x, a1, un, p, o, a2, vecs[l], pieces[l], 0, ())
+        layer_grads[l] = (ga, gb, gc, gva + gvb, gh)
 
     def scatter(g):
         g = lax.psum_scatter(g.astype(BF), "dp", scatter_dimension=0, tiled=True)
@@ -740,11 +1087,9 @@
 
     res = []
     for l in range(LAYERS):
-        gb, gc = grads[l, "bc"]
-        (ga,) = grads[l, "a"]
+        ga, gb, gc, gv, gh = layer_grads[l]
         ga = ga.reshape(4, D, D).transpose(1, 0, 2)
-        gva, gvb, gh = vec_grads[l]
-        gv = scatter_rows((gva + gvb)[:10])
+        gv = scatter_rows(gv[:10])
         gh = scatter_rows(gh[HROW : HROW + 3])
         res.append(
             (
@@ -758,7 +1103,7 @@
                 gh[1:],
             )
         )
-    return (outputs, input_gradient, *(jnp.stack([r[i] for r in res]) for i in range(8)))
+    return (outputs, dy, *(jnp.stack([r[i] for r in res]) for i in range(8)))
 
 
 def solution(mesh):

time: 625 us -> 490 us (0.78)
  starting transfers between devices: 123 us -> 48.4 us
  Pallas kernels: 223 us -> 175 us
  waiting for transfers between devices: 175 us -> 219 us
  other arithmetic: 33.8 us -> 1.84 us
  local copies, waits for them, and re-layouts: 60.7 us -> 34.9 us
    ppermute x16 -> x14, waiting for transfers between devices: 87.6 us -> 23.3 us  [y(): return lax.ppermute(v, 'fsdp', [(i, i ^ 2) for i in range(self.fsdp)])]
    ppermute x24 -> x15, starting transfers between devices: 82.4 us -> 19.2 us  [z(): lax.ppermute(v, 'dp', [(z * self.X + x, (z + k) % self.Z * self.X + x) fo...]
    pallas_call x12 -> x32, Pallas kernels: 223 us -> 175 us  [__call__(): pl.pallas_call(body, out_shape=tuple(out_shape) + tuple((S(v.shape, v.dty...]
    ppermute x24 -> x15, waiting for transfers between devices: 43.3 us -> 90.3 us  [z(): lax.ppermute(v, 'dp', [(z * self.X + x, (z + k) % self.Z * self.X + x) fo...]
    ppermute x0 -> x3, waiting for transfers between devices: none -> 44.2 us  [z_xor(): return lax.ppermute(v, 'dp', [(i, i ^ k * self.X) for i in range(self.dp)])]
    convert_element_type x24 -> x0, other arithmetic: 16.6 us -> none  [add(): return (a.astype(F32) + b.astype(F32)).astype(BF)]
    unnamed x230 -> x86, local copies, waits for them, and re-layouts: 43.2 us -> 29.2 us
    another operation x20 -> x1, other arithmetic: 13.6 us -> 0.6 us  [fast_shards(): gh = jnp.stack([vrows[26:29, :384], vrows[26:29, 384:]])]
  transfers between devices with their start and end apart: 80 -> 59, of which waited for: 26 -> 37; matrix products, arithmetic and copies ran while one was open for 9% -> 2% of each run, Pallas kernels for 29% -> 20%
where the time goes in v2:
time: 490 us; the launch traced here: 481 us
  waiting for transfers between devices  219 us (45%)
  Pallas kernels  175 us (36%)
  starting transfers between devices  48.4 us (10%)
  local copies, waits for them, and re-layouts  34.9 us (7%)
    pallas_call x32, Pallas kernels, __call__(): pl.pallas_call(body, out_shape=tuple(out_shape) + tuple((S(v.shape, v.dty...  175 us
    ppermute x15, waiting for transfers between devices, z(): lax.ppermute(v, 'dp', [(z * self.X + x, (z + k) % self.Z * self.X + x) fo...  90.3 us
    ppermute x14, waiting for transfers between devices, x(): return lax.ppermute(v, 'dp', [(i, i ^ 1) for i in range(self.dp)])  48.2 us
    ppermute x3, waiting for transfers between devices, z_xor(): return lax.ppermute(v, 'dp', [(i, i ^ k * self.X) for i in range(self.dp)])  44.2 us
    unnamed x86, local copies, waits for them, and re-layouts  29.2 us
    ppermute x14, waiting for transfers between devices, y(): return lax.ppermute(v, 'fsdp', [(i, i ^ 2) for i in range(self.fsdp)])  23.3 us
    ppermute x15, starting transfers between devices, z(): lax.ppermute(v, 'dp', [(z * self.X + x, (z + k) % self.Z * self.X + x) fo...  19.2 us
    ppermute x14, starting transfers between devices, y(): return lax.ppermute(v, 'fsdp', [(i, i ^ 2) for i in range(self.fsdp)])  14.4 us
  transfers between devices with their start and end apart: 59, of which 37 were waited for; matrix products, arithmetic and copies ran while one was open for 2% of the time, Pallas kernels for 20%

profile of v2, /device:TPU:0, one launch (start us, length us, event | category | flops | bytes accessed | tf_op | source)
XLA Modules:
  0.0 480.9 jit_solution(9837595216969409277)
XLA Ops:
  2.6 5.1 %collective-permute-start.2 = (bf16[96,768]{1,0:T(8,128)(2,1)S(1)}, bf16[96,768]{1,0:T(8,128)(2,1)S(1)}, u32[]{:S(2)}, u32[]{:S(2)}) collective-permute-start(bf16[96,768]{1,0:T(8,128)(2,1)S(1)} %pack_a.1.refs_4_.refs_1_), channel_id=1, source_target_pairs={{0,24},{4,28},{8,0},{12,4},{16,8},{20,12},{24,16},{28,20},{1,25},{... | collective-permute-start | bytes 442376 | tf_op jit(solution)/shard_map/ppermute | solution.py:563
  15.7 4.5 collective-permute-done.1.refs_3_
  24.9 4.9 %collective-permute-done.7.refs_3_ = bf16[4,48,768]{2,1,0:T(8,128)(2,1)S(1)} collective-permute-done((bf16[4,48,768]{2,1,0:T(8,128)(2,1)S(1)}, bf16[4,48,768]{2,1,0:T(8,128)(2,1)S(1)}, u32[]{:S(2)}, u32[]{:S(2)}) %collective-permute-start.7) | collective-permute-done | bytes 294944 | tf_op jit(solution)/shard_map/ppermute | solution.py:572
  37.1 8.2 %collective-permute-done.5.refs_4_ = bf16[224,768]{1,0:T(8,128)(2,1)S(1)} collective-permute-done((bf16[224,768]{1,0:T(8,128)(2,1)S(1)}, bf16[224,768]{1,0:T(8,128)(2,1)S(1)}, u32[]{:S(2)}, u32[]{:S(2)}) %collective-permute-start.5) | collective-permute-done | bytes 344096 | tf_op jit(solution)/shard_map/ppermute | solution.py:563
  45.3 11.7 %collective-permute-done.4.refs_3_ = bf16[224,768]{1,0:T(8,128)(2,1)S(1)} collective-permute-done((bf16[224,768]{1,0:T(8,128)(2,1)S(1)}, bf16[224,768]{1,0:T(8,128)(2,1)S(1)}, u32[]{:S(2)}, u32[]{:S(2)}) %collective-permute-start.4) | collective-permute-done | bytes 344096 | tf_op jit(solution)/shard_map/ppermute | solution.py:563
  63.6 11.0 %collective-permute-done.13.refs_6_.refs_4_ = bf16[288,768]{1,0:T(8,128)(2,1)S(1)} collective-permute-done((bf16[288,768]{1,0:T(8,128)(2,1)}, bf16[288,768]{1,0:T(8,128)(2,1)S(1)}, u32[]{:S(2)}, u32[]{:S(2)}) %collective-permute-start.13) | collective-permute-done | bytes 442400 | tf_op jit(solution)/shard_map/ppermute | solution.py:563
  86.8 4.7 collective-permute-done.18.refs_3_
  93.0 10.1 %attn_fwd.2 = (f32[256,768]{1,0:T(8,128)}, bf16[256,768]{1,0:T(8,128)(2,1)}, bf16[36,256,64]{2,1,0:T(8,128)(2,1)}, f32[12,256,256]{2,1,0:T(8,128)}, f32[256,768]{1,0:T(8,128)}, /*index=5*/bf16[256,768]{1,0:T(8,128)(2,1)}) custom-call(s32[8]{0:T(128)} %copy-done.22, f32[256,768]{1,0:T(8,128)} %refs_2_.4, f32[16,768]{1,0:T(8,128)} %reshape.67.refs_2_.refs_7_.refs_8_, ...), custom_call_target="tpu_custom_call" | custom-call | flops 7247757312 | bytes 12718592 | tf_op jit(solution)/shard_map/attn_fwd/pallas_call | solution.py:455
  105.5 8.5 %collective-permute-done.16.refs_7_.refs_1_.refs_9_.refs_14_ = bf16[2,4,112,768]{3,2,1,0:T(8,128)(2,1)} collective-permute-done((bf16[2,4,112,768]{3,2,1,0:T(8,128)(2,1)}, bf16[2,4,112,768]{3,2,1,0:T(8,128)(2,1)}, u32[]{:S(2)}, u32[]{:S(2)}) %collective-permute-start.16) | collective-permute-done | bytes 1376288 | tf_op jit(solution)/shard_map/ppermute | solution.py:569
  121.9 19.0 %collective-permute-done.20.refs_1_ = bf16[4,144,768]{2,1,0:T(8,128)(2,1)S(1)} collective-permute-done((bf16[4,144,768]{2,1,0:T(8,128)(2,1)S(1)}, bf16[4,144,768]{2,1,0:T(8,128)(2,1)S(1)}, u32[]{:S(2)}, u32[]{:S(2)}) %collective-permute-start.20) | collective-permute-done | bytes 884768 | tf_op jit(solution)/shard_map/ppermute | solution.py:569
  156.0 13.3 %ff_fwd.2 = (f32[256,768]{1,0:T(8,128)}, bf16[256,768]{1,0:T(8,128)(2,1)}, f32[256,3072]{1,0:T(8,128)}, f32[256,3072]{1,0:T(8,128)}, bf16[256,3072]{1,0:T(8,128)(2,1)}) custom-call(s32[8]{0:T(128)} %copy-done.22, f32[256,768]{1,0:T(8,128)} %get-tuple-element.109.refs_5_.refs_1_.refs_2_, f32[16,768]{1,0:T(8,128)} %reshape.67.refs_2_.refs_7_.refs_8_, ...), custom_call_target="tpu_custom_call" | custom-call | flops 7247757312 | bytes 17437184 | tf_op jit(solution)/shard_map/ff_fwd/pallas_call | solution.py:455
  169.3 11.2 %collective-permute-done.26.refs_6_.refs_3_.refs_8_.refs_13_ = bf16[2,4,48,768]{3,2,1,0:T(8,128)(2,1)} collective-permute-done((bf16[2,4,48,768]{3,2,1,0:T(8,128)(2,1)}, bf16[2,4,48,768]{3,2,1,0:T(8,128)(2,1)}, u32[]{:S(2)}, u32[]{:S(2)}) %collective-permute-start.26) | collective-permute-done | bytes 589856 | tf_op jit(solution)/shard_map/ppermute | solution.py:569
  189.7 10.1 %attn_fwd.3 = (f32[256,768]{1,0:T(8,128)}, bf16[256,768]{1,0:T(8,128)(2,1)}, bf16[36,256,64]{2,1,0:T(8,128)(2,1)}, f32[12,256,256]{2,1,0:T(8,128)}, f32[256,768]{1,0:T(8,128)}, /*index=5*/bf16[256,768]{1,0:T(8,128)(2,1)}) custom-call(s32[8]{0:T(128)} %copy-done.22, f32[256,768]{1,0:T(8,128)} %get-tuple-element.116.refs_4_.refs_1_.refs_2_, ...), custom_call_target="tpu_custom_call" | custom-call | flops 7247757312 | bytes 12718592 | tf_op jit(solution)/shard_map/attn_fwd/pallas_call | solution.py:455
  199.8 4.7 collective-permute-done.31.refs_1_.refs_14_.refs_19_
  214.6 12.8 %ff_fwd.3 = (f32[256,768]{1,0:T(8,128)}, bf16[256,768]{1,0:T(8,128)(2,1)}, f32[256,3072]{1,0:T(8,128)}, f32[256,3072]{1,0:T(8,128)}, bf16[256,3072]{1,0:T(8,128)(2,1)}) custom-call(s32[8]{0:T(128)} %copy-done.22, f32[256,768]{1,0:T(8,128)} %get-tuple-element.119.refs_2_.refs_1_, f32[16,768]{1,0:T(8,128)} %reshape.73.refs_2_.refs_7_.refs_8_, ...), custom_call_target="tpu_custom_call" | custom-call | flops 7247757312 | bytes 17437184 | tf_op jit(solution)/shard_map/ff_fwd/pallas_call | solution.py:455
  227.4 18.3 %ff_bwd.2 = (f32[256,768]{1,0:T(8,128)}, f32[16,768]{1,0:T(8,128)}, f32[16,3072]{1,0:T(8,128)}, bf16[2,2,2,4,96,768]{5,4,3,2,1,0:T(8,128)(2,1)}, bf16[2,2,2,4,96,768]{5,4,3,2,1,0:T(8,128)(2,1)}) custom-call(s32[8]{0:T(128)} %copy-done.22, f32[256,768]{1,0:T(8,128)} %refs_1_.8, f32[256,768]{1,0:T(8,128)} %get-tuple-element.119.refs_2_.refs_1_, ...), custom_call_target="tpu_custom_call" | custom-call | flops 9663676416 | bytes 26874368 | tf_op jit(solution)/shard_map/ff_bwd/pallas_call | solution.py:455
  246.0 17.3 %attn_bwd.2 = (f32[256,768]{1,0:T(8,128)}, f32[16,768]{1,0:T(8,128)}, bf16[2,2,2,4,48,768]{5,4,3,2,1,0:T(8,128)(2,1)}, bf16[2,2,2,4,48,768]{5,4,3,2,1,0:T(8,128)(2,1)}) custom-call(s32[8]{0:T(128)} %copy-done.22, f32[256,768]{1,0:T(8,128)} %get-tuple-element.126.refs_1_.refs_14_, f32[256,768]{1,0:T(8,128)} %get-tuple-element.116.refs_4_.refs_1_.refs_2_, ...), custom_call_target="tpu_custom_call" | custom-call | flops 9663676416 | bytes 17437184 | tf_op jit(solution)/shard_map/attn_bwd/pallas_call | solution.py:455
  272.4 18.1 %ff_bwd.3 = (f32[256,768]{1,0:T(8,128)}, f32[16,768]{1,0:T(8,128)}, f32[16,3072]{1,0:T(8,128)}, bf16[2,2,2,4,96,768]{5,4,3,2,1,0:T(8,128)(2,1)}, bf16[2,2,2,4,96...) custom-call(s32[8]{0:T(128)} %copy-done.22, ...), custom_call_target="tpu_custom_call", output_to_operand_aliasing={{5}: (17, {})} | custom-call | flops 9663676416 | bytes 26874368 | tf_op jit(solution)/shard_map/ff_bwd/pallas_call | solution.py:455
  290.5 5.7 %collective-permute-done.37.refs_6_.refs_10_ = bf16[768,768]{1,0:T(8,128)(2,1)} collective-permute-done((bf16[768,768]{1,0:T(8,128)(2,1)}, bf16[768,768]{1,0:T(8,128)(2,1)}, u32[]{:S(2)}, u32[]{:S(2)}) %collective-permute-start.37) | collective-permute-done | bytes 1179680 | tf_op jit(solution)/shard_map/ppermute | solution.py:572
  297.3 5.0 %sums_2.1 = (bf16[768,768]{1,0:T(8,128)(2,1)}, bf16[768,768]{1,0:T(8,128)(2,1)}, bf16[2,2,2,4,96,768]{5,4,3,2,1,0:T(8,128)(2,1)}) custom-call(s32[8]{0:T(128)} %copy-done.22, bf16[2,2,2,4,48,768]{5,4,3,2,1,0:T(8,128)(2,1)} %get-tuple-element.153.refs_1_.refs_5_, ...), custom_call_target="tpu_custom_call", output_to_operand_aliasing={{2}: (8, {})} | custom-call | bytes 8257536 | tf_op jit(solution)/shard_map/sums_2/pallas_call | solution.py:455
  303.6 7.0 %collective-permute-done.40.refs_6_.refs_2_ = bf16[2,2,2,4,96,768]{5,4,3,2,1,0:T(8,128)(2,1)} collective-permute-done((bf16[2,2,2,4,96,768]{5,4,3,2,1,0:T(8,128)(2,1)}, bf16[2,2,2,4,96,768]{5,4,3,2,1,0:T(8,128)(2,1)}, u32[]{:S(2)}, u32[]{:S(2)}) %collective-permute-start.40) | collective-permute-done | bytes 4718624 | tf_op jit(solution)/shard_map/ppermute | solution.py:575
  310.7 18.7 %attn_bwd.3 = (f32[256,768]{1,0:T(8,128)}, f32[16,768]{1,0:T(8,128)}, bf16[2,2,2,4,64,768]{5,4,3,2,1,0:T(8,128)(2,1)}, bf16[2,2,2,4,64,768]{5,4,3,2,1,0:T(8,128)(2,1)}, bf16[2,2,2,4,96,768]{5,4,3,2,1,0:T(8,128)(2,1)}) custom-call(s32[8]{0:T(128)} %copy-done.22, f32[256,768]{1,0:T(8,128)} %get-tuple-element.142.refs_7_.refs_1_, ...), custom_call_target="tpu_custom_call", output_to_operand_aliasing={{4}: (20, {})} | custom-call | flops 9663676416 | bytes 17437184 | tf_op jit(solution)/shard_map/attn_bwd/pallas_call | solution.py:455
  331.4 7.4 %sums_3.1 = (bf16[960,768]{1,0:T(8,128)(2,1)}, bf16[960,768]{1,0:T(8,128)(2,1)}, bf16[2,192,768]{2,1,0:T(8,128)(2,1)}, bf16[2,192,768]{2,1,0:T(8,128)(2,1)}, bf16[2,2,2,4,64,768]{5,4,3,2,1,0:T(8,128)(2,1)}) custom-call(s32[8]{0:T(128)} %copy-done.22, ...), custom_call_target="tpu_custom_call", output_to_operand_aliasing={{4}: (12, {})} | custom-call | bytes 15335424 | tf_op jit(solution)/shard_map/sums_3/pallas_call | solution.py:455
  340.9 29.0 %collective-permute-done.41.refs_10_.refs_8_.refs_2_ = bf16[2,192,768]{2,1,0:T(8,128)(2,1)} collective-permute-done((bf16[2,192,768]{2,1,0:T(8,128)(2,1)}, bf16[2,192,768]{2,1,0:T(8,128)(2,1)}, u32[]{:S(2)}, u32[]{:S(2)}) %collective-permute-start.41) | collective-permute-done | bytes 589856 | tf_op jit(solution)/shard_map/ppermute | solution.py:566
  375.1 4.6 sums_4.1
  380.9 15.2 %collective-permute-done.44.refs_10_.refs_4_ = bf16[2,96,768]{2,1,0:T(8,128)(2,1)} collective-permute-done((bf16[2,96,768]{2,1,0:T(8,128)(2,1)}, bf16[2,96,768]{2,1,0:T(8,128)(2,1)}, u32[]{:S(2)}, u32[]{:S(2)}) %collective-permute-start.44) | collective-permute-done | bytes 294944 | tf_op jit(solution)/shard_map/ppermute | solution.py:566
  396.1 5.8 %sums_5.1 = (bf16[192,768]{1,0:T(8,128)(2,1)}, bf16[192,768]{1,0:T(8,128)(2,1)}, bf16[192,768]{1,0:T(8,128)(2,1)}, bf16[192,768]{1,0:T(8,128)(2,1)}, bf16[512,76...) custom-call(s32[8]{0:T(128)} %copy-done.22, ...), custom_call_target="tpu_custom_call", output_to_operand_aliasing={{6}: (11, {})} | custom-call | bytes 10616832 | tf_op jit(solution)/shard_map/sums_5/pallas_call | solution.py:455
  406.6 10.4 %collective-permute-done.50.refs_6_.refs_7_ = bf16[192,768]{1,0:T(8,128)(2,1)} collective-permute-done((bf16[192,768]{1,0:T(8,128)(2,1)}, bf16[192,768]{1,0:T(8,128)(2,1)}, u32[]{:S(2)}, u32[]{:S(2)}) %collective-permute-start.50) | collective-permute-done | bytes 294944 | tf_op jit(solution)/shard_map/ppermute | solution.py:563
  417.0 10.0 %collective-permute-done.51.refs_7_.refs_8_ = bf16[192,768]{1,0:T(8,128)(2,1)} collective-permute-done((bf16[192,768]{1,0:T(8,128)(2,1)}, bf16[192,768]{1,0:T(8,128)(2,1)}, u32[]{:S(2)}, u32[]{:S(2)}) %collective-permute-start.51) | collective-permute-done | bytes 294944 | tf_op jit(solution)/shard_map/ppermute | solution.py:563
  431.1 7.8 %collective-permute-done.54.refs_12_.refs_9_ = bf16[192,768]{1,0:T(8,128)(2,1)} collective-permute-done((bf16[192,768]{1,0:T(8,128)(2,1)}, bf16[192,768]{1,0:T(8,128)(2,1)}, u32[]{:S(2)}, u32[]{:S(2)}) %collective-permute-start.54) | collective-permute-done | bytes 294944 | tf_op jit(solution)/shard_map/ppermute | solution.py:563
  449.3 12.2 %collective-permute-done.56.refs_11_ = bf16[128,768]{1,0:T(8,128)(2,1)S(1)} collective-permute-done((bf16[128,768]{1,0:T(8,128)(2,1)}, bf16[128,768]{1,0:T(8,128)(2,1)S(1)}, u32[]{:S(2)}, u32[]{:S(2)}) %collective-permute-start.56) | collective-permute-done | bytes 196640 | tf_op jit(solution)/shard_map/ppermute | solution.py:563
  463.7 4.2 collective-permute-done.58.refs_13_
  (239 shorter events, 143.2 us)
Async XLA Ops:
  32.3 24.8 %collective-permute-start.9 = (bf16[2,4,48,768]{3,2,1,0:T(8,128)(2,1)S(1)}, bf16[2,4,48,768]{3,2,1,0:T(8,128)(2,1)S(1)}, u32[]{:S(2)}, u32[]{:S(2)}) collective-permute-start(bf16[2,4,48,768]{3,2,1,0:T(8,128)(2,1)S(1)} %get-tuple-element.105.refs_2_.refs_7_.refs_17_), channel_id=1, source_target_pairs={{0,4},{4,0},{8,12},{12,8},{16,20},{20,16},{24,28},{28,24},{1,5},{5... | collective-permute-start | bytes 1769480 | tf_op jit(solution)/shard_map/ppermute | solution.py:569
  33.8 23.2 %collective-permute-start.8 = (bf16[2,4,48,768]{3,2,1,0:T(8,128)(2,1)S(1)}, bf16[2,4,48,768]{3,2,1,0:T(8,128)(2,1)S(1)}, u32[]{:S(2)}, u32[]{:S(2)}) collective-permute-start(bf16[2,4,48,768]{3,2,1,0:T(8,128)(2,1)S(1)} %get-tuple-element.104.refs_5_.refs_0_.refs_4_.refs_14_), channel_id=1, source_target_pairs={{0,2},{1,3},{2,0},{3,1},{4,6},{5,7},{6,4},{7,5},{8,10},{9,11},{10,... | collective-permute-start | bytes 1769480 | tf_op jit(solution)/shard_map/ppermute | solution.py:572
  36.3 20.8 %collective-permute-start.4 = (bf16[224,768]{1,0:T(8,128)(2,1)S(1)}, bf16[224,768]{1,0:T(8,128)(2,1)S(1)}, u32[]{:S(2)}, u32[]{:S(2)}) collective-permute-start(bf16[224,768]{1,0:T(8,128)(2,1)S(1)} %pack_vec.1.refs_4_.refs_1_), channel_id=1, source_target_pairs={{0,16},{4,20},{8,24},{12,28},{16,0},{20,4},{24,8},{28,12},{1,17},{... | collective-permute-start | bytes 1032200 | tf_op jit(solution)/shard_map/ppermute | solution.py:563
  58.7 19.2 %collective-permute-start.12 = (bf16[4,2,4,48,768]{4,3,2,1,0:T(8,128)(2,1)S(1)}, bf16[4,2,4,48,768]{4,3,2,1,0:T(8,128)(2,1)}, u32[]{:S(2)}, u32[]{:S(2)}) collective-permute-start(bf16[4,2,4,48,768]{4,3,2,1,0:T(8,128)(2,1)S(1)} %merge.5.refs_4_), channel_id=1, source_target_pairs={{0,1},{1,0},{2,3},{3,2},{4,5},{5,4},{6,7},{7,6},{8,9},{9,8},{10,11... | collective-permute-start | bytes 7077896 | tf_op jit(solution)/shard_map/ppermute | solution.py:575
  58.8 18.2 %collective-permute-start.11 = (bf16[4,112,768]{2,1,0:T(8,128)(2,1)}, bf16[4,112,768]{2,1,0:T(8,128)(2,1)}, u32[]{:S(2)}, u32[]{:S(2)}) collective-permute-start(bf16[4,112,768]{2,1,0:T(8,128)(2,1)} %get-tuple-element.107.refs_2_), channel_id=1, source_target_pairs={{0,2},{1,3},{2,0},{3,1},{4,6},{5,7},{6,4},{7,5},{8,10},{9,11},{10,... | collective-permute-start | bytes 2064392 | tf_op jit(solution)/shard_map/ppermute | solution.py:572
  60.3 17.6 %collective-permute-start.10 = (bf16[4,112,768]{2,1,0:T(8,128)(2,1)S(1)}, bf16[4,112,768]{2,1,0:T(8,128)(2,1)}, u32[]{:S(2)}, u32[]{:S(2)}) collective-permute-start(bf16[4,112,768]{2,1,0:T(8,128)(2,1)S(1)} %get-tuple-element.106.refs_4_.refs_0_), channel_id=1, source_target_pairs={{0,4},{4,0},{8,12},{12,8},{16,20},{20,16},{24,28},{28,24},{1,5},{5... | collective-permute-start | bytes 2064392 | tf_op jit(solution)/shard_map/ppermute | solution.py:569
  63.6 27.8 %collective-permute-start.18 = (bf16[288,768]{1,0:T(8,128)(2,1)}, bf16[288,768]{1,0:T(8,128)(2,1)}, u32[]{:S(2)}, u32[]{:S(2)}) collective-permute-start(bf16[288,768]{1,0:T(8,128)(2,1)} %pack_all.1.refs_5_.refs_1_), channel_id=1, source_target_pairs={{0,16},{4,20},{8,24},{12,28},{16,0},{20,4},{24,8},{28,12},{1,17},{... | collective-permute-start | bytes 1327112 | tf_op jit(solution)/shard_map/ppermute | solution.py:563
  81.1 24.4 %collective-permute-start.19 = (bf16[2,4,112,768]{3,2,1,0:T(8,128)(2,1)}, bf16[2,4,112,768]{3,2,1,0:T(8,128)(2,1)}, u32[]{:S(2)}, u32[]{:S(2)}) collective-permute-start(bf16[2,4,112,768]{3,2,1,0:T(8,128)(2,1)} %get-tuple-element.110.refs_8_.refs_13_), channel_id=1, source_target_pairs={{0,1},{1,0},{2,3},{3,2},{4,5},{5,4},{6,7},{7,6},{8,9},{9,8},{10,11... | collective-permute-start | bytes 4128776 | tf_op jit(solution)/shard_map/ppermute | solution.py:575
  81.1 32.9 %collective-permute-start.16 = (bf16[2,4,112,768]{3,2,1,0:T(8,128)(2,1)}, bf16[2,4,112,768]{3,2,1,0:T(8,128)(2,1)}, u32[]{:S(2)}, u32[]{:S(2)}) collective-permute-start(bf16[2,4,112,768]{3,2,1,0:T(8,128)(2,1)} %get-tuple-element.110.refs_8_.refs_13_), channel_id=1, source_target_pairs={{0,4},{4,0},{8,12},{12,8},{16,20},{20,16},{24,28},{28,24},{1,5},{5... | collective-permute-start | bytes 4128776 | tf_op jit(solution)/shard_map/ppermute | solution.py:569
  82.6 31.4 %collective-permute-start.15 = (bf16[2,4,112,768]{3,2,1,0:T(8,128)(2,1)}, bf16[2,4,112,768]{3,2,1,0:T(8,128)(2,1)}, u32[]{:S(2)}, u32[]{:S(2)}) collective-permute-start(bf16[2,4,112,768]{3,2,1,0:T(8,128)(2,1)} %get-tuple-element.108.refs_9_.refs_4_), channel_id=1, source_target_pairs={{0,1},{1,0},{2,3},{3,2},{4,5},{5,4},{6,7},{7,6},{8,9},{9,8},{10,11... | collective-permute-start | bytes 4128776 | tf_op jit(solution)/shard_map/ppermute | solution.py:575
  82.9 32.7 %collective-permute-start.14 = (bf16[2,4,112,768]{3,2,1,0:T(8,128)(2,1)}, bf16[2,4,112,768]{3,2,1,0:T(8,128)(2,1)}, u32[]{:S(2)}, u32[]{:S(2)}) collective-permute-start(bf16[2,4,112,768]{3,2,1,0:T(8,128)(2,1)} %get-tuple-element.108.refs_9_.refs_4_), channel_id=1, source_target_pairs={{0,2},{1,3},{2,0},{3,1},{4,6},{5,7},{6,4},{7,5},{8,10},{9,11},{10,... | collective-permute-start | bytes 4128776 | tf_op jit(solution)/shard_map/ppermute | solution.py:572
  119.8 21.1 %collective-permute-start.20 = (bf16[4,144,768]{2,1,0:T(8,128)(2,1)S(1)}, bf16[4,144,768]{2,1,0:T(8,128)(2,1)S(1)}, u32[]{:S(2)}, u32[]{:S(2)}) collective-permute-start(bf16[4,144,768]{2,1,0:T(8,128)(2,1)S(1)} %get-tuple-element.111.refs_0_.refs_4_), channel_id=1, source_target_pairs={{0,4},{4,0},{8,12},{12,8},{16,20},{20,16},{24,28},{28,24},{1,5},{5... | collective-permute-start | bytes 2654216 | tf_op jit(solution)/shard_map/ppermute | solution.py:569
  121.3 20.7 %collective-permute-start.21 = (bf16[4,144,768]{2,1,0:T(8,128)(2,1)S(1)}, bf16[4,144,768]{2,1,0:T(8,128)(2,1)S(1)}, u32[]{:S(2)}, u32[]{:S(2)}) collective-permute-start(bf16[4,144,768]{2,1,0:T(8,128)(2,1)S(1)} %get-tuple-element.112.refs_2_), channel_id=1, source_target_pairs={{0,2},{1,3},{2,0},{3,1},{4,6},{5,7},{6,4},{7,5},{8,10},{9,11},{10,... | collective-permute-start | bytes 2654216 | tf_op jit(solution)/shard_map/ppermute | solution.py:572
  150.3 19.0 %collective-permute-start.23 = (bf16[2,4,48,768]{3,2,1,0:T(8,128)(2,1)}, bf16[2,4,48,768]{3,2,1,0:T(8,128)(2,1)}, u32[]{:S(2)}, u32[]{:S(2)}) collective-permute-start(bf16[2,4,48,768]{3,2,1,0:T(8,128)(2,1)} %get-tuple-element.113.refs_4_.refs_0_.refs_9_), channel_id=1, source_target_pairs={{0,2},{1,3},{2,0},{3,1},{4,6},{5,7},{6,4},{7,5},{8,10},{9,11},{10,... | collective-permute-start | bytes 1769480 | tf_op jit(solution)/shard_map/ppermute | solution.py:572
  150.9 29.6 %collective-permute-start.25 = (bf16[2,4,48,768]{3,2,1,0:T(8,128)(2,1)}, bf16[2,4,48,768]{3,2,1,0:T(8,128)(2,1)}, u32[]{:S(2)}, u32[]{:S(2)}) collective-permute-start(bf16[2,4,48,768]{3,2,1,0:T(8,128)(2,1)} %get-tuple-element.114.refs_4_.refs_0_.refs_9_), channel_id=1, source_target_pairs={{0,2},{1,3},{2,0},{3,1},{4,6},{5,7},{6,4},{7,5},{8,10},{9,11},{10,... | collective-permute-start | bytes 1769480 | tf_op jit(solution)/shard_map/ppermute | solution.py:572
  152.3 17.0 %collective-permute-start.24 = (bf16[2,4,48,768]{3,2,1,0:T(8,128)(2,1)}, bf16[2,4,48,768]{3,2,1,0:T(8,128)(2,1)}, u32[]{:S(2)}, u32[]{:S(2)}) collective-permute-start(bf16[2,4,48,768]{3,2,1,0:T(8,128)(2,1)} %get-tuple-element.117.refs_2_.refs_7_.refs_12_), channel_id=1, source_target_pairs={{0,4},{4,0},{8,12},{12,8},{16,20},{20,16},{24,28},{28,24},{1,5},{5... | collective-permute-start | bytes 1769480 | tf_op jit(solution)/shard_map/ppermute | solution.py:569
  152.9 27.6 %collective-permute-start.26 = (bf16[2,4,48,768]{3,2,1,0:T(8,128)(2,1)}, bf16[2,4,48,768]{3,2,1,0:T(8,128)(2,1)}, u32[]{:S(2)}, u32[]{:S(2)}) collective-permute-start(bf16[2,4,48,768]{3,2,1,0:T(8,128)(2,1)} %get-tuple-element.118.refs_2_.refs_7_.refs_12_), channel_id=1, source_target_pairs={{0,4},{4,0},{8,12},{12,8},{16,20},{20,16},{24,28},{28,24},{1,5},{5... | collective-permute-start | bytes 1769480 | tf_op jit(solution)/shard_map/ppermute | solution.py:569
  186.7 26.1 %collective-permute-start.28 = (bf16[4,2,4,48,768]{4,3,2,1,0:T(8,128)(2,1)}, bf16[4,2,4,48,768]{4,3,2,1,0:T(8,128)(2,1)}, u32[]{:S(2)}, u32[]{:S(2)}) collective-permute-start(bf16[4,2,4,48,768]{4,3,2,1,0:T(8,128)(2,1)} %merge.8.refs_9_), channel_id=1, source_target_pairs={{0,1},{1,0},{2,3},{3,2},{4,5},{5,4},{6,7},{7,6},{8,9},{9,8},{10,11... | collective-permute-start | bytes 7077896 | tf_op jit(solution)/shard_map/ppermute | solution.py:575
  245.7 17.6 %collective-permute-start.34 = (bf16[2,2,2,4,96,768]{5,4,3,2,1,0:T(8,128)(2,1)}, bf16[2,2,2,4,96,768]{5,4,3,2,1,0:T(8,128)(2,1)}, u32[]{:S(2)}, u32[]{:S(2)}) collective-permute-start(bf16[2,2,2,4,96,768]{5,4,3,2,1,0:T(8,128)(2,1)} %get-tuple-element.138), channel_id=1, source_target_pairs={{0,1},{1,0},{2,3},{3,2},{4,5},{5,4},{6,7},{7,6},{8,9},{9,8},{10,11... | collective-permute-start | bytes 14155784 | tf_op jit(solution)/shard_map/ppermute | solution.py:575
  267.8 28.4 %collective-permute-start.37 = (bf16[768,768]{1,0:T(8,128)(2,1)}, bf16[768,768]{1,0:T(8,128)(2,1)}, u32[]{:S(2)}, u32[]{:S(2)}) collective-permute-start(bf16[768,768]{1,0:T(8,128)(2,1)} %get-tuple-element.154), channel_id=1, source_target_pairs={{0,2},{1,3},{2,0},{3,1},{4,6},{5,7},{6,4},{7,5},{8,10},{9,11},{10,... | collective-permute-start | bytes 3538952 | tf_op jit(solution)/shard_map/ppermute | solution.py:572
  269.3 28.0 %collective-permute-start.36 = (bf16[768,768]{1,0:T(8,128)(2,1)}, bf16[768,768]{1,0:T(8,128)(2,1)}, u32[]{:S(2)}, u32[]{:S(2)}) collective-permute-start(bf16[768,768]{1,0:T(8,128)(2,1)} %get-tuple-element.140.refs_16_), channel_id=1, source_target_pairs={{0,4},{4,0},{8,12},{12,8},{16,20},{20,16},{24,28},{28,24},{1,5},{5... | collective-permute-start | bytes 3538952 | tf_op jit(solution)/shard_map/ppermute | solution.py:569
  302.4 28.7 %collective-permute-start.39 = (bf16[768,768]{1,0:T(8,128)(2,1)}, bf16[768,768]{1,0:T(8,128)(2,1)}, u32[]{:S(2)}, u32[]{:S(2)}) collective-permute-start(bf16[768,768]{1,0:T(8,128)(2,1)} %get-tuple-element.159), channel_id=1, source_target_pairs={{0,2},{1,3},{2,0},{3,1},{4,6},{5,7},{6,4},{7,5},{8,10},{9,11},{10,... | collective-permute-start | bytes 3538952 | tf_op jit(solution)/shard_map/ppermute | solution.py:572
  303.1 28.4 %collective-permute-start.38 = (bf16[768,768]{1,0:T(8,128)(2,1)}, bf16[768,768]{1,0:T(8,128)(2,1)}, u32[]{:S(2)}, u32[]{:S(2)}) collective-permute-start(bf16[768,768]{1,0:T(8,128)(2,1)} %get-tuple-element.156.refs_19_), channel_id=1, source_target_pairs={{0,4},{4,0},{8,12},{12,8},{16,20},{20,16},{24,28},{28,24},{1,5},{5... | collective-permute-start | bytes 3538952 | tf_op jit(solution)/shard_map/ppermute | solution.py:569
  338.8 36.3 %collective-permute-start.45 = (bf16[2,2,2,4,64,768]{5,4,3,2,1,0:T(8,128)(2,1)}, bf16[2,2,2,4,64,768]{5,4,3,2,1,0:T(8,128)(2,1)}, u32[]{:S(2)}, u32[]{:S(2)}) collective-permute-start(bf16[2,2,2,4,64,768]{5,4,3,2,1,0:T(8,128)(2,1)} %get-tuple-element.166.refs_11_), channel_id=1, source_target_pairs={{0,1},{1,0},{2,3},{3,2},{4,5},{5,4},{6,7},{7,6},{8,9},{9,8},{10,11... | collective-permute-start | bytes 9437192 | tf_op jit(solution)/shard_map/ppermute | solution.py:575
  338.9 35.0 %collective-permute-start.43 = (bf16[960,768]{1,0:T(8,128)(2,1)}, bf16[960,768]{1,0:T(8,128)(2,1)}, u32[]{:S(2)}, u32[]{:S(2)}) collective-permute-start(bf16[960,768]{1,0:T(8,128)(2,1)} %get-tuple-element.165), channel_id=1, source_target_pairs={{0,2},{1,3},{2,0},{3,1},{4,6},{5,7},{6,4},{7,5},{8,10},{9,11},{10,... | collective-permute-start | bytes 4423688 | tf_op jit(solution)/shard_map/ppermute | solution.py:572
  340.4 34.7 %collective-permute-start.42 = (bf16[960,768]{1,0:T(8,128)(2,1)}, bf16[960,768]{1,0:T(8,128)(2,1)}, u32[]{:S(2)}, u32[]{:S(2)}) collective-permute-start(bf16[960,768]{1,0:T(8,128)(2,1)} %get-tuple-element.164.refs_9_), channel_id=1, source_target_pairs={{0,4},{4,0},{8,12},{12,8},{16,20},{20,16},{24,28},{28,24},{1,5},{5... | collective-permute-start | bytes 4423688 | tf_op jit(solution)/shard_map/ppermute | solution.py:569
  340.9 29.0 %collective-permute-start.41 = (bf16[2,192,768]{2,1,0:T(8,128)(2,1)}, bf16[2,192,768]{2,1,0:T(8,128)(2,1)}, u32[]{:S(2)}, u32[]{:S(2)}) collective-permute-start(bf16[2,192,768]{2,1,0:T(8,128)(2,1)} %get-tuple-element.163), channel_id=1, source_target_pairs={{0,16},{4,20},{8,24},{12,28},{16,0},{20,4},{24,8},{28,12},{1,17},{... | collective-permute-start | bytes 1769480 | tf_op jit(solution)/shard_map/ppermute | solution.py:566
  401.9 25.1 %collective-permute-start.48 = (bf16[512,768]{1,0:T(8,128)(2,1)}, bf16[512,768]{1,0:T(8,128)(2,1)}, u32[]{:S(2)}, u32[]{:S(2)}) collective-permute-start(bf16[512,768]{1,0:T(8,128)(2,1)} %get-tuple-element.173), channel_id=1, source_target_pairs={{0,4},{4,0},{8,12},{12,8},{16,20},{20,16},{24,28},{28,24},{1,5},{5... | collective-permute-start | bytes 2359304 | tf_op jit(solution)/shard_map/ppermute | solution.py:569
  403.4 23.6 %collective-permute-start.49 = (bf16[512,768]{1,0:T(8,128)(2,1)}, bf16[512,768]{1,0:T(8,128)(2,1)}, u32[]{:S(2)}, u32[]{:S(2)}) collective-permute-start(bf16[512,768]{1,0:T(8,128)(2,1)} %get-tuple-element.174), channel_id=1, source_target_pairs={{0,2},{1,3},{2,0},{3,1},{4,6},{5,7},{6,4},{7,5},{8,10},{9,11},{10,... | collective-permute-start | bytes 2359304 | tf_op jit(solution)/shard_map/ppermute | solution.py:572
  404.9 22.1 %collective-permute-start.51 = (bf16[192,768]{1,0:T(8,128)(2,1)}, bf16[192,768]{1,0:T(8,128)(2,1)}, u32[]{:S(2)}, u32[]{:S(2)}) collective-permute-start(bf16[192,768]{1,0:T(8,128)(2,1)} %get-tuple-element.177), channel_id=1, source_target_pairs={{0,16},{4,20},{8,24},{12,28},{16,0},{20,4},{24,8},{28,12},{1,17},{... | collective-permute-start | bytes 884744 | tf_op jit(solution)/shard_map/ppermute | solution.py:563
  444.8 23.0 %collective-permute-start.55 = (bf16[288,768]{1,0:T(8,128)(2,1)}, bf16[288,768]{1,0:T(8,128)(2,1)S(1)}, u32[]{:S(2)}, u32[]{:S(2)}) collective-permute-start(bf16[288,768]{1,0:T(8,128)(2,1)} %get-tuple-element.183), channel_id=1, source_target_pairs={{0,8},{4,12},{8,0},{12,4},{16,24},{20,28},{24,16},{28,20},{1,9},{5... | collective-permute-start | bytes 1327112 | tf_op jit(solution)/shard_map/ppermute | solution.py:566
  446.9 20.9 %collective-permute-start.58 = (bf16[128,768]{1,0:T(8,128)(2,1)}, bf16[128,768]{1,0:T(8,128)(2,1)S(1)}, u32[]{:S(2)}, u32[]{:S(2)}) collective-permute-start(bf16[128,768]{1,0:T(8,128)(2,1)} %get-tuple-element.187), channel_id=1, source_target_pairs={{0,24},{4,28},{8,0},{12,4},{16,8},{20,12},{24,16},{28,20},{1,25},{... | collective-permute-start | bytes 589832 | tf_op jit(solution)/shard_map/ppermute | solution.py:563
  (64 other events, 489.3 us)

commit v3 on v2

--- a/solution.py
+++ b/solution.py
@@ -23,6 +23,29 @@
 ANY = pl.BlockSpec(memory_space=pltpu.HBM)
 SMEM = pl.BlockSpec(memory_space=pltpu.SMEM)
 VMEM = pl.BlockSpec(memory_space=pltpu.VMEM)
+LAZY = object()
+
+
+class Lazy:
+    def __init__(self, far, near, sem, out):
+        self.near = near
+        self.copy = pltpu.make_async_copy(near, far, sem) if out else pltpu.make_async_copy(far, near, sem)
+        self.flying = False
+
+    def begin(self):
+        self.copy.start()
+        self.flying = True
+
+    def ready(self):
+        if self.flying:
+            self.copy.wait()
+            self.flying = False
+        return self.near
+
+
+def begin(*operands):
+    for v in operands:
+        v.begin()
 
 G1, G2, G3, C1, BQ, BV, C2, BO, C3, B2 = range(10)
 VROWS = 16
@@ -182,17 +205,22 @@
 
 
 def attn_fwd(plan, npieces, find, m, *refs):
-    scal, x_ref, vec_ref, pb_ref = refs[:4]
+    scal, x_in, vec_in, pb_in = refs[:4]
     pieces = find(refs[4 : 4 + npieces])
-    x1_ref, a1_ref, un_ref, p_ref, o_ref, a2_ref = refs[4 + npieces : 10 + npieces]
+    x1_out, a1_out, un_out, p_out, o_out, a2_out = refs[4 + npieces : 10 + npieces]
     wa, sems = refs[10 + npieces :]
+    begin(x_in, vec_in)
     loads = start(plan.load_a(scal, pieces, m, wa), sems)
+    begin(pb_in)
+    x_ref, vec_ref = x_in.ready(), vec_in.ready()
     n1, _ = ln_stats(x_ref[...])
     a1 = (n1 * vec_ref[G1 : G1 + 1] + vec_ref[C1 : C1 + 1]).astype(BF)
-    a1_ref[...] = a1
+    a1_out.near[...] = a1
+    a1_out.begin()
     seg_row = seg_of(scal, lax.broadcasted_iota(jnp.int32, (T, T), 1))
     seg_col = seg_of(scal, lax.broadcasted_iota(jnp.int32, (T, T), 0))
     same = seg_row == seg_col
+    pb_ref, un_ref = pb_in.ready(), un_out.near
     wait(loads)
     for f in range(4):
         part = dot(a1, wa[:, :, :, :, 512 * f : 512 * f + 512].reshape(D, 512)) + pb_ref[0:1, 512 * f : 512 * f + 512]
@@ -204,34 +232,26 @@
             if u < HEADS:
                 val = val * BF(0.125)
             un_ref[u] = val
+    un_out.begin()
+    o_ref = o_out.near
     for h in range(HEADS):
         s = jnp.where(same, dot_nt(un_ref[h], un_ref[HEADS + h]), -1e30)
         ex = jnp.exp(s - jnp.max(s, axis=-1, keepdims=True))
         p = ex * (1.0 / jnp.sum(ex, axis=-1, keepdims=True))
-        p_ref[h] = p
+        p_out.near[h] = p
         o_ref[:, 64 * h : 64 * h + 64] = dot(p.astype(BF), un_ref[2 * HEADS + h])
+    p_out.begin()
+    o_out.begin()
     n2, _ = ln_stats(o_ref[...])
     a2 = (n2 * vec_ref[G2 : G2 + 1] + vec_ref[C2 : C2 + 1]).astype(BF)
-    a2_ref[...] = a2
+    a2_out.near[...] = a2
+    a2_out.begin()
     z = [dot(a2, wa[:, :, :, :, 2048 + 256 * f : 2304 + 256 * f].reshape(D, 256))[:, 64:] for f in range(4)]
-    x1_ref[...] = x_ref[...] + (jnp.concatenate(z, axis=1) + vec_ref[BO : BO + 1])
-
-
-def ff_fwd(plan, npieces, find, mb, mc, last, *refs):
-    scal, x1_ref, vec_ref, hid_ref = refs[:4]
-    pieces = find(refs[4 : 4 + npieces])
-    x2_ref, a3_ref, sl_ref, n4_ref, a4_ref = refs[4 + npieces : 9 + npieces]
-    wb, wc, sems = refs[9 + npieces :]
-    load_b = start(plan.load_b(scal, pieces, mb, wb), sems)
-    load_c = start(plan.load_c(scal, pieces, mc, wc), sems, len(load_b))
-    n3, _ = ln_stats(x1_ref[...])
-    a3 = (n3 * vec_ref[G3 : G3 + 1] + vec_ref[C3 : C3 + 1]).astype(BF)
-    a3_ref[...] = a3
-    wait(load_b)
-    for f in range(4):
-        cols = slice(768 * f, 768 * f + 768)
-        n4_ref[:, cols] = dot(a3, wb[:, :, :, :, cols].reshape(D, 768)) + hid_ref[B1 : B1 + 1, cols]
-
+    x1_out.near[...] = x_ref[...] + (jnp.concatenate(z, axis=1) + vec_ref[BO : BO + 1])
+    x1_out.begin()
+
+
+def hidden_rows(hid_ref, sl_ref, n4_ref, a4_ref):
     def rows_step(i, carry):
         rows = pl.ds(i * RB, RB)
         total = jnp.zeros((RB, 1), F32)
@@ -259,42 +279,124 @@
         return carry
 
     lax.fori_loop(0, T // RB, rows_step, 0)
-    wait(load_c)
+
+
+def hidden(x1_in, vec_in, hid_in, wb, load_b, a3_out, sl_out, n4_out, a4_out):
+    x1_ref, vec_ref = x1_in.ready(), vec_in.ready()
+    n3, _ = ln_stats(x1_ref[...])
+    a3 = (n3 * vec_ref[G3 : G3 + 1] + vec_ref[C3 : C3 + 1]).astype(BF)
+    a3_out.near[...] = a3
+    a3_out.begin()
+    hid_ref = hid_in.ready()
+    n4_ref = n4_out.near
+    wait(load_b)
+    for f in range(4):
+        cols = slice(768 * f, 768 * f + 768)
+        n4_ref[:, cols] = dot(a3, wb[:, :, :, :, cols].reshape(D, 768)) + hid_ref[B1 : B1 + 1, cols]
+    hidden_rows(hid_ref, sl_out.near, n4_ref, a4_out.near)
+    begin(a4_out, n4_out, sl_out)
+
+
+def down(x1_in, vec_in, a4_ref, wc):
+    x1_ref, vec_ref = x1_in.ready(), vec_in.ready()
     acc = dot_nt(a4_ref[:, 0:768], wc[0].reshape(D, 768))
     for z in range(1, 4):
         acc += dot_nt(a4_ref[:, 768 * z : 768 * z + 768], wc[z].reshape(D, 768))
-    x2 = x1_ref[...] + (acc + vec_ref[B2 : B2 + 1])
+    return x1_ref[...] + (acc + vec_ref[B2 : B2 + 1])
+
+
+def valid_rows(scal):
+    seg = seg_of(scal, lax.broadcasted_iota(jnp.int32, (T, 1), 0))
+    return (seg < SEQS).astype(F32)
+
+
+def ff_fwd(plan, npieces, find, mb, mc, *refs):
+    scal, x1_in, vec_in, hid_in = refs[:4]
+    pieces = find(refs[4 : 4 + npieces])
+    x2_out, a3_out, sl_out, n4_out, a4_out = refs[4 + npieces : 9 + npieces]
+    wb, wc, sems = refs[9 + npieces :]
+    begin(x1_in, vec_in)
+    load_b = start(plan.load_b(scal, pieces, mb, wb), sems)
+    begin(hid_in)
+    load_c = start(plan.load_c(scal, pieces, mc, wc), sems, len(load_b))
+    hidden(x1_in, vec_in, hid_in, wb, load_b, a3_out, sl_out, n4_out, a4_out)
+    wait(load_c)
+    x2_out.near[...] = down(x1_in, vec_in, a4_out.near, wc)
+    x2_out.begin()
+
+
+def ff_mid(plan, npieces, find, nouts, mb, *refs):
+    scal, x1_in, dy_in, vec_in, hid_in = refs[:5]
+    pieces = find(refs[5 : 5 + npieces])
+    a3_out, sl_out, n4_out, a4_out = refs[5 + npieces : 9 + npieces]
+    outs = refs[9 + npieces : 9 + npieces + nouts]
+    wb, gc, sems = refs[9 + npieces + nouts :]
+    begin(x1_in, vec_in)
+    load_b = start(plan.load_b(scal, pieces, mb, wb), sems)
+    begin(hid_in, dy_in)
+    hidden(x1_in, vec_in, hid_in, wb, load_b, a3_out, sl_out, n4_out, a4_out)
+    dz2t = (dy_in.ready()[...] * valid_rows(scal)).astype(BF).T
+    for z in range(4):
+        gc[z] = dot(dz2t, a4_out.near[:, 768 * z : 768 * z + 768]).astype(BF).reshape(4, 2, 2, 48, 768)
+    wait(start(plan.store_c(scal, gc, outs, 0), sems, len(load_b)))
+
+
+def down_grad(plan, nouts, *refs):
+    scal, dy_in, a4_in = refs[:3]
+    outs = refs[3 : 3 + nouts]
+    gc, sems = refs[3 + nouts :]
+    begin(dy_in, a4_in)
+    dz2t = dy_in.ready()[...].astype(BF).T
+    a4_ref = a4_in.ready()
+    for z in range(4):
+        gc[z] = dot(dz2t, a4_ref[:, 768 * z : 768 * z + 768]).astype(BF).reshape(4, 2, 2, 48, 768)
+    wait(start(plan.store_c(scal, gc, outs, 0), sems))
+
+
+def ff_out(plan, npieces, find, mc, *refs):
+    scal, x1_in, a4_in, vec_in = refs[:4]
+    pieces = find(refs[4 : 4 + npieces])
+    out, wc, sems = refs[4 + npieces :]
+    load_c = start(plan.load_c(scal, pieces, mc, wc), sems)
+    begin(a4_in, x1_in, vec_in)
+    wait(load_c)
+    out.near[...] = down(x1_in, vec_in, a4_in.ready(), wc) * valid_rows(scal)
+    out.begin()
+
+
+def ff_bwd(plan, npieces, find, nouts, mb, mc, last, with_c, *refs):
+    scal, dy_in, x1_in, a3_in, sl_in, n4_in, a4_in, vec_in, hid_in = refs[:9]
+    pieces = find(refs[9 : 9 + npieces])
+    dx1_out, gv_out, gh_out = refs[9 + npieces : 12 + npieces]
+    outs = refs[12 + npieces : 12 + npieces + nouts]
+    wb, wc, gb, da4, du_ref, sems = refs[12 + npieces + nouts : 18 + npieces + nouts]
+    gc = refs[18 + npieces + nouts] if with_c else None
+    begin(dy_in)
+    load_c = start(plan.load_c(scal, pieces, mc, wc), sems)
+    if with_c:
+        begin(a4_in)
+    begin(n4_in, hid_in, sl_in)
+    load_b = start(plan.load_b(scal, pieces, mb, wb), sems, len(load_c))
+    begin(a3_in, x1_in, vec_in)
+    base = len(load_c) + len(load_b)
+    gv_ref, gh_ref = gv_out.near, gh_out.near
+    dy = dy_in.ready()[...]
     if last:
-        seg = seg_of(scal, lax.broadcasted_iota(jnp.int32, (T, 1), 0))
-        x2 = x2 * (seg < SEQS).astype(F32)
-    x2_ref[...] = x2
-
-
-def ff_bwd(plan, npieces, find, nouts, mb, mc, last, *refs):
-    scal, dy_ref, x1_ref, a3_ref, sl_ref, n4_ref, a4_ref, vec_ref, hid_ref = refs[:9]
-    pieces = find(refs[9 : 9 + npieces])
-    dx1_ref, gv_ref, gh_ref = refs[9 + npieces : 12 + npieces]
-    outs = refs[12 + npieces : 12 + npieces + nouts]
-    wb, wc, gb, gc, da4, du_ref, sems = refs[12 + npieces + nouts :]
-    load_c = start(plan.load_c(scal, pieces, mc, wc), sems)
-    load_b = start(plan.load_b(scal, pieces, mb, wb), sems, len(load_c))
-    base = len(load_c) + len(load_b)
-    dy = dy_ref[...]
-    if last:
-        seg = seg_of(scal, lax.broadcasted_iota(jnp.int32, (T, 1), 0))
-        dy = dy * (seg < SEQS).astype(F32)
+        dy = dy * valid_rows(scal)
     dz2 = dy.astype(BF)
     gv_ref[...] = jnp.zeros_like(gv_ref)
     gh_ref[...] = jnp.zeros_like(gh_ref)
     gv_ref[B2 : B2 + 1] = jnp.sum(dz2.astype(F32), axis=0, keepdims=True)
-    dz2t = dz2.T
+    dz2t = dz2.T if with_c else None
     wait(load_c)
     for z in range(4):
         cols = slice(768 * z, 768 * z + 768)
         da4[:, cols] = dot(dz2, wc[z].reshape(D, 768))
-        gc[z] = dot(dz2t, a4_ref[:, cols]).astype(BF).reshape(4, 2, 2, 48, 768)
-    saves = start(plan.store_c(scal, gc, outs, 1), sems, base)
+        if with_c:
+            gc[z] = dot(dz2t, a4_in.ready()[:, cols]).astype(BF).reshape(4, 2, 2, 48, 768)
+    saves = start(plan.store_c(scal, gc, outs, 1), sems, base) if with_c else []
     base += len(saves)
+    n4_ref, hid_ref, sl_ref = n4_in.ready(), hid_in.ready(), sl_in.ready()
 
     def rows_step(i, carry):
         rows = pl.ds(i * RB, RB)
@@ -321,7 +423,8 @@
         return carry
 
     lax.fori_loop(0, T // RB, rows_step, 0)
-    a3t = a3_ref[...].T
+    gh_out.begin()
+    a3t = a3_in.ready()[...].T
     wait(load_b)
     da3 = jnp.zeros((T, D), F32)
     for i, (f, rc, ry) in enumerate(plan.blocks(scal)):
@@ -332,37 +435,43 @@
         base += len(more)
         saves += more
         da3 += dot_nt(du, wb[:, :, :, :, cols].reshape(D, 768))
-    n3, inv3 = ln_stats(x1_ref[...])
+    n3, inv3 = ln_stats(x1_in.ready()[...])
+    vec_ref = vec_in.ready()
     part, dg3, dc3 = ln_back(da3, vec_ref[G3 : G3 + 1], n3, inv3)
     gv_ref[G3 : G3 + 1] = dg3
     gv_ref[C3 : C3 + 1] = dc3
-    dx1_ref[...] = dy + part
+    dx1_out.near[...] = dy + part
+    begin(dx1_out, gv_out)
     wait(saves)
 
 
 def attn_bwd(plan, npieces, find, nouts, m, fold, *refs):
-    scal, dx1_ref, x_ref, a1_ref, un_ref, p_ref, o_ref, a2_ref, vec_ref = refs[:9]
+    scal, dx1_in, x_in, a1_in, un_in, p_in, o_in, a2_in, vec_in = refs[:9]
     pos = 9
     others = refs[pos : pos + (5 if fold else 0)]
     pos += len(others)
     pieces = find(refs[pos : pos + npieces])
     pos += npieces
-    dx_ref, gv_ref = refs[pos : pos + 2]
+    dx_out, gv_out = refs[pos : pos + 2]
     outs = refs[pos + 2 : pos + 2 + nouts]
     scratch = refs[pos + 2 + nouts :]
     wa, ga, dpm, dzp, do_ref = scratch[:5]
     vblk = scratch[5] if fold else None
     sems = scratch[-1]
+    begin(dx1_in)
     loads = start(plan.load_a(scal, pieces, m, wa), sems)
+    begin(o_in, vec_in, un_in, p_in, a1_in, a2_in, x_in, *others)
     base = len(loads)
-    dx1 = dx1_ref[...]
+    gv_ref = gv_out.near
+    dx1 = dx1_in.ready()[...]
     dz = dx1.astype(BF)
     gv_ref[...] = jnp.zeros_like(gv_ref)
     gv_ref[BO : BO + 1] = jnp.sum(dz.astype(F32), axis=0, keepdims=True)
     dzp[...] = jnp.concatenate(
         [jnp.concatenate([jnp.zeros((T, 64), BF), dz[:, 192 * f : 192 * f + 192]], axis=1) for f in range(4)], axis=1
     )
-    n2, inv2 = ln_stats(o_ref[...])
+    n2, inv2 = ln_stats(o_in.ready()[...])
+    vec_ref = vec_in.ready()
     wait(loads)
     da2 = dot_nt(dzp[...], wa[:, :, :, :, 2048:3072].reshape(D, 1024))
     do, dg2, dc2 = ln_back(da2, vec_ref[G2 : G2 + 1], n2, inv2)
@@ -371,6 +480,7 @@
     do = do.astype(BF)
     for f in range(4):
         dpm[:, 2048 + 256 * f : 2304 + 256 * f] = jnp.zeros((T, 256), BF)
+    un_ref, p_ref = un_in.ready(), p_in.ready()
     for h in range(HEADS):
         doh = do[:, 64 * h : 64 * h + 64]
         p = p_ref[h]
@@ -390,8 +500,8 @@
             if which != 1:
                 row = BQ if which == 0 else BV
                 gv_ref[row : row + 1, 64 * h : 64 * h + 64] = jnp.sum(grad.astype(F32), axis=0, keepdims=True)
-    a1t = a1_ref[...].T
-    a2t = a2_ref[...].T
+    a1t = a1_in.ready()[...].T
+    a2t = a2_in.ready()[...].T
     saves = []
     for i, (f, rc, ry) in enumerate(plan.blocks(scal)):
         main = dpm[:, pl.ds(pl.multiple_of(f * 512, 512), 512)]
@@ -404,13 +514,14 @@
         base += len(more)
         saves += more
     da1 = dot_nt(dpm[...], wa[...].reshape(D, FF))
-    n1, inv1 = ln_stats(x_ref[...])
+    n1, inv1 = ln_stats(x_in.ready()[...])
     part, dg1, dc1 = ln_back(da1, vec_ref[G1 : G1 + 1], n1, inv1)
     gv_ref[G1 : G1 + 1] = dg1
     gv_ref[C1 : C1 + 1] = dc1
-    dx_ref[...] = dx1 + part
+    dx_out.near[...] = dx1 + part
+    begin(dx_out, gv_out)
     if fold:
-        va0, vb1, va1, gh0, gh1 = (r[...] for r in others)
+        va0, vb1, va1, gh0, gh1 = (r.ready()[...] for r in others)
         v0 = gv_ref[...] + va0
         v1 = vb1 + va1
         for d in range(8):
@@ -433,31 +544,47 @@
         self.chained = chained
         self.token = None
         self.held = []
+        self.carrying = []
         self.carried = []
 
     def hold(self, *arrays):
         self.held += arrays
 
     def carry(self, *arrays):
-        self.carried = list(arrays)
+        self.carrying = list(arrays)
 
     def __call__(self, kernel, out_shape, in_specs, out_specs, args, scratch=(), mib=24, **options):
         deps = [self.token] if self.chained and self.token is not None else []
         deps += self.held
-        carried = self.carried
-        self.held, self.carried = [], []
+        carried = self.carrying
+        self.held, self.carrying = [], []
         n, k, m, q = len(args), len(deps), len(carried), len(out_shape)
+        lazy_in = [i for i, v in enumerate(in_specs) if v is LAZY]
+        lazy_out = [i for i, v in enumerate(out_specs) if v is LAZY]
+        lazy_scratch = [pltpu.VMEM(args[i].shape, args[i].dtype) for i in lazy_in]
+        lazy_scratch += [pltpu.VMEM(out_shape[i].shape, out_shape[i].dtype) for i in lazy_out]
+        if lazy_scratch:
+            lazy_scratch.append(pltpu.SemaphoreType.DMA((len(lazy_scratch),)))
 
         def body(*refs):
             first = n + k + m
-            kernel(*refs[:n], *refs[first : first + q], *refs[first + q + m :])
+            ins, outs = list(refs[:n]), list(refs[first : first + q])
+            rest = list(refs[first + q + m :])
+            near = rest[len(scratch) :]
+            made = []
+            for j, (group, i) in enumerate([(ins, i) for i in lazy_in] + [(outs, i) for i in lazy_out]):
+                made.append(Lazy(group[i], near[j], near[-1].at[j], group is outs))
+                group[i] = made[-1]
+            kernel(*ins, *outs, *rest[: len(scratch)])
+            for v in made:
+                v.ready()
 
         res = pl.pallas_call(
             body,
             out_shape=tuple(out_shape) + tuple(S(v.shape, v.dtype) for v in carried),
-            in_specs=list(in_specs) + [ANY] * (k + m),
-            out_specs=tuple(out_specs) + (ANY,) * m,
-            scratch_shapes=list(scratch),
+            in_specs=[ANY if v is LAZY else v for v in in_specs] + [ANY] * (k + m),
+            out_specs=tuple(ANY if v is LAZY else v for v in out_specs) + (ANY,) * m,
+            scratch_shapes=list(scratch) + lazy_scratch,
             input_output_aliases={n + k + i: q + i for i in range(m)},
             compiler_params=pltpu.CompilerParams(vmem_limit_bytes=mib * MIB),
             **options,
@@ -479,8 +606,8 @@
     return seq(
         functools.partial(attn_fwd, plan, n, find, m),
         (S((T, D), F32), S((T, D), BF), S((36, T, HD), BF), S((HEADS, T, T), F32), S((T, D), F32), S((T, D), BF)),
-        [SMEM, VMEM, VMEM, VMEM] + [ANY] * n,
-        [VMEM] * 6,
+        [SMEM, LAZY, LAZY, LAZY] + [ANY] * n,
+        [LAZY] * 6,
         (scal, x, vec, pbias, *pieces),
         [WA, pltpu.SemaphoreType.DMA((32,))],
         cost_estimate=cost(2 * T * D * FF * 6, WBYTES + 8e6),
@@ -489,14 +616,14 @@
     )
 
 
-def call_ff_fwd(seq, plan, scal, x1, vec, hid, pieces, mb, mc, last):
+def call_ff_fwd(seq, plan, scal, x1, vec, hid, pieces, mb, mc):
     pieces, find = flat(pieces)
     n = len(pieces)
     return seq(
-        functools.partial(ff_fwd, plan, n, find, mb, mc, last),
+        functools.partial(ff_fwd, plan, n, find, mb, mc),
         (S((T, D), F32), S((T, D), BF), S((T, FF), F32), S((T, FF), F32), S((T, FF), BF)),
-        [SMEM, VMEM, VMEM, VMEM] + [ANY] * n,
-        [VMEM] * 5,
+        [SMEM, LAZY, LAZY, LAZY] + [ANY] * n,
+        [LAZY] * 5,
         (scal, x1, vec, hid, *pieces),
         [WA, WC, pltpu.SemaphoreType.DMA((48,))],
         cost_estimate=cost(2 * T * D * FF * 6, 2 * WBYTES + 8e6),
@@ -505,23 +632,72 @@
     )
 
 
+def call_ff_mid(seq, plan, scal, x1, dy, vec, hid, pieces, mb):
+    pieces, find = flat(pieces)
+    n = len(pieces)
+    g = grad_shapes(plan, 1)
+    res = seq(
+        functools.partial(ff_mid, plan, n, find, len(g), mb),
+        (S((T, D), BF), S((T, FF), F32), S((T, FF), F32), S((T, FF), BF), *g),
+        [SMEM] + [LAZY] * 4 + [ANY] * n,
+        [LAZY] * 4 + [ANY] * len(g),
+        (scal, x1, dy, vec, hid, *pieces),
+        [WA, WC, pltpu.SemaphoreType.DMA((48,))],
+        cost_estimate=cost(2 * T * D * FF * 6, 2 * WBYTES + 8e6),
+        name="ff_mid",
+        mib=64,
+    )
+    return res[:4], res[4:]
+
+
+def call_down_grad(seq, plan, scal, dy, a4):
+    g = grad_shapes(plan, 1)
+    return seq(
+        functools.partial(down_grad, plan, len(g)),
+        g,
+        [SMEM, LAZY, LAZY],
+        [ANY] * len(g),
+        (scal, dy, a4),
+        [WC, pltpu.SemaphoreType.DMA((32,))],
+        cost_estimate=cost(2 * T * D * FF, WBYTES + 3e6),
+        name="ff_down_grad",
+        mib=64,
+    )
+
+
+def call_ff_out(seq, plan, scal, x1, a4, vec, pieces, mc):
+    pieces, find = flat(pieces)
+    n = len(pieces)
+    return seq(
+        functools.partial(ff_out, plan, n, find, mc),
+        [S((T, D), F32)],
+        [SMEM, LAZY, LAZY, LAZY] + [ANY] * n,
+        [LAZY],
+        (scal, x1, a4, vec, *pieces),
+        [WC, pltpu.SemaphoreType.DMA((32,))],
+        cost_estimate=cost(2 * T * D * FF * 3, WBYTES + 3e6),
+        name="ff_out",
+        mib=64,
+    )[0]
+
+
 def grad_shapes(plan, n, extra=0):
     if not plan.fast:
         return [S((4, 4, 2, 2, 48, D), BF)] * n
     return [S((2, 2, 2, 4, n * 48 + extra, D), BF)] * 2
 
 
-def call_ff_bwd(seq, plan, scal, dy, x1, a3, sl, n4, a4, vec, hid, pieces, mb, mc, last):
+def call_ff_bwd(seq, plan, scal, dy, x1, a3, sl, n4, a4, vec, hid, pieces, mb, mc, last, with_c):
     pieces, find = flat(pieces)
     n = len(pieces)
-    g = grad_shapes(plan, 2)
+    g = grad_shapes(plan, 2 if with_c else 1)
     res = seq(
-        functools.partial(ff_bwd, plan, n, find, len(g), mb, mc, last),
+        functools.partial(ff_bwd, plan, n, find, len(g), mb, mc, last, with_c),
         (S((T, D), F32), S((VROWS, D), F32), S((VROWS, FF), F32), *g),
-        [SMEM] + [VMEM] * 8 + [ANY] * n,
-        [VMEM] * 3 + [ANY] * len(g),
+        [SMEM] + [LAZY] * 8 + [ANY] * n,
+        [LAZY] * 3 + [ANY] * len(g),
         (scal, dy, x1, a3, sl, n4, a4, vec, hid, *pieces),
-        [WA, WC, WC, WC, pltpu.VMEM((T, FF), F32), pltpu.VMEM((T, FF), BF), pltpu.SemaphoreType.DMA((112,))],
+        [WA, WC, WC, pltpu.VMEM((T, FF), F32), pltpu.VMEM((T, FF), BF), pltpu.SemaphoreType.DMA((112,))] + [WC] * with_c,
         cost_estimate=cost(2 * T * D * FF * 8, 4 * WBYTES + 8e6),
         name="ff_bwd",
         mib=64,
@@ -538,8 +714,8 @@
     res = seq(
         functools.partial(attn_bwd, plan, n, find, len(g), m, fold),
         (S((T, D), F32), S((VROWS, D), F32), *g),
-        [SMEM] + [VMEM] * (8 + len(others)) + [ANY] * n,
-        [VMEM] * 2 + [ANY] * len(g),
+        [SMEM] + [LAZY] * (8 + len(others)) + [ANY] * n,
+        [LAZY] * 2 + [ANY] * len(g),
         (scal, dx1, x, a1, un, p, o, a2, vec, *others, *pieces),
         [WA, WC, pltpu.VMEM((T, FF), BF), pltpu.VMEM((T, 1024), BF), pltpu.VMEM((T, D), BF), *vblk, pltpu.SemaphoreType.DMA((64,))],
         cost_estimate=cost(2 * T * D * FF * 8, 2 * WBYTES + 8e6),
@@ -625,61 +801,177 @@
     )[0]
 
 
-def pack_all_kernel(l, wqkv, wo, w1, w2, out):
+def pack_ab_kernel(l, wqkv, wo, w1, out):
     a = jnp.concatenate([wqkv[l], wo[l]], axis=1)
-    out[0:48] = a[0:48]
-    out[144:192] = a[48:96]
-    pack_bc_rows(l, w1, w2, out, 48, 192)
-
-
-def pack_all(seq, l, weights):
+    for i in range(2):
+        out[96 * i : 96 * i + 48] = a[48 * i : 48 * i + 48]
+        out[96 * i + 48 : 96 * i + 96] = w1[l, 48 * i : 48 * i + 48]
+
+
+def pack_ab(seq, l, weights):
     return seq(
-        functools.partial(pack_all_kernel, l),
-        [S((288, D), BF)],
-        [VMEM] * 4,
+        functools.partial(pack_ab_kernel, l),
+        [S((192, D), BF)],
+        [VMEM] * 3,
         [VMEM],
         weights,
-        cost_estimate=cost(0, 4 * 288 * D),
-        name="pack_all",
+        cost_estimate=cost(0, 4 * 192 * D),
+        name="pack_ab",
     )[0]
 
 
-def zcat_kernel(r1, scal, p0, p1, p2, p3, o1, o2):
-    for k, ref in enumerate((p0, p1, p2, p3)):
+def pack_c_kernel(l, w2, o1, o2):
+    t = w2[l].T
+    for i, out in enumerate((o1, o2)):
+        for j in range(2):
+            out[:, 384 * j : 384 * j + 384] = t[96 * j + 48 * i : 96 * j + 48 * i + 48]
+
+
+def pack_c(seq, l, w2):
+    return seq(
+        functools.partial(pack_c_kernel, l),
+        [S((48, D), BF)] * 2,
+        [VMEM],
+        [VMEM] * 2,
+        (w2,),
+        cost_estimate=cost(0, 4 * 96 * D),
+        name="pack_c",
+    )
+
+
+def join_kernel(a, b, c, d, o1, o2):
+    o1[0] = a[...]
+    o1[1] = b[...]
+    o2[0] = c[...]
+    o2[1] = d[...]
+
+
+def join(seq, *parts):
+    shape = S((2, *parts[0].shape), BF)
+    return seq(join_kernel, [shape] * 2, [VMEM] * 4, [VMEM] * 2, parts, cost_estimate=cost(0, 16 * parts[0].size), name="join")
+
+
+Q_CUTS = ((0, 2), (2, 1), (3, 1))
+
+
+def zquad_kernel(scal, *refs):
+    high = scal[2] // 2
+    out = refs[-1]
+    first = 0
+    for k in range(0, len(refs) - 1, 2):
+        rows = refs[k].shape[1]
+        for part, pos in ((refs[k], high), (refs[k + 1], 1 - high)):
+            for i in range(2):
+                for r in range(rows):
+                    for ri in range(2):
+                        out[first + r, ri, 2 * pos + i] = part[i, r, ri]
+        first += rows
+
+
+def zquad(seq, scal, *parts):
+    return seq(
+        zquad_kernel,
+        [S((2, 2, 4, 48, D), BF)],
+        [SMEM] + [VMEM] * len(parts),
+        [VMEM],
+        (scal, *parts),
+        cost_estimate=cost(0, 64 * 48 * D),
+        name="zquad",
+        mib=64,
+    )[0]
+
+
+def pile_vec_kernel(scal, h1, x1, h2, y2, o1, o2, own, *outs):
+    for i, (out, parts) in enumerate(((o1, (h1, x1)), (o2, (h2, y2)))):
+        for k, part in enumerate(parts):
+            out[k] = part[...]
+            own[i, k] = part[...]
+    for l in range(LAYERS):
+        low, high = [], []
+        for z in range(4):
+            for x in range(2):
+                rows = o1[lax.rem(scal[3] + x, 2), z, 96:112].astype(F32)
+                low.append(rows[:, 96 * l : 96 * l + 96])
+                high.append(rows[:, 384 * l : 384 * l + 384])
+        vec = jnp.concatenate(low, axis=1)
+        outs[3 * l][...] = vec
+        outs[3 * l + 1][...] = jnp.concatenate(high, axis=1)
+        bias = jnp.concatenate([vec[BQ : BQ + 1], jnp.zeros((1, D), F32), vec[BV : BV + 1]], axis=1)
+        parts = [bias[:, 576 * f : 576 * f + 512] for f in range(4)]
+        for f in range(4):
+            parts += [bias[:, 576 * f + 512 : 576 * f + 576], jnp.zeros((1, 64), F32)]
+        outs[3 * l + 2][...] = jnp.concatenate(parts, axis=1)
+
+
+def pile_vec(seq, scal, parts):
+    rows = parts[0].shape[1]
+    outs = [S((2, 4, rows, D), BF)] * 2 + [S((2, 2, 4, rows, D), BF)]
+    outs += [S((VROWS, D), F32), S((VROWS, FF), F32), S((1, 2560), F32)] * LAYERS
+    res = seq(
+        pile_vec_kernel,
+        outs,
+        [SMEM] + [VMEM] * 4,
+        [VMEM] * len(outs),
+        (scal, *parts),
+        cost_estimate=cost(0, 120 * rows * D),
+        name="pile_vec",
+        mib=64,
+    )
+    return res[:2], res[2], res[3::3], res[4::3], res[5::3]
+
+
+def zcat_kernel(r1, scal, *refs):
+    n = (len(refs) - 2) if len(refs) == 6 else (len(refs) - 3)
+    o1, o2 = refs[n : n + 2]
+    for k, ref in enumerate(refs[:4]):
         z = lax.rem(scal[2] + 4 - k, 4)
         o1[z] = ref[0:r1]
         o2[z] = ref[r1:]
-
-
-def zcat(seq, scal, parts, r1):
+    for i, ref in enumerate(refs[4:n]):
+        refs[-1][i] = ref[...]
+
+
+def zcat(seq, scal, parts, r1, *riders):
     r2 = parts[0].shape[0] - r1
+    outs = [S((4, r1, D), BF), S((4, r2, D), BF)]
+    if riders:
+        outs.append(S((len(riders), *riders[0].shape), BF))
     return seq(
         functools.partial(zcat_kernel, r1),
-        (S((4, r1, D), BF), S((4, r2, D), BF)),
-        [SMEM] + [VMEM] * 4,
-        [VMEM] * 2,
-        (scal, *parts),
+        outs,
+        [SMEM] + [VMEM] * (4 + len(riders)),
+        [VMEM] * len(outs),
+        (scal, *parts, *riders),
         cost_estimate=cost(0, 8 * (r1 + r2) * D * 2),
         name="zcat",
     )
 
 
-def pile_kernel(first, rows, h1, x1, h2, y2, o1, o2):
-    mine = pl.ds(first, rows)
-    o1[0] = h1[:, mine]
-    o1[1] = x1[:, mine]
-    o2[0] = h2[:, mine]
-    o2[1] = y2[:, mine]
-
-
-def pile(seq, first, rows, parts):
+def pile_kernel(cuts, scal, h1, x1, h2, y2, *refs):
+    outs = refs[-2 * len(cuts) :] if len(refs) == 2 * len(cuts) else refs[2 : 2 + 2 * len(cuts)]
+    for i, (first, rows) in enumerate(cuts):
+        mine = pl.ds(first, rows)
+        for j, parts in enumerate(((h1, x1), (h2, y2))):
+            for k, part in enumerate(parts):
+                outs[2 * i + j][k] = part[:, mine]
+    if len(refs) > 2 * len(cuts):
+        low = lax.rem(scal[2], 2)
+        for (first, rows), out in zip(Q_CUTS, refs[2 + 2 * len(cuts) :]):
+            out[low] = refs[0][first : first + rows]
+            out[1 - low] = refs[1][first : first + rows]
+
+
+def pile(seq, scal, parts, cuts, pair=()):
+    outs = [S((2, 4, rows, D), BF) for _, rows in cuts for _ in range(2)]
+    if pair:
+        outs += [S((2, rows, *pair[0].shape[1:]), BF) for _, rows in Q_CUTS]
     return seq(
-        functools.partial(pile_kernel, first, rows),
-        [S((2, 4, rows, D), BF)] * 2,
-        [VMEM] * 4,
-        [VMEM] * 2,
-        parts,
-        cost_estimate=cost(0, 64 * rows * D),
+        functools.partial(pile_kernel, cuts),
+        outs,
+        [SMEM] + [VMEM] * (4 + len(pair)),
+        [VMEM] * len(outs),
+        (scal, *parts, *pair),
+        cost_estimate=cost(0, 64 * sum(rows for _, rows in cuts) * D),
         name="pile",
     )
 
@@ -757,22 +1049,20 @@
 
 
 def finish_kernel(scal, *refs):
-    keep_bc, got_bc, keep_a, got_a, last = refs[:5]
-    in_out, out_out, up_out, down_out, vec_out = refs[13:]
+    last = refs[4]
+    in_out, out_out, up_out, down_out, vec_out = refs[17:]
     i = lax.rem(scal[2], 2)
-    upper = total([keep_bc[i], got_bc[i], last[0:192]])
-    a1 = total([keep_a[i], got_a[i], last[192:]])
-    lower = total([r[...] for r in refs[5:9]])
-    rows_a = total([r[...] for r in refs[9:13]])
+    b1, c1 = (total([refs[2 * k][i], refs[2 * k + 1][i], last[96 * k : 96 * k + 96]]) for k in range(2))
+    both = total([r[...] for r in refs[5:9]])
+    b0 = total([r[...] for r in refs[9:13]])
+    rows_a = total([r[...] for r in refs[13:17]])
     vec_out[0:VROWS] = rows_a[48:64]
     vec_out[VROWS:] = rows_a[112:128]
     a0 = jnp.concatenate([rows_a[:48], rows_a[64:112]], axis=0)
-    for l, a, bc in ((0, a0, lower), (1, a1, upper)):
+    for l, a, b, c in ((0, a0, b0, both[96:]), (1, both[:96], b1, c1)):
         in_out[l] = a[:, :576]
         out_out[l] = a[:, 576:]
-        up_out[l, 0:48] = bc[0:48]
-        up_out[l, 48:96] = bc[96:144]
-        c = jnp.concatenate([bc[48:96], bc[144:192]], axis=0)
+        up_out[l] = b
         for j in range(2):
             down_out[l, :, 96 * j : 96 * j + 96] = c[:, 384 * j : 384 * j + 384].T
 
@@ -786,6 +1076,7 @@
         (scal, *parts),
         cost_estimate=cost(0, 8e6),
         name="finish",
+        mib=64,
     )
 
 
@@ -796,26 +1087,18 @@
     def z_all(self, pack):
         self.parts = [pack] + [self.ring.z(pack, k) for k in (1, 2, 3)]
 
-    def xy_first(self):
-        h1, h2 = zcat(self.seq, self.scal, self.parts, self.parts[0].shape[0] // 2)
+    def xy_first(self, *riders):
+        h1, h2, *rest = zcat(self.seq, self.scal, self.parts, self.parts[0].shape[0] // 2, *riders)
         self.both = h1, self.ring.x(h1), h2, self.ring.y(h2)
-
-    def xy_second(self, both, first, rows):
-        self.h1, self.h2 = pile(self.seq, first, rows, both)
+        return rest[0] if riders else None
+
+    def xy_second(self, h1, h2):
+        self.h1, self.h2 = h1, h2
         self.y1, self.x2 = self.ring.y(self.h1), self.ring.x(self.h2)
 
     def core(self):
         both = self.ring.c(merge(self.seq, self.h1, self.y1, self.h2, self.x2))
         self.other = [(both, i) for i in range(4)]
-        return both
-
-    def core_own(self):
-        self.own = self.ring.c(self.h1), self.ring.c(self.h2)
-        return self.own
-
-    def core_got(self):
-        both = self.ring.c(merge(self.seq, self.y1, self.x2))
-        self.other = [self.own[0], (both, 0), self.own[1], (both, 1)]
         return both
 
     def pieces(self):
@@ -878,28 +1161,21 @@
                 self.block(sums, outs[k], lambda first, n, i=i: lambda scal: (i, pl.ds(first, n)), z)
         return outs
 
-    def third_direct(self, sums):
-        outs = [sums.out(2 * self.rows) for _ in range(4)]
-        for k in (1, 2, 3, 0):
-            self.block(sums, outs[k], rows_at, lambda scal, k=k: lax.rem(scal[2] + k, 4))
-        return outs
+
+def third_direct(sums, *chunks):
+    outs = [sums.out(sum(2 * c.rows for c in chunks)) for _ in range(4)]
+    for k in (1, 2, 3, 0):
+        at = 0
+        for c in chunks:
+            c.block(sums, outs[k], lambda first, n, at=at: rows_at(at + first, n), lambda scal, k=k: lax.rem(scal[2] + k, 4))
+            at += 2 * c.rows
+    return outs
 
 
 def fourth(sums, out, at, keep, got):
     rows = keep.shape[1]
     where = lambda scal: (1 - lax.rem(scal[2], 2),)
     sums.add(out, rows_at(at, rows), [(keep, where, False), (got, where, False)], rows)
-
-
-def unpack_vec(rows):
-    rows = rows.astype(F32)
-    vecs, hids = [], []
-    for l in range(LAYERS):
-        v = rows[:, :, 96 * l : 96 * l + 96].transpose(1, 0, 2).reshape(VROWS, D)
-        h = rows[:, :, 384 * l : 384 * l + 384].transpose(1, 0, 2).reshape(VROWS, FF)
-        vecs.append(v)
-        hids.append(h)
-    return vecs, hids
 
 
 def proj_bias(vec):
@@ -917,119 +1193,139 @@
     place = jnp.stack([dpi // ring.X, xme, fi // 2, fi % 2]).astype(jnp.int32)
     scal = jnp.concatenate([lengths[0], place, jnp.zeros((2,), jnp.int32)])
 
-    a, b, c, d, e = (Gather(seq, ring, scal) for _ in range(5))
+    a, b, c, d = (Gather(seq, ring, scal) for _ in range(4))
     a.z_all(pack_a(seq, 0, in_projection, out_projection))
-    cd = pack_all(seq, 1, (in_projection, out_projection, up_weight, down_weight))
+    q1, q2 = pack_c(seq, 1, down_weight)
+    q1, q2 = join(seq, q1, ring.x(q1), q2, ring.y(q2))
+    q1_got, q2_got = ring.y(q1), ring.x(q2)
+    seq.hold(q1_got, q2_got)
     a.xy_first()
     b.z_all(pack_vec(seq, up_weight, down_weight, (norm_gains, biases, hidden_gains, hidden_biases)))
+    cd = pack_ab(seq, 1, (in_projection, out_projection, up_weight))
     seq.hold(b.parts[1])
-    a.xy_second(a.both, 0, 48)
+    a.xy_second(*pile(seq, scal, a.both, ((0, 48),)))
     seq.hold(a.y1, a.x2)
     b.xy_first()
     c.z_all(cd)
+    q = merge(seq, q1, q1_got, q2, q2_got)
     seq.hold(a.core(), c.parts[3])
-    b.xy_second(b.both, 0, 112)
-    rows = b.h1[:, :, 96:112]
-    rows = jnp.where(xme == 0, rows, rows[::-1]).transpose(1, 0, 2, 3).reshape(8, VROWS, D)
-    vecs, hids = unpack_vec(rows)
-    pb = [proj_bias(v) for v in vecs]
+    h, own, vecs, hids, pb = pile_vec(seq, scal, b.both)
+    b.xy_second(*h)
+    b.own = ring.c(own)
     kept = [None, None]
     x = inputs
     x1, a1, un, p, o, a2 = call_attn_fwd(seq, plan, scal, x, vecs[0], pb[0], a.pieces(), 0)
-    seq.hold(b.y1, b.x2, *b.core_own())
-    c.xy_first()
-    c.xy_second(c.both, 0, 48)
-    d.xy_second(c.both, 48, 48)
-    e.xy_second(c.both, 96, 48)
-    b.core_got()
-    x2, a3, sl, n4, a4 = call_ff_fwd(seq, plan, scal, x1, vecs[0], hids[0], b.pieces(), 0, 1, False)
+    seq.hold(b.y1, b.x2, b.own)
+    rest = ring.c(c.xy_first(b.y1, b.x2))
+    b.other = [(b.own, 0), (rest, 0), (b.own, 1), (rest, 1)]
+    seq.hold(rest)
+    h = pile(seq, scal, c.both, ((0, 48), (48, 48)), (q, ring.z_xor(q, 1)))
+    c.xy_second(*h[:2])
+    d.xy_second(*h[2:4])
+    parts_q = h[4:]
+    got_q = [ring.z_xor(v, 2) for v in parts_q]
+    x2, a3, sl, n4, a4 = call_ff_fwd(seq, plan, scal, x1, vecs[0], hids[0], b.pieces(), 0, 1)
     kept[0] = (x, x1, a1, un, p, o, a2, a3, sl, n4, a4)
     x = x2
-    seq.hold(d.y1, d.x2)
+    seq.hold(d.y1, d.x2, got_q[0])
     c.core()
     d.core()
     x1, a1, un, p, o, a2 = call_attn_fwd(seq, plan, scal, x, vecs[1], pb[1], c.pieces(), 0)
-    e.core_own()
-    e.core_got()
-    outputs, a3, sl, n4, a4 = call_ff_fwd(seq, plan, scal, x1, vecs[1], hids[1], d.pieces() + e.pieces(), 0, 0, True)
-
-    (dx1, gva1, gh1), grads = call_ff_bwd(seq, plan, scal, cotangent, x1, a3, sl, n4, a4, vecs[1], hids[1], d.pieces() + e.pieces(), 0, 0, True)
-    s1 = Scatter(ring, grads)
-    s1.core(s1.send)
+    q1 = zquad(seq, scal, parts_q[0], got_q[0])
+    (a3, sl, n4, a4), grads = call_ff_mid(seq, plan, scal, x1, cotangent, vecs[1], hids[1], d.pieces(), 0)
+    q2 = zquad(seq, scal, parts_q[1], got_q[1], parts_q[2], got_q[2])
+    pieces_c = [(v, i) for v in (q1, ring.c(q1), q2, ring.c(q2)) for i in range(2)]
+
+    sc = Scatter(ring, grads)
+    sc.core(sc.send)
+    pieces = d.pieces() + pieces_c
+    (dx1, gva1, gh1), grads = call_ff_bwd(seq, plan, scal, cotangent, x1, a3, sl, n4, a4, vecs[1], hids[1], pieces, 0, 0, True, False)
+    sb = Scatter(ring, grads)
+
+    sums = Sums(scal)
+    sc.first(sums, sums.out(384), sums.out(384))
+    seq.carry(sb.send)
+    u, v = sums.run(seq, "sums_1")
+    sb.core(*seq.carried)
+    sc.x1st, sc.y1st = ring.x(u), ring.y(v)
+
+    x1_last, a4_last = x1, a4
     (dy, gvb1), grads = call_attn_bwd(seq, plan, scal, dx1, x, a1, un, p, o, a2, vecs[1], c.pieces(), 0, ())
-    s2 = Scatter(ring, grads)
+    sa = Scatter(ring, grads)
+
+    sums = Sums(scal)
+    outs = sums.out(576), sums.out(576)
+    sc.second(sums, *outs)
+    sb.first(sums, *outs, 192)
+    seq.carry(sa.send)
+    u, v = sums.run(seq, "sums_2")
+    sa.core(*seq.carried)
+    sb.x1st, sb.y1st = sc.x2nd, sc.y2nd = ring.x(u), ring.y(v)
+
+    x, x1, a1, un, p, o, a2, a3, sl, n4, a4 = kept[0]
+    s3 = Scatter(ring, call_down_grad(seq, plan, scal, dy, a4))
+    s3.core(s3.send)
+    (dx1, gva0, gh0), grads = call_ff_bwd(seq, plan, scal, dy, x1, a3, sl, n4, a4, vecs[0], hids[0], b.pieces(), 0, 1, False, False)
+    s4 = Scatter(ring, grads)
+
+    sums = Sums(scal)
+    outs = sums.out(960), sums.out(960)
+    sb.second(sums, *outs)
+    sa.first(sums, *outs, 192)
+    s3.first(sums, *outs, 576)
+    sc.third_pair(sums)
+    seq.carry(s4.send)
+    u, v, keep_c, send = sums.run(seq, "sums_3")
+    s4.core(*seq.carried)
+    sa.x1st, sa.y1st = sb.x2nd, sb.y2nd = s3.x1st, s3.y1st = ring.x(u), ring.y(v)
+    got_c = ring.z_xor(send, 2)
+
+    others = (gva0, gva1, gvb1, gh0, gh1)
+    (input_gradient, _), grads = call_attn_bwd(seq, plan, scal, dx1, x, a1, un, p, o, a2, vecs[0], a.pieces(), 0, others)
+    s5 = Scatter(ring, grads)
 
     sums = Sums(scal)
     outs = sums.out(768), sums.out(768)
-    s1.first(sums, *outs)
-    seq.carry(s2.send)
-    u, v = sums.run(seq, "sums_1")
-    s2.core(*seq.carried)
-    s1.x1st, s1.y1st = ring.x(u), ring.y(v)
-
-    x, x1, a1, un, p, o, a2, a3, sl, n4, a4 = kept[0]
-    (dx1, gva0, gh0), grads = call_ff_bwd(seq, plan, scal, dy, x1, a3, sl, n4, a4, vecs[0], hids[0], b.pieces(), 0, 1, False)
-    s3 = Scatter(ring, grads)
+    sa.second(sums, *outs)
+    s3.second(sums, *outs, 192)
+    s4.first(sums, *outs, 384)
+    sb.third_pair(sums)
+    seq.hold(got_c)
+    seq.carry(s5.send)
+    u, v, keep_b, send = sums.run(seq, "sums_4")
+    s5.core(*seq.carried)
+    s4.x1st, s4.y1st = sa.x2nd, sa.y2nd = s3.x2nd, s3.y2nd = ring.x(u), ring.y(v)
+    got_b = ring.z_xor(send, 2)
+    outputs = call_ff_out(seq, plan, scal, x1_last, a4_last, vecs[1], pieces, 0)
 
     sums = Sums(scal)
-    outs = sums.out(768), sums.out(768)
-    s2.first(sums, *outs)
-    s1.second(sums, *outs, 384)
-    seq.carry(s3.send)
-    u, v = sums.run(seq, "sums_2")
-    s3.core(*seq.carried)
-    s2.x1st, s2.y1st = s1.x2nd, s1.y2nd = ring.x(u), ring.y(v)
-
-    others = (gva0, gva1, gvb1, gh0, gh1)
-    (input_gradient, _), grads = call_attn_bwd(seq, plan, scal, dx1, x, a1, un, p, o, a2, vecs[0], a.pieces(), 0, others)
-    s4 = Scatter(ring, grads)
+    outs = sums.out(704), sums.out(704)
+    s4.second(sums, *outs)
+    s5.first(sums, *outs, 192)
+    third_direct(sums, sa, s3)
+    seq.hold(got_b)
+    u, v, *res = sums.run(seq, "sums_5")
+    s4.x2nd, s4.y2nd = s5.x1st, s5.y1st = ring.x(u), ring.y(v)
+    parts1 = [res[0]] + [ring.z(res[k], k) for k in (1, 2, 3)]
 
     sums = Sums(scal)
-    outs = sums.out(960), sums.out(960)
-    s2.second(sums, *outs)
-    s3.first(sums, *outs, 192)
-    s1.third_pair(sums)
-    seq.carry(s4.send)
-    u, v, keep1, send1 = sums.run(seq, "sums_3")
-    s4.core(*seq.carried)
-    s3.x1st, s3.y1st = s2.x2nd, s2.y2nd = ring.x(u), ring.y(v)
-    got1 = ring.z_xor(send1, 2)
+    s5.second(sums, sums.out(256), sums.out(256))
+    third_direct(sums, s4)
+    seq.hold(*parts1[1:])
+    u, v, *res = sums.run(seq, "sums_6")
+    s5.x2nd, s5.y2nd = ring.x(u), ring.y(v)
+    parts2 = [res[0]] + [ring.z(res[k], k) for k in (1, 2, 3)]
 
     sums = Sums(scal)
-    outs = sums.out(384), sums.out(384)
-    s3.second(sums, *outs)
-    s2.third_pair(sums)
-    seq.hold(got1)
-    u, v, keep2, send2 = sums.run(seq, "sums_4")
-    s3.x2nd, s3.y2nd = ring.x(u), ring.y(v)
-    got2 = ring.z_xor(send2, 2)
-
-    sums = Sums(scal)
-    s3.third_direct(sums)
-    outs = sums.out(512), sums.out(512)
-    s4.first(sums, *outs)
-    seq.hold(got2)
-    *parts3, u, v = sums.run(seq, "sums_5")
-    parts3 = parts3[:1] + [ring.z(parts3[k], k) for k in (1, 2, 3)]
-    s4.x1st, s4.y1st = ring.x(u), ring.y(v)
-
-    sums = Sums(scal)
-    outs = sums.out(256), sums.out(256)
-    s4.second(sums, *outs)
-    seq.hold(*parts3[1:3])
-    u, v = sums.run(seq, "sums_6")
-    s4.x2nd, s4.y2nd = ring.x(u), ring.y(v)
-
-    sums = Sums(scal)
-    s4.third_direct(sums)
-    out = sums.out(288)
-    fourth(sums, out, 0, keep1, got1)
-    fourth(sums, out, 192, keep2, got2)
-    seq.hold(parts3[3])
+    third_direct(sums, s5)
+    out = sums.out(192)
+    fourth(sums, out, 0, keep_b, got_b)
+    fourth(sums, out, 96, keep_c, got_c)
+    seq.hold(*parts2[1:])
     res = sums.run(seq, "sums_7")
-    parts4 = [res[0]] + [ring.z(res[k], k) for k in (1, 2, 3)]
+    parts3 = [res[0]] + [ring.z(res[k], k) for k in (1, 2, 3)]
     last = ring.z_xor(res[4], 1)
-    g_in, g_out, g_up, g_down, vrows = finish(seq, scal, [keep1, got1, keep2, got2, last, *parts3, *parts4])
+    g_in, g_out, g_up, g_down, vrows = finish(seq, scal, [keep_b, got_b, keep_c, got_c, last, *parts1, *parts2, *parts3])
     gv = jnp.stack([vrows[:10, :96], vrows[:10, 96:192]])
     gh = jnp.stack([vrows[26:29, :384], vrows[26:29, 384:]])
     return outputs, input_gradient, g_in, g_out, g_up, g_down, gv[:, :3], gv[:, 3:], gh[:, :1], gh[:, 1:]
@@ -1064,16 +1360,17 @@
     kept = []
     for l in range(LAYERS):
         x1, a1, un, p, o, a2 = call_attn_fwd(seq, plan, scal, x, vecs[l], pb[l], pieces[l], 0)
-        x2, a3, sl, n4, a4 = call_ff_fwd(seq, plan, scal, x1, vecs[l], hids[l], pieces[l], 0, 0, l == LAYERS - 1)
+        x2, a3, sl, n4, a4 = call_ff_fwd(seq, plan, scal, x1, vecs[l], hids[l], pieces[l], 0, 0)
         kept.append((x, x1, a1, un, p, o, a2, a3, sl, n4, a4))
         x = x2
-    outputs = x
+    places = jnp.arange(inputs.shape[0], dtype=jnp.int32)[:, None]
+    outputs = x * (seg_of(scal, places) < SEQS).astype(F32)
     dy = cotangent
     layer_grads = [None] * LAYERS
     for l in reversed(range(LAYERS)):
         x, x1, a1, un, p, o, a2, a3, sl, n4, a4 = kept[l]
         last = l == LAYERS - 1
-        (dx1, gva, gh), (gb, gc) = call_ff_bwd(seq, plan, scal, dy, x1, a3, sl, n4, a4, vecs[l], hids[l], pieces[l], 0, 0, last)
+        (dx1, gva, gh), (gb, gc) = call_ff_bwd(seq, plan, scal, dy, x1, a3, sl, n4, a4, vecs[l], hids[l], pieces[l], 0, 0, last, True)
         (dy, gvb), (ga,) = call_attn_bwd(seq, plan, scal, dx1, x, a1, un, p, o, a2, vecs[l], pieces[l], 0, ())
         layer_grads[l] = (ga, gb, gc, gva + gvb, gh)
 

time: 490 us -> 470 us (0.959)
  waiting for transfers between devices: 219 us -> 186 us
  starting transfers between devices: 48.4 us -> 73.7 us
  local copies, waits for them, and re-layouts: 34.9 us -> 21 us
    ppermute x14 -> x15, waiting for transfers between devices: 48.2 us -> 10.4 us  [x(): return lax.ppermute(v, 'dp', [(i, i ^ 1) for i in range(self.dp)])]
    ppermute x14 -> x15, waiting for transfers between devices: 23.3 us -> 52.7 us  [y(): return lax.ppermute(v, 'fsdp', [(i, i ^ 2) for i in range(self.fsdp)])]
    ppermute x15 -> x18, starting transfers between devices: 19.2 us -> 31.8 us  [z(): lax.ppermute(v, 'dp', [(z * self.X + x, (z + k) % self.Z * self.X + x) fo...]
    ppermute x3 -> x7, waiting for transfers between devices: 44.2 us -> 31.9 us  [z_xor(): return lax.ppermute(v, 'dp', [(i, i ^ k * self.X) for i in range(self.dp)])]
    ppermute x3 -> x7, starting transfers between devices: 0.08 us -> 10.8 us  [z_xor(): return lax.ppermute(v, 'dp', [(i, i ^ k * self.X) for i in range(self.dp)])]
    unnamed x86 -> x61, local copies, waits for them, and re-layouts: 29.2 us -> 18.7 us
    ppermute x13, waiting for transfers between devices: 13.1 us -> 5.3 us  [c(): return lax.ppermute(v, 'fsdp', [(i, i ^ 1) for i in range(self.fsdp)])]
    ppermute x15 -> x18, waiting for transfers between devices: 90.3 us -> 85.5 us  [z(): lax.ppermute(v, 'dp', [(z * self.X + x, (z + k) % self.Z * self.X + x) fo...]
  transfers between devices with their start and end apart: 59 -> 68, of which waited for: 37 -> 33; matrix products, arithmetic and copies ran while one was open for 2% -> 1% of each run, Pallas kernels for 20% -> 27%
where the time goes in v3:
time: 470 us; the launch traced here: 461 us
  waiting for transfers between devices  186 us (40%)
  Pallas kernels  178 us (38%)
  starting transfers between devices  73.7 us (16%)
  local copies, waits for them, and re-layouts  21 us (4%)
    pallas_call x35, Pallas kernels, __call__(): pl.pallas_call(body, out_shape=tuple(out_shape) + tuple((S(v.shape, v.dty...  178 us
    ppermute x18, waiting for transfers between devices, z(): lax.ppermute(v, 'dp', [(z * self.X + x, (z + k) % self.Z * self.X + x) fo...  85.5 us
    ppermute x15, waiting for transfers between devices, y(): return lax.ppermute(v, 'fsdp', [(i, i ^ 2) for i in range(self.fsdp)])  52.7 us
    ppermute x7, waiting for transfers between devices, z_xor(): return lax.ppermute(v, 'dp', [(i, i ^ k * self.X) for i in range(self.dp)])  31.9 us
    ppermute x18, starting transfers between devices, z(): lax.ppermute(v, 'dp', [(z * self.X + x, (z + k) % self.Z * self.X + x) fo...  31.8 us
    unnamed x61, local copies, waits for them, and re-layouts  18.7 us
    ppermute x15, starting transfers between devices, x(): return lax.ppermute(v, 'dp', [(i, i ^ 1) for i in range(self.dp)])  14.8 us
    ppermute x15, starting transfers between devices, y(): return lax.ppermute(v, 'fsdp', [(i, i ^ 2) for i in range(self.fsdp)])  14 us
  transfers between devices with their start and end apart: 68, of which 33 were waited for; matrix products, arithmetic and copies ran while one was open for 1% of the time, Pallas kernels for 27%

profile of v3, /device:TPU:0, one launch (start us, length us, event | category | flops | bytes accessed | tf_op | source)
XLA Modules:
  0.0 461.0 jit_solution(13329898866233498511)
XLA Ops:
  17.0 7.1 %collective-permute-done.1.refs_3_ = bf16[96,768]{1,0:T(8,128)(2,1)S(1)} collective-permute-done((bf16[96,768]{1,0:T(8,128)(2,1)S(1)}, bf16[96,768]{1,0:T(8,128)(2,1)S(1)}, u32[]{:S(2)}, u32[]{:S(2)}) %collective-permute-start.1) | collective-permute-done | bytes 147488 | tf_op jit(solution)/shard_map/ppermute | solution.py:739
  26.7 6.7 %collective-permute-done.11.refs_4_ = bf16[4,48,768]{2,1,0:T(8,128)(2,1)S(1)} collective-permute-done((bf16[4,48,768]{2,1,0:T(8,128)(2,1)S(1)}, bf16[4,48,768]{2,1,0:T(8,128)(2,1)S(1)}, u32[]{:S(2)}, u32[]{:S(2)}) %collective-permute-start.11) | collective-permute-done | bytes 294944 | tf_op jit(solution)/shard_map/ppermute | solution.py:748
  40.4 8.0 %collective-permute-done.9.refs_4_ = bf16[224,768]{1,0:T(8,128)(2,1)S(1)} collective-permute-done((bf16[224,768]{1,0:T(8,128)(2,1)S(1)}, bf16[224,768]{1,0:T(8,128)(2,1)S(1)}, u32[]{:S(2)}, u32[]{:S(2)}) %collective-permute-start.9) | collective-permute-done | bytes 344096 | tf_op jit(solution)/shard_map/ppermute | solution.py:739
  48.4 11.9 %collective-permute-done.8.refs_3_ = bf16[224,768]{1,0:T(8,128)(2,1)S(1)} collective-permute-done((bf16[224,768]{1,0:T(8,128)(2,1)S(1)}, bf16[224,768]{1,0:T(8,128)(2,1)S(1)}, u32[]{:S(2)}, u32[]{:S(2)}) %collective-permute-start.8) | collective-permute-done | bytes 344096 | tf_op jit(solution)/shard_map/ppermute | solution.py:739
  69.3 6.4 %collective-permute-done.17.refs_7_.refs_4_ = bf16[192,768]{1,0:T(8,128)(2,1)S(1)} collective-permute-done((bf16[192,768]{1,0:T(8,128)(2,1)S(1)}, bf16[192,768]{1,0:T(8,128)(2,1)S(1)}, u32[]{:S(2)}, u32[]{:S(2)}) %collective-permute-start.17) | collective-permute-done | bytes 294944 | tf_op jit(solution)/shard_map/ppermute | solution.py:739
  75.6 5.8 %collective-permute-done.15.refs_4_ = bf16[4,112,768]{2,1,0:T(8,128)(2,1)S(1)} collective-permute-done((bf16[4,112,768]{2,1,0:T(8,128)(2,1)S(1)}, bf16[4,112,768]{2,1,0:T(8,128)(2,1)S(1)}, u32[]{:S(2)}, u32[]{:S(2)}) %collective-permute-start.15) | collective-permute-done | bytes 688160 | tf_op jit(solution)/shard_map/ppermute | solution.py:748
  94.0 9.7 %attn_fwd.2 = (f32[256,768]{1,0:T(8,128)}, bf16[256,768]{1,0:T(8,128)(2,1)}, bf16[36,256,64]{2,1,0:T(8,128)(2,1)}, f32[12,256,256]{2,1,0:T(8,128)}, f32[256,768]{1,0:T(8,128)}, /*index=5*/bf16[256,768]{1,0:T(8,128)(2,1)}) custom-call(s32[8]{0:T(128)} %copy-done.21, f32[256,768]{1,0:T(8,128)} %refs_2_.6, ...), custom_call_target="tpu_custom_call" | custom-call | flops 7247757312 | bytes 12718592 | tf_op jit(solution)/shard_map/attn_fwd/pallas_call | solution.py:582
  103.7 9.0 %collective-permute-done.21.refs_3_ = bf16[192,768]{1,0:T(8,128)(2,1)} collective-permute-done((bf16[192,768]{1,0:T(8,128)(2,1)}, bf16[192,768]{1,0:T(8,128)(2,1)}, u32[]{:S(2)}, u32[]{:S(2)}) %collective-permute-start.21) | collective-permute-done | bytes 294944 | tf_op jit(solution)/shard_map/ppermute | solution.py:739
  112.7 7.8 %collective-permute-done.22.refs_6_.refs_9_.refs_14_ = bf16[2,4,112,768]{3,2,1,0:T(8,128)(2,1)} collective-permute-done((bf16[2,4,112,768]{3,2,1,0:T(8,128)(2,1)}, bf16[2,4,112,768]{3,2,1,0:T(8,128)(2,1)}, u32[]{:S(2)}, u32[]{:S(2)}) %collective-permute-start.22) | collective-permute-done | bytes 1376288 | tf_op jit(solution)/shard_map/ppermute | solution.py:745
  129.8 13.8 %collective-permute-done.26.refs_6_ = bf16[4,2,48,768]{3,2,1,0:T(8,128)(2,1)S(1)} collective-permute-done((bf16[4,2,48,768]{3,2,1,0:T(8,128)(2,1)S(1)}, bf16[4,2,48,768]{3,2,1,0:T(8,128)(2,1)S(1)}, u32[]{:S(2)}, u32[]{:S(2)}) %collective-permute-start.26) | collective-permute-done | bytes 589856 | tf_op jit(solution)/shard_map/ppermute | solution.py:742
  154.0 12.8 %ff_fwd.1 = (f32[256,768]{1,0:T(8,128)}, bf16[256,768]{1,0:T(8,128)(2,1)}, f32[256,3072]{1,0:T(8,128)}, f32[256,3072]{1,0:T(8,128)}, bf16[256,3072]{1,0:T(8,128)(2,1)}) custom-call(s32[8]{0:T(128)} %copy-done.21, f32[256,768]{1,0:T(8,128)} %get-tuple-element.132.refs_7_.refs_1_.refs_2_, f32[16,768]{1,0:T(8,128)} %get-tuple-element.129.refs_2_.refs_7_.refs_8_, ...), custom_call_target="tpu_custom_call" | custom-call | flops 7247757312 | bytes 17437184 | tf_op jit(solution)/shard_map/ff_fwd/pallas_call | solution.py:582
  166.8 8.7 %collective-permute-done.31.refs_7_.refs_2_ = bf16[2,2,2,48,768]{4,3,2,1,0:T(8,128)(2,1)} collective-permute-done((bf16[2,2,2,48,768]{4,3,2,1,0:T(8,128)(2,1)}, bf16[2,2,2,48,768]{4,3,2,1,0:T(8,128)(2,1)}, u32[]{:S(2)}, u32[]{:S(2)}) %collective-permute-start.31) | collective-permute-done | bytes 589856 | tf_op jit(solution)/shard_map/ppermute | solution.py:742
  189.2 9.8 %attn_fwd.3 = (f32[256,768]{1,0:T(8,128)}, bf16[256,768]{1,0:T(8,128)(2,1)}, bf16[36,256,64]{2,1,0:T(8,128)(2,1)}, f32[12,256,256]{2,1,0:T(8,128)}, f32[256,768]{1,0:T(8,128)}, /*index=5*/bf16[256,768]{1,0:T(8,128)(2,1)}) custom-call(s32[8]{0:T(128)} %copy-done.21, f32[256,768]{1,0:T(8,128)} %get-tuple-element.140.refs_4_.refs_1_.refs_2_, ...), custom_call_target="tpu_custom_call" | custom-call | flops 7247757312 | bytes 12718592 | tf_op jit(solution)/shard_map/attn_fwd/pallas_call | solution.py:582
  201.4 13.4 %ff_mid.1 = (bf16[256,768]{1,0:T(8,128)(2,1)}, f32[256,3072]{1,0:T(8,128)}, f32[256,3072]{1,0:T(8,128)}, bf16[256,3072]{1,0:T(8,128)(2,1)}, bf16[2,2,2,4,48,768]...) custom-call(s32[8]{0:T(128)} %copy-done.21, f32[256,768]{1,0:T(8,128)} %get-tuple-element.147.refs_3_.refs_1_.refs_2_, ...), custom_call_target="tpu_custom_call" | custom-call | flops 7247757312 | bytes 17437184 | tf_op jit(solution)/shard_map/ff_mid/pallas_call | solution.py:582
  223.1 13.9 %ff_bwd.2 = (f32[256,768]{1,0:T(8,128)}, f32[16,768]{1,0:T(8,128)}, f32[16,3072]{1,0:T(8,128)}, bf16[2,2,2,4,48,768]{5,4,3,2,1,0:T(8,128)(2,1)}, bf16[2,2,2,4,48,768]{5,4,3,2,1,0:T(8,128)(2,1)}) custom-call(s32[8]{0:T(128)} %copy-done.21, f32[256,768]{1,0:T(8,128)} %refs_1_.8, f32[256,768]{1,0:T(8,128)} %get-tuple-element.147.refs_3_.refs_1_.refs_2_, ...), custom_call_target="tpu_custom_call" | custom-call | flops 9663676416 | bytes 26874368 | tf_op jit(solution)/shard_map/ff_bwd/pallas_call | solution.py:582
  242.1 15.8 %attn_bwd.2 = (f32[256,768]{1,0:T(8,128)}, f32[16,768]{1,0:T(8,128)}, bf16[2,2,2,4,48,768]{5,4,3,2,1,0:T(8,128)(2,1)}, bf16[2,2,2,4,48,768]{5,4,3,2,1,0:T(8,128)(2,1)}) custom-call(s32[8]{0:T(128)} %copy-done.21, f32[256,768]{1,0:T(8,128)} %get-tuple-element.155.refs_3_.refs_1_, f32[256,768]{1,0:T(8,128)} %get-tuple-element.140.refs_4_.refs_1_.refs_2_, ...), custom_call_target="tpu_custom_call" | custom-call | flops 9663676416 | bytes 17437184 | tf_op jit(solution)/shard_map/attn_bwd/pallas_call | solution.py:582
  261.8 6.2 %ff_down_grad.1 = (bf16[2,2,2,4,48,768]{5,4,3,2,1,0:T(8,128)(2,1)}, bf16[2,2,2,4,48,768]{5,4,3,2,1,0:T(8,128)(2,1)}) custom-call(s32[8]{0:T(128)} %copy-done.21, f32[256,768]{1,0:T(8,128)} %get-tuple-element.169.refs_7_.refs_1_, bf16[256,3072]{1,0:T(8,128)(2,1)} %get-tuple-element.174.refs_2_.refs_6_, bf16[576,768]{1,0:T(8,128)(2,1)} %get-tuple-element.172.refs_3_), custom_call_target="tpu_custom_call" | custom-call | flops 1207959552 | bytes 7718592 | tf_op jit(solution)/shard_map/ff_down_grad/pallas_call | solution.py:582
  270.8 13.4 %ff_bwd.3 = (f32[256,768]{1,0:T(8,128)}, f32[16,768]{1,0:T(8,128)}, f32[16,3072]{1,0:T(8,128)}, bf16[2,2,2,4,48,768]{5,4,3,2,1,0:T(8,128)(2,1)}, bf16[2,2,2,4,48,768]{5,4,3,2,1,0:T(8,128)(2,1)}) custom-call(s32[8]{0:T(128)} %copy-done.21, f32[256,768]{1,0:T(8,128)} %get-tuple-element.169.refs_7_.refs_1_, ...), custom_call_target="tpu_custom_call" | custom-call | flops 9663676416 | bytes 26874368 | tf_op jit(solution)/shard_map/ff_bwd/pallas_call | solution.py:582
  284.2 7.4 %collective-permute-done.44.refs_4_.refs_12_ = bf16[576,768]{1,0:T(8,128)(2,1)} collective-permute-done((bf16[576,768]{1,0:T(8,128)(2,1)}, bf16[576,768]{1,0:T(8,128)(2,1)}, u32[]{:S(2)}, u32[]{:S(2)}) %collective-permute-start.44) | collective-permute-done | bytes 884768 | tf_op jit(solution)/shard_map/ppermute | solution.py:748
  291.7 6.4 %sums_3.1 = (bf16[960,768]{1,0:T(8,128)(2,1)}, bf16[960,768]{1,0:T(8,128)(2,1)}, bf16[2,96,768]{2,1,0:T(8,128)(2,1)}, bf16[2,96,768]{2,1,0:T(8,128)(2,1)}, bf16[2,2,2,4,48,768]{5,4,3,2,1,0:T(8,128)(2,1)}) custom-call(s32[8]{0:T(128)} %copy-done.21, ...), custom_call_target="tpu_custom_call", output_to_operand_aliasing={{4}: (14, {})} | custom-call | bytes 12386304 | tf_op jit(solution)/shard_map/sums_3/pallas_call | solution.py:582
  300.0 16.3 %attn_bwd.3 = (f32[256,768]{1,0:T(8,128)}, f32[16,768]{1,0:T(8,128)}, bf16[2,2,2,4,64,768]{5,4,3,2,1,0:T(8,128)(2,1)}, bf16[2,2,2,4,64,768]{5,4,3,2,1,0:T(8,128)(2,1)}) custom-call(s32[8]{0:T(128)} %copy-done.21, f32[256,768]{1,0:T(8,128)} %get-tuple-element.180.refs_13_.refs_1_, f32[256,768]{1,0:T(8,128)} %refs_2_.6, ...), custom_call_target="tpu_custom_call" | custom-call | flops 9663676416 | bytes 17437184 | tf_op jit(solution)/shard_map/attn_bwd/pallas_call | solution.py:582
  316.4 16.8 %collective-permute-done.47.refs_4_.refs_10_ = bf16[960,768]{1,0:T(8,128)(2,1)} collective-permute-done((bf16[960,768]{1,0:T(8,128)(2,1)}, bf16[960,768]{1,0:T(8,128)(2,1)}, u32[]{:S(2)}, u32[]{:S(2)}) %collective-permute-start.47) | collective-permute-done | bytes 1474592 | tf_op jit(solution)/shard_map/ppermute | solution.py:748
  333.8 6.1 %sums_4.1 = (bf16[768,768]{1,0:T(8,128)(2,1)}, bf16[768,768]{1,0:T(8,128)(2,1)}, bf16[2,96,768]{2,1,0:T(8,128)(2,1)}, bf16[2,96,768]{2,1,0:T(8,128)(2,1)}, bf16[2,2,2,4,64,768]{5,4,3,2,1,0:T(8,128)(2,1)}) custom-call(s32[8]{0:T(128)} %copy-done.21, ...), custom_call_target="tpu_custom_call", output_to_operand_aliasing={{4}: (15, {})} | custom-call | bytes 11206656 | tf_op jit(solution)/shard_map/sums_4/pallas_call | solution.py:582
  342.1 6.5 %ff_out.1.refs_13_ = f32[256,768]{1,0:T(8,128)} custom-call(s32[8]{0:T(128)} %copy-done.21, f32[256,768]{1,0:T(8,128)} %get-tuple-element.147.refs_3_.refs_1_.refs_2_, bf16[256,3072]{1,0:T(8,128)(2,1)} %get-tuple-element.149.refs_6_.refs_2_, f32[16,768]{1,0:T(8,128)} %get-tuple-element.141.refs_2_.refs_3_.refs_7_.refs_8_, ...), custom_call_target="tpu_custom_call" | custom-call | flops 3623878656 | bytes 7718592 | tf_op jit(solution)/shard_map/ff_out/pallas_call | solution.py:582
  348.6 9.5 %collective-permute-done.50.refs_14_.refs_8_.refs_2_ = bf16[2,96,768]{2,1,0:T(8,128)(2,1)} collective-permute-done((bf16[2,96,768]{2,1,0:T(8,128)(2,1)}, bf16[2,96,768]{2,1,0:T(8,128)(2,1)}, u32[]{:S(2)}, u32[]{:S(2)}) %collective-permute-start.50) | collective-permute-done | bytes 294944 | tf_op jit(solution)/shard_map/ppermute | solution.py:742
  358.1 10.5 %collective-permute-done.53.refs_4_.refs_8_ = bf16[768,768]{1,0:T(8,128)(2,1)} collective-permute-done((bf16[768,768]{1,0:T(8,128)(2,1)}, bf16[768,768]{1,0:T(8,128)(2,1)}, u32[]{:S(2)}, u32[]{:S(2)}) %collective-permute-start.53) | collective-permute-done | bytes 1179680 | tf_op jit(solution)/shard_map/ppermute | solution.py:748
  369.5 6.9 %sums_5.1 = (bf16[704,768]{1,0:T(8,128)(2,1)}, bf16[704,768]{1,0:T(8,128)(2,1)}, bf16[192,768]{1,0:T(8,128)(2,1)}, bf16[192,768]{1,0:T(8,128)(2,1)}, bf16[192,768]{1,0:T(8,128)(2,1)}, /*index=5*/bf16[192,768]{1,0:T(8,128)(2,1)}) custom-call(s32[8]{0:T(128)} %copy-done.21, bf16[2,2,2,4,48,768]{5,4,3,2,1,0:T(8,128)(2,1)} %get-tuple-element.184.refs_7_.refs_1_.refs_5_, ...), custom_call_target="tpu_custom_call" | custom-call | bytes 12976128 | tf_op jit(solution)/shard_map/sums_5/pallas_call | solution.py:582
  381.8 8.3 %collective-permute-done.56.refs_10_.refs_7_ = bf16[192,768]{1,0:T(8,128)(2,1)} collective-permute-done((bf16[192,768]{1,0:T(8,128)(2,1)}, bf16[192,768]{1,0:T(8,128)(2,1)}, u32[]{:S(2)}, u32[]{:S(2)}) %collective-permute-start.56) | collective-permute-done | bytes 294944 | tf_op jit(solution)/shard_map/ppermute | solution.py:739
  390.1 10.5 %collective-permute-done.57.refs_11_.refs_8_ = bf16[192,768]{1,0:T(8,128)(2,1)} collective-permute-done((bf16[192,768]{1,0:T(8,128)(2,1)}, bf16[192,768]{1,0:T(8,128)(2,1)}, u32[]{:S(2)}, u32[]{:S(2)}) %collective-permute-start.57) | collective-permute-done | bytes 294944 | tf_op jit(solution)/shard_map/ppermute | solution.py:739
  408.5 5.0 %collective-permute-start.61 = (bf16[96,768]{1,0:T(8,128)(2,1)}, bf16[96,768]{1,0:T(8,128)(2,1)}, u32[]{:S(2)}, u32[]{:S(2)}) collective-permute-start(bf16[96,768]{1,0:T(8,128)(2,1)} %get-tuple-element.213), channel_id=1, source_target_pairs={{0,8},{4,12},{8,16},{12,20},{16,24},{20,28},{24,0},{28,4},{1,9},{5... | collective-permute-start | bytes 442376 | tf_op jit(solution)/shard_map/ppermute | solution.py:739
  418.0 4.8 %collective-permute-done.62.refs_13_.refs_12_ = bf16[96,768]{1,0:T(8,128)(2,1)} collective-permute-done((bf16[96,768]{1,0:T(8,128)(2,1)}, bf16[96,768]{1,0:T(8,128)(2,1)}, u32[]{:S(2)}, u32[]{:S(2)}) %collective-permute-start.62) | collective-permute-done | bytes 147488 | tf_op jit(solution)/shard_map/ppermute | solution.py:739
  435.8 9.0 %collective-permute-done.65.refs_15_ = bf16[128,768]{1,0:T(8,128)(2,1)} collective-permute-done((bf16[128,768]{1,0:T(8,128)(2,1)}, bf16[128,768]{1,0:T(8,128)(2,1)}, u32[]{:S(2)}, u32[]{:S(2)}) %collective-permute-start.65) | collective-permute-done | bytes 196640 | tf_op jit(solution)/shard_map/ppermute | solution.py:739
  (208 shorter events, 155.2 us)
Async XLA Ops:
  36.8 23.4 %collective-permute-start.13 = (bf16[2,4,48,768]{3,2,1,0:T(8,128)(2,1)S(1)}, bf16[2,4,48,768]{3,2,1,0:T(8,128)(2,1)S(1)}, u32[]{:S(2)}, u32[]{:S(2)}) collective-permute-start(bf16[2,4,48,768]{3,2,1,0:T(8,128)(2,1)S(1)} %get-tuple-element.126.refs_2_.refs_7_.refs_17_), channel_id=1, source_target_pairs={{0,4},{4,0},{8,12},{12,8},{16,20},{20,16},{24,28},{28,24},{1,5},{5... | collective-permute-start | bytes 1769480 | tf_op jit(solution)/shard_map/ppermute | solution.py:745
  37.4 22.9 %collective-permute-start.12 = (bf16[2,4,48,768]{3,2,1,0:T(8,128)(2,1)S(1)}, bf16[2,4,48,768]{3,2,1,0:T(8,128)(2,1)S(1)}, u32[]{:S(2)}, u32[]{:S(2)}) collective-permute-start(bf16[2,4,48,768]{3,2,1,0:T(8,128)(2,1)S(1)} %get-tuple-element.125.refs_5_.refs_0_.refs_4_.refs_14_), channel_id=1, source_target_pairs={{0,2},{1,3},{2,0},{3,1},{4,6},{5,7},{6,4},{7,5},{8,10},{9,11},{10,... | collective-permute-start | bytes 1769480 | tf_op jit(solution)/shard_map/ppermute | solution.py:748
  39.8 20.4 %collective-permute-start.8 = (bf16[224,768]{1,0:T(8,128)(2,1)S(1)}, bf16[224,768]{1,0:T(8,128)(2,1)S(1)}, u32[]{:S(2)}, u32[]{:S(2)}) collective-permute-start(bf16[224,768]{1,0:T(8,128)(2,1)S(1)} %pack_vec.1.refs_3_.refs_1_), channel_id=1, source_target_pairs={{0,16},{4,20},{8,24},{12,28},{16,0},{20,4},{24,8},{28,12},{1,17},{... | collective-permute-start | bytes 1032200 | tf_op jit(solution)/shard_map/ppermute | solution.py:739
  63.6 19.6 %collective-permute-start.16 = (bf16[4,2,4,48,768]{4,3,2,1,0:T(8,128)(2,1)S(1)}, bf16[4,2,4,48,768]{4,3,2,1,0:T(8,128)(2,1)}, u32[]{:S(2)}, u32[]{:S(2)}) collective-permute-start(bf16[4,2,4,48,768]{4,3,2,1,0:T(8,128)(2,1)S(1)} %merge.5.refs_5_), channel_id=1, source_target_pairs={{0,1},{1,0},{2,3},{3,2},{4,5},{5,4},{6,7},{7,6},{8,9},{9,8},{10,11... | collective-permute-start | bytes 7077896 | tf_op jit(solution)/shard_map/ppermute | solution.py:751
  87.7 34.1 %collective-permute-start.19 = (bf16[2,2,4,112,768]{4,3,2,1,0:T(8,128)(2,1)}, bf16[2,2,4,112,768]{4,3,2,1,0:T(8,128)(2,1)}, u32[]{:S(2)}, u32[]{:S(2)}) collective-permute-start(bf16[2,2,4,112,768]{4,3,2,1,0:T(8,128)(2,1)} %get-tuple-element.134), channel_id=1, source_target_pairs={{0,1},{1,0},{2,3},{3,2},{4,5},{5,4},{6,7},{7,6},{8,9},{9,8},{10,11... | collective-permute-start | bytes 8257544 | tf_op jit(solution)/shard_map/ppermute | solution.py:751
  87.7 32.9 %collective-permute-start.22 = (bf16[2,4,112,768]{3,2,1,0:T(8,128)(2,1)}, bf16[2,4,112,768]{3,2,1,0:T(8,128)(2,1)}, u32[]{:S(2)}, u32[]{:S(2)}) collective-permute-start(bf16[2,4,112,768]{3,2,1,0:T(8,128)(2,1)} %get-tuple-element.135.refs_8_.refs_13_), channel_id=1, source_target_pairs={{0,4},{4,0},{8,12},{12,8},{16,20},{20,16},{24,28},{28,24},{1,5},{5... | collective-permute-start | bytes 4128776 | tf_op jit(solution)/shard_map/ppermute | solution.py:745
  89.3 32.6 %collective-permute-start.18 = (bf16[2,4,112,768]{3,2,1,0:T(8,128)(2,1)}, bf16[2,4,112,768]{3,2,1,0:T(8,128)(2,1)}, u32[]{:S(2)}, u32[]{:S(2)}) collective-permute-start(bf16[2,4,112,768]{3,2,1,0:T(8,128)(2,1)} %get-tuple-element.131.refs_9_.refs_4_), channel_id=1, source_target_pairs={{0,2},{1,3},{2,0},{3,1},{4,6},{5,7},{6,4},{7,5},{8,10},{9,11},{10,... | collective-permute-start | bytes 4128776 | tf_op jit(solution)/shard_map/ppermute | solution.py:748
  90.1 22.6 %collective-permute-start.21 = (bf16[192,768]{1,0:T(8,128)(2,1)}, bf16[192,768]{1,0:T(8,128)(2,1)}, u32[]{:S(2)}, u32[]{:S(2)}) collective-permute-start(bf16[192,768]{1,0:T(8,128)(2,1)} %copy-done.5), channel_id=1, source_target_pairs={{0,16},{4,20},{8,24},{12,28},{16,0},{20,4},{24,8},{28,12},{1,17},{... | collective-permute-start | bytes 884744 | tf_op jit(solution)/shard_map/ppermute | solution.py:739
  90.1 22.6 %collective-permute-start.20 = (bf16[192,768]{1,0:T(8,128)(2,1)}, bf16[192,768]{1,0:T(8,128)(2,1)}, u32[]{:S(2)}, u32[]{:S(2)}) collective-permute-start(bf16[192,768]{1,0:T(8,128)(2,1)} %copy-done.5), channel_id=1, source_target_pairs={{0,8},{4,12},{8,16},{12,20},{16,24},{20,28},{24,0},{28,4},{1,9},{5... | collective-permute-start | bytes 884744 | tf_op jit(solution)/shard_map/ppermute | solution.py:739
  146.7 28.8 %collective-permute-start.31 = (bf16[2,2,2,48,768]{4,3,2,1,0:T(8,128)(2,1)}, bf16[2,2,2,48,768]{4,3,2,1,0:T(8,128)(2,1)}, u32[]{:S(2)}, u32[]{:S(2)}) collective-permute-start(bf16[2,2,2,48,768]{4,3,2,1,0:T(8,128)(2,1)} %get-tuple-element.146.refs_1_), channel_id=1, source_target_pairs={{0,16},{4,20},{8,24},{12,28},{16,0},{20,4},{24,8},{28,12},{1,17},{... | collective-permute-start | bytes 1769480 | tf_op jit(solution)/shard_map/ppermute | solution.py:742
  150.0 25.5 %collective-permute-start.28 = (bf16[2,4,48,768]{3,2,1,0:T(8,128)(2,1)}, bf16[2,4,48,768]{3,2,1,0:T(8,128)(2,1)}, u32[]{:S(2)}, u32[]{:S(2)}) collective-permute-start(bf16[2,4,48,768]{3,2,1,0:T(8,128)(2,1)} %get-tuple-element.143.refs_2_.refs_7_.refs_12_), channel_id=1, source_target_pairs={{0,4},{4,0},{8,12},{12,8},{16,20},{20,16},{24,28},{28,24},{1,5},{5... | collective-permute-start | bytes 1769480 | tf_op jit(solution)/shard_map/ppermute | solution.py:745
  151.5 24.0 %collective-permute-start.27 = (bf16[2,4,48,768]{3,2,1,0:T(8,128)(2,1)}, bf16[2,4,48,768]{3,2,1,0:T(8,128)(2,1)}, u32[]{:S(2)}, u32[]{:S(2)}) collective-permute-start(bf16[2,4,48,768]{3,2,1,0:T(8,128)(2,1)} %get-tuple-element.139.refs_10_.refs_0_.refs_4_.refs_9_), channel_id=1, source_target_pairs={{0,2},{1,3},{2,0},{3,1},{4,6},{5,7},{6,4},{7,5},{8,10},{9,11},{10,... | collective-permute-start | bytes 1769480 | tf_op jit(solution)/shard_map/ppermute | solution.py:748
  152.7 25.5 %collective-permute-start.29 = (bf16[2,4,48,768]{3,2,1,0:T(8,128)(2,1)}, bf16[2,4,48,768]{3,2,1,0:T(8,128)(2,1)}, u32[]{:S(2)}, u32[]{:S(2)}) collective-permute-start(bf16[2,4,48,768]{3,2,1,0:T(8,128)(2,1)} %get-tuple-element.144.refs_0_.refs_5_.refs_9_.refs_4_), channel_id=1, source_target_pairs={{0,2},{1,3},{2,0},{3,1},{4,6},{5,7},{6,4},{7,5},{8,10},{9,11},{10,... | collective-permute-start | bytes 1769480 | tf_op jit(solution)/shard_map/ppermute | solution.py:748
  153.5 24.6 %collective-permute-start.30 = (bf16[2,4,48,768]{3,2,1,0:T(8,128)(2,1)}, bf16[2,4,48,768]{3,2,1,0:T(8,128)(2,1)}, u32[]{:S(2)}, u32[]{:S(2)}) collective-permute-start(bf16[2,4,48,768]{3,2,1,0:T(8,128)(2,1)} %get-tuple-element.145.refs_2_.refs_8_.refs_12_.refs_7_), channel_id=1, source_target_pairs={{0,4},{4,0},{8,12},{12,8},{16,20},{20,16},{24,28},{28,24},{1,5},{5... | collective-permute-start | bytes 1769480 | tf_op jit(solution)/shard_map/ppermute | solution.py:745
  184.8 30.6 %collective-permute-start.35 = (bf16[2,1,2,48,768]{4,3,2,1,0:T(8,128)(2,1)}, bf16[2,1,2,48,768]{4,3,2,1,0:T(8,128)(2,1)}, u32[]{:S(2)}, u32[]{:S(2)}) collective-permute-start(bf16[2,1,2,48,768]{4,3,2,1,0:T(8,128)(2,1)} %get-tuple-element.150.refs_1_), channel_id=1, source_target_pairs={{0,16},{4,20},{8,24},{12,28},{16,0},{20,4},{24,8},{28,12},{1,17},{... | collective-permute-start | bytes 884744 | tf_op jit(solution)/shard_map/ppermute | solution.py:742
  185.1 30.2 %collective-permute-start.36 = (bf16[2,1,2,48,768]{4,3,2,1,0:T(8,128)(2,1)}, bf16[2,1,2,48,768]{4,3,2,1,0:T(8,128)(2,1)}, u32[]{:S(2)}, u32[]{:S(2)}) collective-permute-start(bf16[2,1,2,48,768]{4,3,2,1,0:T(8,128)(2,1)} %get-tuple-element.151.refs_3_), channel_id=1, source_target_pairs={{0,16},{4,20},{8,24},{12,28},{16,0},{20,4},{24,8},{28,12},{1,17},{... | collective-permute-start | bytes 884744 | tf_op jit(solution)/shard_map/ppermute | solution.py:742
  214.8 22.2 %collective-permute-start.38 = (bf16[2,2,2,4,48,768]{5,4,3,2,1,0:T(8,128)(2,1)}, bf16[2,2,2,4,48,768]{5,4,3,2,1,0:T(8,128)(2,1)}, u32[]{:S(2)}, u32[]{:S(2)}) collective-permute-start(bf16[2,2,2,4,48,768]{5,4,3,2,1,0:T(8,128)(2,1)} %get-tuple-element.162), channel_id=1, source_target_pairs={{0,1},{1,0},{2,3},{3,2},{4,5},{5,4},{6,7},{7,6},{8,9},{9,8},{10,11... | collective-permute-start | bytes 7077896 | tf_op jit(solution)/shard_map/ppermute | solution.py:751
  261.7 30.0 %collective-permute-start.42 = (bf16[2,2,2,4,48,768]{5,4,3,2,1,0:T(8,128)(2,1)}, bf16[2,2,2,4,48,768]{5,4,3,2,1,0:T(8,128)(2,1)}, u32[]{:S(2)}, u32[]{:S(2)}) collective-permute-start(bf16[2,2,2,4,48,768]{5,4,3,2,1,0:T(8,128)(2,1)} %get-tuple-element.171), channel_id=1, source_target_pairs={{0,1},{1,0},{2,3},{3,2},{4,5},{5,4},{6,7},{7,6},{8,9},{9,8},{10,11... | collective-permute-start | bytes 7077896 | tf_op jit(solution)/shard_map/ppermute | solution.py:751
  268.0 23.7 %collective-permute-start.45 = (bf16[2,2,2,4,48,768]{5,4,3,2,1,0:T(8,128)(2,1)}, bf16[2,2,2,4,48,768]{5,4,3,2,1,0:T(8,128)(2,1)}, u32[]{:S(2)}, u32[]{:S(2)}) collective-permute-start(bf16[2,2,2,4,48,768]{5,4,3,2,1,0:T(8,128)(2,1)} %get-tuple-element.176), channel_id=1, source_target_pairs={{0,1},{1,0},{2,3},{3,2},{4,5},{5,4},{6,7},{7,6},{8,9},{9,8},{10,11... | collective-permute-start | bytes 7077896 | tf_op jit(solution)/shard_map/ppermute | solution.py:751
  268.6 23.1 %collective-permute-start.43 = (bf16[576,768]{1,0:T(8,128)(2,1)}, bf16[576,768]{1,0:T(8,128)(2,1)}, u32[]{:S(2)}, u32[]{:S(2)}) collective-permute-start(bf16[576,768]{1,0:T(8,128)(2,1)} %get-tuple-element.172.refs_3_), channel_id=1, source_target_pairs={{0,4},{4,0},{8,12},{12,8},{16,20},{20,16},{24,28},{28,24},{1,5},{5... | collective-permute-start | bytes 2654216 | tf_op jit(solution)/shard_map/ppermute | solution.py:745
  270.0 21.7 %collective-permute-start.44 = (bf16[576,768]{1,0:T(8,128)(2,1)}, bf16[576,768]{1,0:T(8,128)(2,1)}, u32[]{:S(2)}, u32[]{:S(2)}) collective-permute-start(bf16[576,768]{1,0:T(8,128)(2,1)} %get-tuple-element.173), channel_id=1, source_target_pairs={{0,2},{1,3},{2,0},{3,1},{4,6},{5,7},{6,4},{7,5},{8,10},{9,11},{10,... | collective-permute-start | bytes 2654216 | tf_op jit(solution)/shard_map/ppermute | solution.py:748
  298.1 35.7 %collective-permute-start.48 = (bf16[2,2,2,4,48,768]{5,4,3,2,1,0:T(8,128)(2,1)}, bf16[2,2,2,4,48,768]{5,4,3,2,1,0:T(8,128)(2,1)}, u32[]{:S(2)}, u32[]{:S(2)}) collective-permute-start(bf16[2,2,2,4,48,768]{5,4,3,2,1,0:T(8,128)(2,1)} %get-tuple-element.185), channel_id=1, source_target_pairs={{0,1},{1,0},{2,3},{3,2},{4,5},{5,4},{6,7},{7,6},{8,9},{9,8},{10,11... | collective-permute-start | bytes 7077896 | tf_op jit(solution)/shard_map/ppermute | solution.py:751
  298.2 35.0 %collective-permute-start.47 = (bf16[960,768]{1,0:T(8,128)(2,1)}, bf16[960,768]{1,0:T(8,128)(2,1)}, u32[]{:S(2)}, u32[]{:S(2)}) collective-permute-start(bf16[960,768]{1,0:T(8,128)(2,1)} %get-tuple-element.183), channel_id=1, source_target_pairs={{0,2},{1,3},{2,0},{3,1},{4,6},{5,7},{6,4},{7,5},{8,10},{9,11},{10,... | collective-permute-start | bytes 4423688 | tf_op jit(solution)/shard_map/ppermute | solution.py:748
  299.1 34.7 %collective-permute-start.46 = (bf16[960,768]{1,0:T(8,128)(2,1)}, bf16[960,768]{1,0:T(8,128)(2,1)}, u32[]{:S(2)}, u32[]{:S(2)}) collective-permute-start(bf16[960,768]{1,0:T(8,128)(2,1)} %get-tuple-element.182.refs_19_), channel_id=1, source_target_pairs={{0,4},{4,0},{8,12},{12,8},{16,20},{20,16},{24,28},{28,24},{1,5},{5... | collective-permute-start | bytes 4423688 | tf_op jit(solution)/shard_map/ppermute | solution.py:745
  339.9 29.7 %collective-permute-start.51 = (bf16[2,2,2,4,64,768]{5,4,3,2,1,0:T(8,128)(2,1)}, bf16[2,2,2,4,64,768]{5,4,3,2,1,0:T(8,128)(2,1)}, u32[]{:S(2)}, u32[]{:S(2)}) collective-permute-start(bf16[2,2,2,4,64,768]{5,4,3,2,1,0:T(8,128)(2,1)} %get-tuple-element.204), channel_id=1, source_target_pairs={{0,1},{1,0},{2,3},{3,2},{4,5},{5,4},{6,7},{7,6},{8,9},{9,8},{10,11... | collective-permute-start | bytes 9437192 | tf_op jit(solution)/shard_map/ppermute | solution.py:751
  339.9 28.7 %collective-permute-start.53 = (bf16[768,768]{1,0:T(8,128)(2,1)}, bf16[768,768]{1,0:T(8,128)(2,1)}, u32[]{:S(2)}, u32[]{:S(2)}) collective-permute-start(bf16[768,768]{1,0:T(8,128)(2,1)} %get-tuple-element.205), channel_id=1, source_target_pairs={{0,2},{1,3},{2,0},{3,1},{4,6},{5,7},{6,4},{7,5},{8,10},{9,11},{10,... | collective-permute-start | bytes 3538952 | tf_op jit(solution)/shard_map/ppermute | solution.py:748
  341.2 28.4 %collective-permute-start.52 = (bf16[768,768]{1,0:T(8,128)(2,1)}, bf16[768,768]{1,0:T(8,128)(2,1)}, u32[]{:S(2)}, u32[]{:S(2)}) collective-permute-start(bf16[768,768]{1,0:T(8,128)(2,1)} %get-tuple-element.199.refs_13_), channel_id=1, source_target_pairs={{0,4},{4,0},{8,12},{12,8},{16,20},{20,16},{24,28},{28,24},{1,5},{5... | collective-permute-start | bytes 3538952 | tf_op jit(solution)/shard_map/ppermute | solution.py:745
  376.4 25.5 %collective-permute-start.55 = (bf16[704,768]{1,0:T(8,128)(2,1)}, bf16[704,768]{1,0:T(8,128)(2,1)}, u32[]{:S(2)}, u32[]{:S(2)}) collective-permute-start(bf16[704,768]{1,0:T(8,128)(2,1)} %get-tuple-element.207), channel_id=1, source_target_pairs={{0,2},{1,3},{2,0},{3,1},{4,6},{5,7},{6,4},{7,5},{8,10},{9,11},{10,... | collective-permute-start | bytes 3244040 | tf_op jit(solution)/shard_map/ppermute | solution.py:748
  377.4 25.1 %collective-permute-start.54 = (bf16[704,768]{1,0:T(8,128)(2,1)}, bf16[704,768]{1,0:T(8,128)(2,1)}, u32[]{:S(2)}, u32[]{:S(2)}) collective-permute-start(bf16[704,768]{1,0:T(8,128)(2,1)} %get-tuple-element.206.refs_9_), channel_id=1, source_target_pairs={{0,4},{4,0},{8,12},{12,8},{16,20},{20,16},{24,28},{28,24},{1,5},{5... | collective-permute-start | bytes 3244040 | tf_op jit(solution)/shard_map/ppermute | solution.py:745
  378.6 22.1 %collective-permute-start.57 = (bf16[192,768]{1,0:T(8,128)(2,1)}, bf16[192,768]{1,0:T(8,128)(2,1)}, u32[]{:S(2)}, u32[]{:S(2)}) collective-permute-start(bf16[192,768]{1,0:T(8,128)(2,1)} %get-tuple-element.209), channel_id=1, source_target_pairs={{0,16},{4,20},{8,24},{12,28},{16,0},{20,4},{24,8},{28,12},{1,17},{... | collective-permute-start | bytes 884744 | tf_op jit(solution)/shard_map/ppermute | solution.py:739
  379.4 21.2 %collective-permute-start.58 = (bf16[192,768]{1,0:T(8,128)(2,1)}, bf16[192,768]{1,0:T(8,128)(2,1)}, u32[]{:S(2)}, u32[]{:S(2)}) collective-permute-start(bf16[192,768]{1,0:T(8,128)(2,1)} %get-tuple-element.210), channel_id=1, source_target_pairs={{0,24},{4,28},{8,0},{12,4},{16,8},{20,12},{24,16},{28,20},{1,25},{... | collective-permute-start | bytes 884744 | tf_op jit(solution)/shard_map/ppermute | solution.py:739
  426.8 23.8 %collective-permute-start.64 = (bf16[192,768]{1,0:T(8,128)(2,1)}, bf16[192,768]{1,0:T(8,128)(2,1)}, u32[]{:S(2)}, u32[]{:S(2)}) collective-permute-start(bf16[192,768]{1,0:T(8,128)(2,1)} %get-tuple-element.216), channel_id=1, source_target_pairs={{0,8},{4,12},{8,0},{12,4},{16,24},{20,28},{24,16},{28,20},{1,9},{5... | collective-permute-start | bytes 884744 | tf_op jit(solution)/shard_map/ppermute | solution.py:742
  (63 other events, 717.0 us)

commit v4 on v3

--- a/solution.py
+++ b/solution.py
@@ -558,10 +558,12 @@
         deps += self.held
         carried = self.carrying
         self.held, self.carrying = [], []
+        parts = {i: v[1] for i, v in enumerate(args) if isinstance(v, tuple)}
+        args = [v[0] if isinstance(v, tuple) else v for v in args]
         n, k, m, q = len(args), len(deps), len(carried), len(out_shape)
         lazy_in = [i for i, v in enumerate(in_specs) if v is LAZY]
         lazy_out = [i for i, v in enumerate(out_specs) if v is LAZY]
-        lazy_scratch = [pltpu.VMEM(args[i].shape, args[i].dtype) for i in lazy_in]
+        lazy_scratch = [pltpu.VMEM(args[i].shape[i in parts :], args[i].dtype) for i in lazy_in]
         lazy_scratch += [pltpu.VMEM(out_shape[i].shape, out_shape[i].dtype) for i in lazy_out]
         if lazy_scratch:
             lazy_scratch.append(pltpu.SemaphoreType.DMA((len(lazy_scratch),)))
@@ -573,6 +575,8 @@
             near = rest[len(scratch) :]
             made = []
             for j, (group, i) in enumerate([(ins, i) for i in lazy_in] + [(outs, i) for i in lazy_out]):
+                if group is ins and i in parts:
+                    group[i] = group[i].at[parts[i]]
                 made.append(Lazy(group[i], near[j], near[-1].at[j], group is outs))
                 group[i] = made[-1]
             kernel(*ins, *outs, *rest[: len(scratch)])
@@ -600,7 +604,7 @@
 WBYTES = D * FF * 2
 
 
-def call_attn_fwd(seq, plan, scal, x, vec, pbias, pieces, m):
+def call_attn_fwd(seq, plan, scal, x, vec, pbias, pieces, m, weight=1.0):
     pieces, find = flat(pieces)
     n = len(pieces)
     return seq(
@@ -610,13 +614,13 @@
         [LAZY] * 6,
         (scal, x, vec, pbias, *pieces),
         [WA, pltpu.SemaphoreType.DMA((32,))],
-        cost_estimate=cost(2 * T * D * FF * 6, WBYTES + 8e6),
+        cost_estimate=cost(weight * 2 * T * D * FF * 6, weight * WBYTES),
         name="attn_fwd",
         mib=64,
     )
 
 
-def call_ff_fwd(seq, plan, scal, x1, vec, hid, pieces, mb, mc):
+def call_ff_fwd(seq, plan, scal, x1, vec, hid, pieces, mb, mc, weight=1.0):
     pieces, find = flat(pieces)
     n = len(pieces)
     return seq(
@@ -626,7 +630,7 @@
         [LAZY] * 5,
         (scal, x1, vec, hid, *pieces),
         [WA, WC, pltpu.SemaphoreType.DMA((48,))],
-        cost_estimate=cost(2 * T * D * FF * 6, 2 * WBYTES + 8e6),
+        cost_estimate=cost(weight * 2 * T * D * FF * 6, weight * 2 * WBYTES),
         name="ff_fwd",
         mib=64,
     )
@@ -705,7 +709,7 @@
     return res[:3], res[3:]
 
 
-def call_attn_bwd(seq, plan, scal, dx1, x, a1, un, p, o, a2, vec, pieces, m, others):
+def call_attn_bwd(seq, plan, scal, dx1, x, a1, un, p, o, a2, vec, pieces, m, others, weight=1.0):
     pieces, find = flat(pieces)
     n = len(pieces)
     fold = len(others) > 0
@@ -718,7 +722,7 @@
         [LAZY] * 2 + [ANY] * len(g),
         (scal, dx1, x, a1, un, p, o, a2, vec, *others, *pieces),
         [WA, WC, pltpu.VMEM((T, FF), BF), pltpu.VMEM((T, 1024), BF), pltpu.VMEM((T, D), BF), *vblk, pltpu.SemaphoreType.DMA((64,))],
-        cost_estimate=cost(2 * T * D * FF * 8, 2 * WBYTES + 8e6),
+        cost_estimate=cost(weight * 2 * T * D * FF * 8, weight * (2 * WBYTES + 8e6)),
         name="attn_bwd",
         mib=64,
     )
@@ -768,20 +772,39 @@
 
 
 def pack_bc_rows(l, w1, w2, out, first, second):
-    t = w2[l].T
+    t = w2[l]
     for i, at in enumerate((first, second)):
         out[at : at + 48] = w1[l, 48 * i : 48 * i + 48]
         for j in range(2):
             out[at + 48 : at + 96, 384 * j : 384 * j + 384] = t[96 * j + 48 * i : 96 * j + 48 * i + 48]
 
 
-def pack_vec_kernel(w1, w2, ng, bi, hg, hb, out):
+def pack_bc_kernel(l, w1, w2, out):
+    pack_bc_rows(l, w1, w2, out, 0, 96)
+
+
+def pack_bc(seq, l, w1, w2):
+    return seq(
+        functools.partial(pack_bc_kernel, l),
+        [S((192, D), BF)],
+        [VMEM] * 2,
+        [VMEM],
+        (w1, w2),
+        cost_estimate=cost(0, 4 * 192 * D),
+        name="pack_bc",
+    )[0]
+
+
+def pack_ab_kernel(l, wqkv, wo, w1, ng, bi, hg, hb, out):
     def column(v, u, w, first):
         v = jnp.concatenate([v.astype(F32), u.astype(F32)], axis=0)
         parts = [jnp.zeros((first, w), F32)] if first else []
         return jnp.concatenate(parts + [v, jnp.zeros((VROWS - first - v.shape[0], w), F32)], axis=0)
 
-    pack_bc_rows(0, w1, w2, out, 0, 112)
+    a = jnp.concatenate([wqkv[l], wo[l]], axis=1)
+    for i in range(2):
+        out[112 * i : 112 * i + 48] = a[48 * i : 48 * i + 48]
+        out[112 * i + 48 : 112 * i + 96] = w1[l, 48 * i : 48 * i + 48]
     low = [column(ng[i], bi[i], 96, 0) for i in range(LAYERS)]
     hid = [column(hg[i], hb[i], 384, HROW) for i in range(LAYERS)]
     low = jnp.concatenate(low + [jnp.zeros((VROWS, 576), F32)], axis=1)
@@ -789,39 +812,20 @@
     out[208:224] = jnp.zeros((VROWS, D), BF)
 
 
-def pack_vec(seq, w1, w2, vectors):
-    return seq(
-        pack_vec_kernel,
-        [S((224, D), BF)],
-        [VMEM] * 6,
-        [VMEM],
-        (w1, w2, *vectors),
-        cost_estimate=cost(0, 4 * 224 * D),
-        name="pack_vec",
-    )[0]
-
-
-def pack_ab_kernel(l, wqkv, wo, w1, out):
-    a = jnp.concatenate([wqkv[l], wo[l]], axis=1)
-    for i in range(2):
-        out[96 * i : 96 * i + 48] = a[48 * i : 48 * i + 48]
-        out[96 * i + 48 : 96 * i + 96] = w1[l, 48 * i : 48 * i + 48]
-
-
-def pack_ab(seq, l, weights):
+def pack_ab(seq, l, weights, vectors):
     return seq(
         functools.partial(pack_ab_kernel, l),
-        [S((192, D), BF)],
-        [VMEM] * 3,
+        [S((224, D), BF)],
+        [VMEM] * 7,
         [VMEM],
-        weights,
-        cost_estimate=cost(0, 4 * 192 * D),
+        (*weights, *vectors),
+        cost_estimate=cost(0, 4 * 224 * D),
         name="pack_ab",
     )[0]
 
 
 def pack_c_kernel(l, w2, o1, o2):
-    t = w2[l].T
+    t = w2[l]
     for i, out in enumerate((o1, o2)):
         for j in range(2):
             out[:, 384 * j : 384 * j + 384] = t[96 * j + 48 * i : 96 * j + 48 * i + 48]
@@ -879,45 +883,6 @@
         name="zquad",
         mib=64,
     )[0]
-
-
-def pile_vec_kernel(scal, h1, x1, h2, y2, o1, o2, own, *outs):
-    for i, (out, parts) in enumerate(((o1, (h1, x1)), (o2, (h2, y2)))):
-        for k, part in enumerate(parts):
-            out[k] = part[...]
-            own[i, k] = part[...]
-    for l in range(LAYERS):
-        low, high = [], []
-        for z in range(4):
-            for x in range(2):
-                rows = o1[lax.rem(scal[3] + x, 2), z, 96:112].astype(F32)
-                low.append(rows[:, 96 * l : 96 * l + 96])
-                high.append(rows[:, 384 * l : 384 * l + 384])
-        vec = jnp.concatenate(low, axis=1)
-        outs[3 * l][...] = vec
-        outs[3 * l + 1][...] = jnp.concatenate(high, axis=1)
-        bias = jnp.concatenate([vec[BQ : BQ + 1], jnp.zeros((1, D), F32), vec[BV : BV + 1]], axis=1)
-        parts = [bias[:, 576 * f : 576 * f + 512] for f in range(4)]
-        for f in range(4):
-            parts += [bias[:, 576 * f + 512 : 576 * f + 576], jnp.zeros((1, 64), F32)]
-        outs[3 * l + 2][...] = jnp.concatenate(parts, axis=1)
-
-
-def pile_vec(seq, scal, parts):
-    rows = parts[0].shape[1]
-    outs = [S((2, 4, rows, D), BF)] * 2 + [S((2, 2, 4, rows, D), BF)]
-    outs += [S((VROWS, D), F32), S((VROWS, FF), F32), S((1, 2560), F32)] * LAYERS
-    res = seq(
-        pile_vec_kernel,
-        outs,
-        [SMEM] + [VMEM] * 4,
-        [VMEM] * len(outs),
-        (scal, *parts),
-        cost_estimate=cost(0, 120 * rows * D),
-        name="pile_vec",
-        mib=64,
-    )
-    return res[:2], res[2], res[3::3], res[4::3], res[5::3]
 
 
 def zcat_kernel(r1, scal, *refs):
@@ -947,33 +912,72 @@
     )
 
 
-def pile_kernel(cuts, scal, h1, x1, h2, y2, *refs):
-    outs = refs[-2 * len(cuts) :] if len(refs) == 2 * len(cuts) else refs[2 : 2 + 2 * len(cuts)]
+def pile_kernel(cuts, h1, x1, h2, y2, *outs):
     for i, (first, rows) in enumerate(cuts):
         mine = pl.ds(first, rows)
         for j, parts in enumerate(((h1, x1), (h2, y2))):
             for k, part in enumerate(parts):
                 outs[2 * i + j][k] = part[:, mine]
-    if len(refs) > 2 * len(cuts):
-        low = lax.rem(scal[2], 2)
-        for (first, rows), out in zip(Q_CUTS, refs[2 + 2 * len(cuts) :]):
-            out[low] = refs[0][first : first + rows]
-            out[1 - low] = refs[1][first : first + rows]
-
-
-def pile(seq, scal, parts, cuts, pair=()):
+                if len(outs) > 2 * len(cuts):
+                    outs[-1][j, k] = part[:, mine]
+
+
+def pile(seq, parts, cuts, again=False):
     outs = [S((2, 4, rows, D), BF) for _, rows in cuts for _ in range(2)]
-    if pair:
-        outs += [S((2, rows, *pair[0].shape[1:]), BF) for _, rows in Q_CUTS]
+    if again:
+        outs.append(S((2, *outs[0].shape), BF))
     return seq(
         functools.partial(pile_kernel, cuts),
         outs,
-        [SMEM] + [VMEM] * (4 + len(pair)),
+        [VMEM] * 4,
         [VMEM] * len(outs),
-        (scal, *parts, *pair),
+        parts,
         cost_estimate=cost(0, 64 * sum(rows for _, rows in cuts) * D),
         name="pile",
     )
+
+
+def pile_last_kernel(cuts, scal, h1, x1, h2, y2, q, q_got, *refs):
+    n = 2 * len(cuts)
+    pile_kernel(cuts, h1, x1, h2, y2, *refs[:n])
+    low = lax.rem(scal[2], 2)
+    for (first, rows), out in zip(Q_CUTS, refs[n:]):
+        out[low] = q[first : first + rows]
+        out[1 - low] = q_got[first : first + rows]
+    vecs, hids, biases = refs[-3:]
+    own = lax.convert_element_type(scal[3] == 0, F32)
+    for l in range(LAYERS):
+        low, high = [], []
+        for z in range(4):
+            mine, other = h1[z, 96:112].astype(F32), x1[z, 96:112].astype(F32)
+            for rows in (own * mine + (1 - own) * other, own * other + (1 - own) * mine):
+                low.append(rows[:, 96 * l : 96 * l + 96])
+                high.append(rows[:, 384 * l : 384 * l + 384])
+        vec = jnp.concatenate(low, axis=1)
+        vecs[l] = vec
+        hids[l] = jnp.concatenate(high, axis=1)
+        bias = jnp.concatenate([vec[BQ : BQ + 1], jnp.zeros((1, D), F32), vec[BV : BV + 1]], axis=1)
+        parts = [bias[:, 576 * f : 576 * f + 512] for f in range(4)]
+        for f in range(4):
+            parts += [bias[:, 576 * f + 512 : 576 * f + 576], jnp.zeros((1, 64), F32)]
+        biases[l] = jnp.concatenate(parts, axis=1)
+
+
+def pile_last(seq, scal, parts, cuts, q, q_got):
+    outs = [S((2, 4, rows, D), BF) for _, rows in cuts for _ in range(2)]
+    outs += [S((2, rows, *q.shape[1:]), BF) for _, rows in Q_CUTS]
+    outs += [S((LAYERS, VROWS, D), F32), S((LAYERS, VROWS, FF), F32), S((LAYERS, 1, 2560), F32)]
+    res = seq(
+        functools.partial(pile_last_kernel, cuts),
+        outs,
+        [SMEM] + [VMEM] * 6,
+        [VMEM] * len(outs),
+        (scal, *parts, q, q_got),
+        cost_estimate=cost(0, 64 * sum(rows for _, rows in cuts) * D),
+        name="pile_last",
+    )
+    n = 2 * len(cuts)
+    return res[:n], res[n : n + 3], *([(v, l) for l in range(LAYERS)] for v in res[n + 3 :])
 
 
 def merge_kernel(*refs):
@@ -1049,30 +1053,37 @@
 
 
 def finish_kernel(scal, *refs):
-    last = refs[4]
-    in_out, out_out, up_out, down_out, vec_out = refs[17:]
+    in_out, out_out, up_out, down_out, gain_out, bias_out, hgain_out, hbias_out = refs[14:]
     i = lax.rem(scal[2], 2)
-    b1, c1 = (total([refs[2 * k][i], refs[2 * k + 1][i], last[96 * k : 96 * k + 96]]) for k in range(2))
-    both = total([r[...] for r in refs[5:9]])
-    b0 = total([r[...] for r in refs[9:13]])
-    rows_a = total([r[...] for r in refs[13:17]])
-    vec_out[0:VROWS] = rows_a[48:64]
-    vec_out[VROWS:] = rows_a[112:128]
+    c1 = total([refs[0][i], refs[1][i], refs[4][0:96]])
+    ba1 = total([refs[2][i], refs[3][i], refs[4][96:288]])
+    c0 = total([refs[5][i], refs[6][i], refs[4][288:384]])
+    b0 = total([refs[7][i], refs[8][i], refs[9][...]])
+    rows_a = total([r[...] for r in refs[10:14]])
+    for l in range(LAYERS):
+        for r in range(3):
+            gain_out[r, l : l + 1] = rows_a[48 + r : 49 + r, 96 * l : 96 * l + 96]
+        for r in range(7):
+            bias_out[r, l : l + 1] = rows_a[51 + r : 52 + r, 96 * l : 96 * l + 96]
+        hid = rows_a[112 + HROW : 115 + HROW, 384 * l : 384 * l + 384]
+        hgain_out[0, l : l + 1] = hid[0:1]
+        hbias_out[0, l : l + 1] = hid[1:2]
+        hbias_out[1, l : l + 1] = hid[2:3]
     a0 = jnp.concatenate([rows_a[:48], rows_a[64:112]], axis=0)
-    for l, a, b, c in ((0, a0, b0, both[96:]), (1, both[:96], b1, c1)):
+    for l, a, b, c in ((0, a0, b0, c0), (1, ba1[96:], ba1[:96], c1)):
         in_out[l] = a[:, :576]
         out_out[l] = a[:, 576:]
         up_out[l] = b
         for j in range(2):
-            down_out[l, :, 96 * j : 96 * j + 96] = c[:, 384 * j : 384 * j + 384].T
+            down_out[l, 96 * j : 96 * j + 96] = c[:, 384 * j : 384 * j + 384]
 
 
 def finish(seq, scal, parts):
     return seq(
         finish_kernel,
-        [S((2, 96, 576), F32), S((2, 96, 192), F32), S((2, 96, D), F32), S((2, 384, 192), F32), S((2 * VROWS, D), F32)],
+        [S((2, 96, 576), F32), S((2, 96, 192), F32), S((2, 96, D), F32), S((2, 192, 384), F32), S((3, 2, 96), F32), S((7, 2, 96), F32), S((1, 2, 384), F32), S((2, 2, 384), F32)],
         [SMEM] + [VMEM] * len(parts),
-        [VMEM] * 5,
+        [VMEM] * 8,
         (scal, *parts),
         cost_estimate=cost(0, 8e6),
         name="finish",
@@ -1149,17 +1160,21 @@
             sources += [(a, sent(self.at1), False), (b, sent(self.at2), False)]
             sums.add(out, where(h * n, n), sources, n)
 
-    def third_pair(self, sums):
-        outs = [sums.out(2, 2 * self.rows) for _ in range(2)]
-        for k in (1, 0):
-            for i in range(2):
-
-                def z(scal, k=k, i=i):
-                    high = scal[2] // 2
-                    return 2 * (1 - high if k else high) + i
-
-                self.block(sums, outs[k], lambda first, n, i=i: lambda scal: (i, pl.ds(first, n)), z)
-        return outs
+
+def third_pair(sums, *chunks):
+    outs = [sums.out(2, sum(2 * c.rows for c in chunks)) for _ in range(2)]
+    for k in (1, 0):
+        for i in range(2):
+
+            def z(scal, k=k, i=i):
+                high = scal[2] // 2
+                return 2 * (1 - high if k else high) + i
+
+            at = 0
+            for c in chunks:
+                c.block(sums, outs[k], lambda first, n, i=i, at=at: lambda scal: (i, pl.ds(at + first, n)), z)
+                at += 2 * c.rows
+    return outs
 
 
 def third_direct(sums, *chunks):
@@ -1193,6 +1208,8 @@
     place = jnp.stack([dpi // ring.X, xme, fi // 2, fi % 2]).astype(jnp.int32)
     scal = jnp.concatenate([lengths[0], place, jnp.zeros((2,), jnp.int32)])
 
+    down_weight = down_weight.transpose(0, 2, 1)
+
     a, b, c, d = (Gather(seq, ring, scal) for _ in range(4))
     a.z_all(pack_a(seq, 0, in_projection, out_projection))
     q1, q2 = pack_c(seq, 1, down_weight)
@@ -1200,31 +1217,30 @@
     q1_got, q2_got = ring.y(q1), ring.x(q2)
     seq.hold(q1_got, q2_got)
     a.xy_first()
-    b.z_all(pack_vec(seq, up_weight, down_weight, (norm_gains, biases, hidden_gains, hidden_biases)))
-    cd = pack_ab(seq, 1, (in_projection, out_projection, up_weight))
+    b.z_all(pack_bc(seq, 0, up_weight, down_weight))
+    cd = pack_ab(seq, 1, (in_projection, out_projection, up_weight), (norm_gains, biases, hidden_gains, hidden_biases))
     seq.hold(b.parts[1])
-    a.xy_second(*pile(seq, scal, a.both, ((0, 48),)))
+    a.xy_second(*pile(seq, a.both, ((0, 48),)))
     seq.hold(a.y1, a.x2)
     b.xy_first()
     c.z_all(cd)
     q = merge(seq, q1, q1_got, q2, q2_got)
     seq.hold(a.core(), c.parts[3])
-    h, own, vecs, hids, pb = pile_vec(seq, scal, b.both)
+    *h, own = pile(seq, b.both, ((0, 96),), True)
     b.xy_second(*h)
     b.own = ring.c(own)
     kept = [None, None]
     x = inputs
-    x1, a1, un, p, o, a2 = call_attn_fwd(seq, plan, scal, x, vecs[0], pb[0], a.pieces(), 0)
     seq.hold(b.y1, b.x2, b.own)
     rest = ring.c(c.xy_first(b.y1, b.x2))
     b.other = [(b.own, 0), (rest, 0), (b.own, 1), (rest, 1)]
     seq.hold(rest)
-    h = pile(seq, scal, c.both, ((0, 48), (48, 48)), (q, ring.z_xor(q, 1)))
+    h, parts_q, vecs, hids, pb = pile_last(seq, scal, c.both, ((0, 48), (48, 48)), q, ring.z_xor(q, 1))
     c.xy_second(*h[:2])
-    d.xy_second(*h[2:4])
-    parts_q = h[4:]
+    d.xy_second(*h[2:])
+    x1, a1, un, p, o, a2 = call_attn_fwd(seq, plan, scal, x, vecs[0], pb[0], a.pieces(), 0, 0.01)
     got_q = [ring.z_xor(v, 2) for v in parts_q]
-    x2, a3, sl, n4, a4 = call_ff_fwd(seq, plan, scal, x1, vecs[0], hids[0], b.pieces(), 0, 1)
+    x2, a3, sl, n4, a4 = call_ff_fwd(seq, plan, scal, x1, vecs[0], hids[0], b.pieces(), 0, 1, 0.01)
     kept[0] = (x, x1, a1, un, p, o, a2, a3, sl, n4, a4)
     x = x2
     seq.hold(d.y1, d.x2, got_q[0])
@@ -1254,81 +1270,96 @@
     sa = Scatter(ring, grads)
 
     sums = Sums(scal)
-    outs = sums.out(576), sums.out(576)
-    sc.second(sums, *outs)
-    sb.first(sums, *outs, 192)
+    sc.second(sums, sums.out(192), sums.out(192))
     seq.carry(sa.send)
-    u, v = sums.run(seq, "sums_2")
+    u, v = sums.run(seq, "sums_2a")
     sa.core(*seq.carried)
-    sb.x1st, sb.y1st = sc.x2nd, sc.y2nd = ring.x(u), ring.y(v)
+    sc.x2nd, sc.y2nd = ring.x(u), ring.y(v)
 
     x, x1, a1, un, p, o, a2, a3, sl, n4, a4 = kept[0]
     s3 = Scatter(ring, call_down_grad(seq, plan, scal, dy, a4))
-    s3.core(s3.send)
+
+    sums = Sums(scal)
+    outs = sums.out(768), sums.out(768)
+    sb.first(sums, *outs)
+    sa.first(sums, *outs, 384)
+    third_pair(sums, sc)
+    seq.carry(s3.send)
+    u, v, keep_c, send = sums.run(seq, "sums_2b")
+    got_c = ring.z_xor(send, 2)
+    s3.core(*seq.carried)
+    sb.x1st, sb.y1st = sa.x1st, sa.y1st = ring.x(u), ring.y(v)
+
     (dx1, gva0, gh0), grads = call_ff_bwd(seq, plan, scal, dy, x1, a3, sl, n4, a4, vecs[0], hids[0], b.pieces(), 0, 1, False, False)
     s4 = Scatter(ring, grads)
 
     sums = Sums(scal)
-    outs = sums.out(960), sums.out(960)
+    outs = sums.out(384), sums.out(384)
     sb.second(sums, *outs)
-    sa.first(sums, *outs, 192)
-    s3.first(sums, *outs, 576)
-    sc.third_pair(sums)
+    sa.second(sums, *outs, 192)
+    s3.first(sums, sums.out(384), sums.out(384))
+    seq.hold(got_c)
     seq.carry(s4.send)
-    u, v, keep_c, send = sums.run(seq, "sums_3")
+    u, v, u3, v3 = sums.run(seq, "sums_3")
     s4.core(*seq.carried)
-    sa.x1st, sa.y1st = sb.x2nd, sb.y2nd = s3.x1st, s3.y1st = ring.x(u), ring.y(v)
-    got_c = ring.z_xor(send, 2)
+    sb.x2nd, sb.y2nd = sa.x2nd, sa.y2nd = ring.x(u), ring.y(v)
+    s3.x1st, s3.y1st = ring.x(u3), ring.y(v3)
 
     others = (gva0, gva1, gvb1, gh0, gh1)
-    (input_gradient, _), grads = call_attn_bwd(seq, plan, scal, dx1, x, a1, un, p, o, a2, vecs[0], a.pieces(), 0, others)
+    (input_gradient, _), grads = call_attn_bwd(seq, plan, scal, dx1, x, a1, un, p, o, a2, vecs[0], a.pieces(), 0, others, 0.01)
     s5 = Scatter(ring, grads)
 
     sums = Sums(scal)
-    outs = sums.out(768), sums.out(768)
-    sa.second(sums, *outs)
-    s3.second(sums, *outs, 192)
-    s4.first(sums, *outs, 384)
-    sb.third_pair(sums)
-    seq.hold(got_c)
+    third_pair(sums, sb, sa)
+    keep_ba, send = sums.run(seq, "sums_4a")
+    got_ba = ring.z_xor(send, 2)
+
+    sums = Sums(scal)
+    outs = sums.out(576), sums.out(576)
+    s3.second(sums, *outs)
+    s4.first(sums, *outs, 192)
     seq.carry(s5.send)
-    u, v, keep_b, send = sums.run(seq, "sums_4")
+    u, v = sums.run(seq, "sums_4b")
     s5.core(*seq.carried)
-    s4.x1st, s4.y1st = sa.x2nd, sa.y2nd = s3.x2nd, s3.y2nd = ring.x(u), ring.y(v)
-    got_b = ring.z_xor(send, 2)
+    s4.x1st, s4.y1st = s3.x2nd, s3.y2nd = ring.x(u), ring.y(v)
     outputs = call_ff_out(seq, plan, scal, x1_last, a4_last, vecs[1], pieces, 0)
 
     sums = Sums(scal)
-    outs = sums.out(704), sums.out(704)
-    s4.second(sums, *outs)
-    s5.first(sums, *outs, 192)
-    third_direct(sums, sa, s3)
-    seq.hold(got_b)
-    u, v, *res = sums.run(seq, "sums_5")
-    s4.x2nd, s4.y2nd = s5.x1st, s5.y1st = ring.x(u), ring.y(v)
-    parts1 = [res[0]] + [ring.z(res[k], k) for k in (1, 2, 3)]
+    s5.first(sums, sums.out(512), sums.out(512))
+    u, v = sums.run(seq, "sums_4c")
+    s5.x1st, s5.y1st = ring.x(u), ring.y(v)
+
+    sums = Sums(scal)
+    s4.second(sums, sums.out(192), sums.out(192))
+    third_pair(sums, s3)
+    seq.hold(got_ba)
+    u, v, keep_c0, send = sums.run(seq, "sums_5")
+    s4.x2nd, s4.y2nd = ring.x(u), ring.y(v)
+    got_c0 = ring.z_xor(send, 2)
 
     sums = Sums(scal)
     s5.second(sums, sums.out(256), sums.out(256))
-    third_direct(sums, s4)
-    seq.hold(*parts1[1:])
-    u, v, *res = sums.run(seq, "sums_6")
+    third_pair(sums, s4)
+    out = sums.out(384)
+    fourth(sums, out, 0, keep_c, got_c)
+    fourth(sums, out, 96, keep_ba, got_ba)
+    fourth(sums, out, 288, keep_c0, got_c0)
+    u, v, keep_b0, send, last1 = sums.run(seq, "sums_6")
     s5.x2nd, s5.y2nd = ring.x(u), ring.y(v)
-    parts2 = [res[0]] + [ring.z(res[k], k) for k in (1, 2, 3)]
+    got_b0 = ring.z_xor(send, 2)
+    last1 = ring.z_xor(last1, 1)
 
     sums = Sums(scal)
     third_direct(sums, s5)
-    out = sums.out(192)
-    fourth(sums, out, 0, keep_b, got_b)
-    fourth(sums, out, 96, keep_c, got_c)
-    seq.hold(*parts2[1:])
-    res = sums.run(seq, "sums_7")
-    parts3 = [res[0]] + [ring.z(res[k], k) for k in (1, 2, 3)]
-    last = ring.z_xor(res[4], 1)
-    g_in, g_out, g_up, g_down, vrows = finish(seq, scal, [keep_b, got_b, keep_c, got_c, last, *parts1, *parts2, *parts3])
-    gv = jnp.stack([vrows[:10, :96], vrows[:10, 96:192]])
-    gh = jnp.stack([vrows[26:29, :384], vrows[26:29, 384:]])
-    return outputs, input_gradient, g_in, g_out, g_up, g_down, gv[:, :3], gv[:, 3:], gh[:, :1], gh[:, 1:]
+    out = sums.out(96)
+    fourth(sums, out, 0, keep_b0, got_b0)
+    seq.hold(last1)
+    *parts, last0 = sums.run(seq, "sums_7")
+    parts = parts[:1] + [ring.z(parts[k], k) for k in (1, 2, 3)]
+    last0 = ring.z_xor(last0, 1)
+    grads = finish(seq, scal, [keep_c, got_c, keep_ba, got_ba, last1, keep_c0, got_c0, keep_b0, got_b0, last0, *parts])
+    down, *rows = grads[3:]
+    return outputs, input_gradient, *grads[:3], down.transpose(0, 2, 1), *(v.transpose(1, 0, 2) for v in rows)
 
 
 def whole_shards(inputs, lengths, in_projection, out_projection, up_weight, down_weight, norm_gains, biases, hidden_gains, hidden_biases, cotangent):

time: 470 us -> 441 us (0.938)
  waiting for transfers between devices: 186 us -> 170 us
  local copies, waits for them, and re-layouts: 21 us -> 12.8 us
    ppermute x7 -> x10, waiting for transfers between devices: 31.9 us -> 69.8 us  [z_xor(): return lax.ppermute(v, 'dp', [(i, i ^ k * self.X) for i in range(self.dp)])]
    ppermute x15 -> x18, waiting for transfers between devices: 52.7 us -> 25.4 us  [y(): return lax.ppermute(v, 'fsdp', [(i, i ^ 2) for i in range(self.fsdp)])]
    ppermute x18 -> x12, waiting for transfers between devices: 85.5 us -> 63.8 us  [z(): lax.ppermute(v, 'dp', [(z * self.X + x, (z + k) % self.Z * self.X + x) fo...]
    ppermute x18 -> x12, starting transfers between devices: 31.8 us -> 19.1 us  [z(): lax.ppermute(v, 'dp', [(z * self.X + x, (z + k) % self.Z * self.X + x) fo...]
    unnamed x61 -> x59, local copies, waits for them, and re-layouts: 18.7 us -> 12.1 us
    ppermute x15 -> x18, starting transfers between devices: 14 us -> 18.4 us  [y(): return lax.ppermute(v, 'fsdp', [(i, i ^ 2) for i in range(self.fsdp)])]
    ppermute x15 -> x18, waiting for transfers between devices: 10.4 us -> 6.13 us  [x(): return lax.ppermute(v, 'dp', [(i, i ^ 1) for i in range(self.dp)])]
    ppermute x15 -> x18, starting transfers between devices: 14.8 us -> 18.8 us  [x(): return lax.ppermute(v, 'dp', [(i, i ^ 1) for i in range(self.dp)])]
  transfers between devices with their start and end apart: 68 -> 71, of which waited for: 33 -> 30; matrix products, arithmetic and copies ran while one was open for 1% -> 0% of each run, Pallas kernels for 27% -> 33%
where the time goes in v4:
time: 441 us; the launch traced here: 432 us
  Pallas kernels  178 us (40%)
  waiting for transfers between devices  170 us (39%)
  starting transfers between devices  69.5 us (16%)
  local copies, waits for them, and re-layouts  12.8 us (3%)
    pallas_call x38, Pallas kernels, __call__(): pl.pallas_call(body, out_shape=tuple(out_shape) + tuple((S(v.shape, v.dty...  178 us
    ppermute x10, waiting for transfers between devices, z_xor(): return lax.ppermute(v, 'dp', [(i, i ^ k * self.X) for i in range(self.dp)])  69.8 us
    ppermute x12, waiting for transfers between devices, z(): lax.ppermute(v, 'dp', [(z * self.X + x, (z + k) % self.Z * self.X + x) fo...  63.8 us
    ppermute x18, waiting for transfers between devices, y(): return lax.ppermute(v, 'fsdp', [(i, i ^ 2) for i in range(self.fsdp)])  25.4 us
    ppermute x12, starting transfers between devices, z(): lax.ppermute(v, 'dp', [(z * self.X + x, (z + k) % self.Z * self.X + x) fo...  19.1 us
    ppermute x18, starting transfers between devices, x(): return lax.ppermute(v, 'dp', [(i, i ^ 1) for i in range(self.dp)])  18.8 us
    ppermute x18, starting transfers between devices, y(): return lax.ppermute(v, 'fsdp', [(i, i ^ 2) for i in range(self.fsdp)])  18.4 us
    unnamed x59, local copies, waits for them, and re-layouts  12.1 us
  transfers between devices with their start and end apart: 71, of which 30 were waited for; matrix products, arithmetic and copies ran while one was open for 0% of the time, Pallas kernels for 33%

profile of v4, /device:TPU:0, one launch (start us, length us, event | category | flops | bytes accessed | tf_op | source)
XLA Modules:
  0.0 432.0 jit_solution(9967663391443200132)
XLA Ops:
  16.1 7.7 %collective-permute-done.1.refs_3_ = bf16[96,768]{1,0:T(8,128)(2,1)S(1)} collective-permute-done((bf16[96,768]{1,0:T(8,128)(2,1)S(1)}, bf16[96,768]{1,0:T(8,128)(2,1)S(1)}, u32[]{:S(2)}, u32[]{:S(2)}) %collective-permute-start.1) | collective-permute-done | bytes 147488 | tf_op jit(solution)/shard_map/ppermute | solution.py:743
  27.4 8.3 %collective-permute-done.10.refs_5_.refs_2_ = bf16[192,768]{1,0:T(8,128)(2,1)S(1)} collective-permute-done((bf16[192,768]{1,0:T(8,128)(2,1)S(1)}, bf16[192,768]{1,0:T(8,128)(2,1)S(1)}, u32[]{:S(2)}, u32[]{:S(2)}) %collective-permute-start.10) | collective-permute-done | bytes 294944 | tf_op jit(solution)/shard_map/ppermute | solution.py:743
  40.4 6.6 %collective-permute-done.12.refs_4_ = bf16[192,768]{1,0:T(8,128)(2,1)S(1)} collective-permute-done((bf16[192,768]{1,0:T(8,128)(2,1)S(1)}, bf16[192,768]{1,0:T(8,128)(2,1)S(1)}, u32[]{:S(2)}, u32[]{:S(2)}) %collective-permute-start.12) | collective-permute-done | bytes 294944 | tf_op jit(solution)/shard_map/ppermute | solution.py:743
  47.0 10.1 %collective-permute-done.11.refs_3_ = bf16[192,768]{1,0:T(8,128)(2,1)S(1)} collective-permute-done((bf16[192,768]{1,0:T(8,128)(2,1)S(1)}, bf16[192,768]{1,0:T(8,128)(2,1)S(1)}, u32[]{:S(2)}, u32[]{:S(2)}) %collective-permute-start.11) | collective-permute-done | bytes 294944 | tf_op jit(solution)/shard_map/ppermute | solution.py:743
  63.2 7.4 %collective-permute-done.9.refs_6_.refs_4_ = bf16[224,768]{1,0:T(8,128)(2,1)S(1)} collective-permute-done((bf16[224,768]{1,0:T(8,128)(2,1)S(1)}, bf16[224,768]{1,0:T(8,128)(2,1)S(1)}, u32[]{:S(2)}, u32[]{:S(2)}) %collective-permute-start.9) | collective-permute-done | bytes 344096 | tf_op jit(solution)/shard_map/ppermute | solution.py:743
  82.1 22.3 %collective-permute-done.8.refs_3_ = bf16[224,768]{1,0:T(8,128)(2,1)S(1)} collective-permute-done((bf16[224,768]{1,0:T(8,128)(2,1)S(1)}, bf16[224,768]{1,0:T(8,128)(2,1)S(1)}, u32[]{:S(2)}, u32[]{:S(2)}) %collective-permute-start.8) | collective-permute-done | bytes 344096 | tf_op jit(solution)/shard_map/ppermute | solution.py:743
  109.5 15.2 %collective-permute-done.25.refs_6_ = bf16[4,2,48,768]{3,2,1,0:T(8,128)(2,1)S(1)} collective-permute-done((bf16[4,2,48,768]{3,2,1,0:T(8,128)(2,1)S(1)}, bf16[4,2,48,768]{3,2,1,0:T(8,128)(2,1)S(1)}, u32[]{:S(2)}, u32[]{:S(2)}) %collective-permute-start.25) | collective-permute-done | bytes 589856 | tf_op jit(solution)/shard_map/ppermute | solution.py:746
  134.8 9.7 %attn_fwd.2 = (f32[256,768]{1,0:T(8,128)}, bf16[256,768]{1,0:T(8,128)(2,1)}, bf16[36,256,64]{2,1,0:T(8,128)(2,1)}, f32[12,256,256]{2,1,0:T(8,128)}, f32[256,768]{1,0:T(8,128)}, /*index=5*/bf16[256,768]{1,0:T(8,128)(2,1)}) custom-call(s32[8]{0:T(128)} %copy-done.21, f32[256,768]{1,0:T(8,128)} %refs_2_.5, f32[2,16,768]{2,1,0:T(8,128)} %copy-done.10, ...), custom_call_target="tpu_custom_call" | custom-call | flops 72477576 | bytes 47185 | tf_op jit(solution)/shard_map/attn_fwd/pallas_call | solution.py:586
  144.6 12.8 %ff_fwd.1 = (f32[256,768]{1,0:T(8,128)}, bf16[256,768]{1,0:T(8,128)(2,1)}, f32[256,3072]{1,0:T(8,128)}, f32[256,3072]{1,0:T(8,128)}, bf16[256,3072]{1,0:T(8,128)(2,1)}) custom-call(s32[8]{0:T(128)} %copy-done.21, f32[256,768]{1,0:T(8,128)} %get-tuple-element.142.refs_1_.refs_10_.refs_2_, f32[2,16,768]{2,1,0:T(8,128)} %copy-done.10, ...), custom_call_target="tpu_custom_call" | custom-call | flops 72477576 | bytes 94371 | tf_op jit(solution)/shard_map/ff_fwd/pallas_call | solution.py:586
  168.7 9.9 %attn_fwd.3 = (f32[256,768]{1,0:T(8,128)}, bf16[256,768]{1,0:T(8,128)(2,1)}, bf16[36,256,64]{2,1,0:T(8,128)(2,1)}, f32[12,256,256]{2,1,0:T(8,128)}, f32[256,768]{1,0:T(8,128)}, /*index=5*/bf16[256,768]{1,0:T(8,128)(2,1)}) custom-call(s32[8]{0:T(128)} %copy-done.21, f32[256,768]{1,0:T(8,128)} %get-tuple-element.144.refs_4_.refs_1_.refs_2_, ...), custom_call_target="tpu_custom_call" | custom-call | flops 7247757312 | bytes 4718592 | tf_op jit(solution)/shard_map/attn_fwd/pallas_call | solution.py:586
  181.0 13.3 %ff_mid.1 = (bf16[256,768]{1,0:T(8,128)(2,1)}, f32[256,3072]{1,0:T(8,128)}, f32[256,3072]{1,0:T(8,128)}, bf16[256,3072]{1,0:T(8,128)(2,1)}, bf16[2,2,2,4,48,768]...) custom-call(s32[8]{0:T(128)} %copy-done.21, f32[256,768]{1,0:T(8,128)} %get-tuple-element.149.refs_3_.refs_1_.refs_2_, ...), custom_call_target="tpu_custom_call" | custom-call | flops 7247757312 | bytes 17437184 | tf_op jit(solution)/shard_map/ff_mid/pallas_call | solution.py:586
  202.6 13.8 %ff_bwd.2 = (f32[256,768]{1,0:T(8,128)}, f32[16,768]{1,0:T(8,128)}, f32[16,3072]{1,0:T(8,128)}, bf16[2,2,2,4,48,768]{5,4,3,2,1,0:T(8,128)(2,1)}, bf16[2,2,2,4,48,768]{5,4,3,2,1,0:T(8,128)(2,1)}) custom-call(s32[8]{0:T(128)} %copy-done.21, f32[256,768]{1,0:T(8,128)} %refs_1_.7, f32[256,768]{1,0:T(8,128)} %get-tuple-element.149.refs_3_.refs_1_.refs_2_, ...), custom_call_target="tpu_custom_call" | custom-call | flops 9663676416 | bytes 26874368 | tf_op jit(solution)/shard_map/ff_bwd/pallas_call | solution.py:586
  222.0 15.8 %attn_bwd.2 = (f32[256,768]{1,0:T(8,128)}, f32[16,768]{1,0:T(8,128)}, bf16[2,2,2,4,48,768]{5,4,3,2,1,0:T(8,128)(2,1)}, bf16[2,2,2,4,48,768]{5,4,3,2,1,0:T(8,128)(2,1)}) custom-call(s32[8]{0:T(128)} %copy-done.21, f32[256,768]{1,0:T(8,128)} %get-tuple-element.156.refs_3_.refs_1_, f32[256,768]{1,0:T(8,128)} %get-tuple-element.144.refs_4_.refs_1_.refs_2_, ...), custom_call_target="tpu_custom_call" | custom-call | flops 9663676416 | bytes 17437184 | tf_op jit(solution)/shard_map/attn_bwd/pallas_call | solution.py:586
  243.1 6.2 %ff_down_grad.1 = (bf16[2,2,2,4,48,768]{5,4,3,2,1,0:T(8,128)(2,1)}, bf16[2,2,2,4,48,768]{5,4,3,2,1,0:T(8,128)(2,1)}) custom-call(s32[8]{0:T(128)} %copy-done.21, f32[256,768]{1,0:T(8,128)} %get-tuple-element.166.refs_5_.refs_1_, bf16[256,3072]{1,0:T(8,128)(2,1)} %get-tuple-element.167.refs_2_.refs_6_, bf16[192,768]{1,0:T(8,128)(2,1)} %get-tuple-element.170.refs_3_), custom_call_target="tpu_custom_call" | custom-call | flops 1207959552 | bytes 7718592 | tf_op jit(solution)/shard_map/ff_down_grad/pallas_call | solution.py:586
  251.0 5.7 %sums_2b.1 = (bf16[768,768]{1,0:T(8,128)(2,1)}, bf16[768,768]{1,0:T(8,128)(2,1)}, bf16[2,96,768]{2,1,0:T(8,128)(2,1)}, bf16[2,96,768]{2,1,0:T(8,128)(2,1)}, bf16[2,2,2,4,48,768]{5,4,3,2,1,0:T(8,128)(2,1)}) custom-call(s32[8]{0:T(128)} %copy-done.21, bf16[2,2,2,4,48,768]{5,4,3,2,1,0:T(8,128)(2,1)} %get-tuple-element.172.refs_1_, ...), custom_call_target="tpu_custom_call", output_to_operand_aliasing={{4}: (12, {})} | custom-call | bytes 10027008 | tf_op jit(solution)/shard_map/sums_2b/pallas_call | solution.py:586
  261.8 13.4 %ff_bwd.3 = (f32[256,768]{1,0:T(8,128)}, f32[16,768]{1,0:T(8,128)}, f32[16,3072]{1,0:T(8,128)}, bf16[2,2,2,4,48,768]{5,4,3,2,1,0:T(8,128)(2,1)}, bf16[2,2,2,4,48,768]{5,4,3,2,1,0:T(8,128)(2,1)}) custom-call(s32[8]{0:T(128)} %copy-done.21, f32[256,768]{1,0:T(8,128)} %get-tuple-element.166.refs_5_.refs_1_, ...), custom_call_target="tpu_custom_call" | custom-call | flops 9663676416 | bytes 26874368 | tf_op jit(solution)/shard_map/ff_bwd/pallas_call | solution.py:586
  275.5 10.0 %collective-permute-done.47.refs_4_.refs_5_ = bf16[768,768]{1,0:T(8,128)(2,1)} collective-permute-done((bf16[768,768]{1,0:T(8,128)(2,1)}, bf16[768,768]{1,0:T(8,128)(2,1)}, u32[]{:S(2)}, u32[]{:S(2)}) %collective-permute-start.47) | collective-permute-done | bytes 1179680 | tf_op jit(solution)/shard_map/ppermute | solution.py:752
  286.7 4.7 %sums_3.1 = (bf16[384,768]{1,0:T(8,128)(2,1)}, bf16[384,768]{1,0:T(8,128)(2,1)}, bf16[384,768]{1,0:T(8,128)(2,1)}, bf16[384,768]{1,0:T(8,128)(2,1)}, bf16[2,2,2,4,48,768]{5,4,3,2,1,0:T(8,128)(2,1)}) custom-call(s32[8]{0:T(128)} %copy-done.21, bf16[2,2,2,4,48,768]{5,4,3,2,1,0:T(8,128)(2,1)} %get-tuple-element.172.refs_1_, ...), custom_call_target="tpu_custom_call", output_to_operand_aliasing={{4}: (11, {})} | custom-call | bytes 8257536 | tf_op jit(solution)/shard_map/sums_3/pallas_call | solution.py:586
  295.6 16.4 %attn_bwd.3 = (f32[256,768]{1,0:T(8,128)}, f32[16,768]{1,0:T(8,128)}, bf16[2,2,2,4,64,768]{5,4,3,2,1,0:T(8,128)(2,1)}, bf16[2,2,2,4,64,768]{5,4,3,2,1,0:T(8,128)(2,1)}) custom-call(s32[8]{0:T(128)} %copy-done.21, f32[256,768]{1,0:T(8,128)} %get-tuple-element.184.refs_9_.refs_1_, f32[256,768]{1,0:T(8,128)} %refs_2_.5, ...), custom_call_target="tpu_custom_call" | custom-call | flops 96636768 | bytes 174371 | tf_op jit(solution)/shard_map/attn_bwd/pallas_call | solution.py:586
  312.0 4.7 %sums_4a.1 = (bf16[2,192,768]{2,1,0:T(8,128)(2,1)}, bf16[2,192,768]{2,1,0:T(8,128)(2,1)}) custom-call(s32[8]{0:T(128)} %copy-done.21, bf16[2,2,2,4,48,768]{5,4,3,2,1,0:T(8,128)(2,1)} %get-tuple-element.172.refs_1_, bf16[2,2,2,4,48,768]{5,4,3,2,1,0:T(8,128)(2,1)} %collective-permute-done.41.refs_2_, bf16[768,768]{1,0:T(8,128)(2,1)} %collective-permute-done.46.refs_3_, ...), custom_call_target="tpu_custom_call" | custom-call | bytes 5898240 | tf_op jit(solution)/shard_map/sums_4a/pallas_call | solution.py:586
  316.7 3.8 collective-permute-done.49.refs_3_.refs_7_
  320.4 3.8 sums_4b.1
  329.3 6.5 %ff_out.1.refs_3_ = f32[256,768]{1,0:T(8,128)} custom-call(s32[8]{0:T(128)} %copy-done.21, f32[256,768]{1,0:T(8,128)} %get-tuple-element.149.refs_3_.refs_1_.refs_2_, bf16[256,3072]{1,0:T(8,128)(2,1)} %get-tuple-element.150.refs_6_.refs_2_, f32[2,16,768]{2,1,0:T(8,128)} %copy-done.10, ...), custom_call_target="tpu_custom_call" | custom-call | flops 3623878656 | bytes 7718592 | tf_op jit(solution)/shard_map/ff_out/pallas_call | solution.py:586
  340.6 15.1 %collective-permute-done.54.refs_10_.refs_14_.refs_4_ = bf16[2,192,768]{2,1,0:T(8,128)(2,1)} collective-permute-done((bf16[2,192,768]{2,1,0:T(8,128)(2,1)}, bf16[2,192,768]{2,1,0:T(8,128)(2,1)}, u32[]{:S(2)}, u32[]{:S(2)}) %collective-permute-start.54) | collective-permute-done | bytes 589856 | tf_op jit(solution)/shard_map/ppermute | solution.py:746
  355.7 3.9 sums_5.1
  361.4 8.5 %collective-permute-done.60.refs_8_ = bf16[192,768]{1,0:T(8,128)(2,1)} collective-permute-done((bf16[192,768]{1,0:T(8,128)(2,1)}, bf16[192,768]{1,0:T(8,128)(2,1)}, u32[]{:S(2)}, u32[]{:S(2)}) %collective-permute-start.60) | collective-permute-done | bytes 294944 | tf_op jit(solution)/shard_map/ppermute | solution.py:752
  369.9 5.7 %collective-permute-done.62.refs_16_.refs_7_ = bf16[2,96,768]{2,1,0:T(8,128)(2,1)} collective-permute-done((bf16[2,96,768]{2,1,0:T(8,128)(2,1)}, bf16[2,96,768]{2,1,0:T(8,128)(2,1)}, u32[]{:S(2)}, u32[]{:S(2)}) %collective-permute-start.62) | collective-permute-done | bytes 294944 | tf_op jit(solution)/shard_map/ppermute | solution.py:746
  375.6 5.0 %sums_6.1 = (bf16[256,768]{1,0:T(8,128)(2,1)}, bf16[256,768]{1,0:T(8,128)(2,1)}, bf16[2,96,768]{2,1,0:T(8,128)(2,1)}, bf16[2,96,768]{2,1,0:T(8,128)(2,1)}, bf16[384,768]{1,0:T(8,128)(2,1)}) custom-call(s32[8]{0:T(128)} %copy-done.21, bf16[2,2,2,4,64,768]{5,4,3,2,1,0:T(8,128)(2,1)} %get-tuple-element.209.refs_1_, ...), custom_call_target="tpu_custom_call" | custom-call | bytes 7864320 | tf_op jit(solution)/shard_map/sums_6/pallas_call | solution.py:586
  384.8 15.5 %collective-permute-done.64.refs_8_.refs_9_ = bf16[2,96,768]{2,1,0:T(8,128)(2,1)} collective-permute-done((bf16[2,96,768]{2,1,0:T(8,128)(2,1)}, bf16[2,96,768]{2,1,0:T(8,128)(2,1)}, u32[]{:S(2)}, u32[]{:S(2)}) %collective-permute-start.64) | collective-permute-done | bytes 294944 | tf_op jit(solution)/shard_map/ppermute | solution.py:746
  402.6 3.8 sums_7.1
  410.8 14.6 %collective-permute-done.67.refs_10_ = bf16[96,768]{1,0:T(8,128)(2,1)} collective-permute-done((bf16[96,768]{1,0:T(8,128)(2,1)}, bf16[96,768]{1,0:T(8,128)(2,1)}, u32[]{:S(2)}, u32[]{:S(2)}) %collective-permute-start.67) | collective-permute-done | bytes 147488 | tf_op jit(solution)/shard_map/ppermute | solution.py:746
  425.4 3.6 finish.1
  (209 shorter events, 126.5 us)
Async XLA Ops:
  35.8 21.3 %collective-permute-start.16 = (bf16[2,4,48,768]{3,2,1,0:T(8,128)(2,1)S(1)}, bf16[2,4,48,768]{3,2,1,0:T(8,128)(2,1)S(1)}, u32[]{:S(2)}, u32[]{:S(2)}) collective-permute-start(bf16[2,4,48,768]{3,2,1,0:T(8,128)(2,1)S(1)} %get-tuple-element.130.refs_2_.refs_7_.refs_17_), channel_id=1, source_target_pairs={{0,4},{4,0},{8,12},{12,8},{16,20},{20,16},{24,28},{28,24},{1,5},{5... | collective-permute-start | bytes 1769480 | tf_op jit(solution)/shard_map/ppermute | solution.py:749
  36.4 20.7 %collective-permute-start.15 = (bf16[2,4,48,768]{3,2,1,0:T(8,128)(2,1)S(1)}, bf16[2,4,48,768]{3,2,1,0:T(8,128)(2,1)S(1)}, u32[]{:S(2)}, u32[]{:S(2)}) collective-permute-start(bf16[2,4,48,768]{3,2,1,0:T(8,128)(2,1)S(1)} %get-tuple-element.129.refs_5_.refs_0_.refs_4_.refs_14_), channel_id=1, source_target_pairs={{0,2},{1,3},{2,0},{3,1},{4,6},{5,7},{6,4},{7,5},{8,10},{9,11},{10,... | collective-permute-start | bytes 1769480 | tf_op jit(solution)/shard_map/ppermute | solution.py:752
  75.9 29.6 %collective-permute-start.22 = (bf16[2,2,4,96,768]{4,3,2,1,0:T(8,128)(2,1)S(1)}, bf16[2,2,4,96,768]{4,3,2,1,0:T(8,128)(2,1)S(1)}, u32[]{:S(2)}, u32[]{:S(2)}) collective-permute-start(bf16[2,2,4,96,768]{4,3,2,1,0:T(8,128)(2,1)S(1)} %get-tuple-element.135), channel_id=1, source_target_pairs={{0,1},{1,0},{2,3},{3,2},{4,5},{5,4},{6,7},{7,6},{8,9},{9,8},{10,11... | collective-permute-start | bytes 7077896 | tf_op jit(solution)/shard_map/ppermute | solution.py:755
  75.9 28.5 %collective-permute-start.21 = (bf16[2,4,96,768]{3,2,1,0:T(8,128)(2,1)S(1)}, bf16[2,4,96,768]{3,2,1,0:T(8,128)(2,1)S(1)}, u32[]{:S(2)}, u32[]{:S(2)}) collective-permute-start(bf16[2,4,96,768]{3,2,1,0:T(8,128)(2,1)S(1)} %get-tuple-element.134.refs_8_.refs_13_), channel_id=1, source_target_pairs={{0,4},{4,0},{8,12},{12,8},{16,20},{20,16},{24,28},{28,24},{1,5},{5... | collective-permute-start | bytes 3538952 | tf_op jit(solution)/shard_map/ppermute | solution.py:749
  77.4 28.1 %collective-permute-start.20 = (bf16[2,4,96,768]{3,2,1,0:T(8,128)(2,1)S(1)}, bf16[2,4,96,768]{3,2,1,0:T(8,128)(2,1)S(1)}, u32[]{:S(2)}, u32[]{:S(2)}) collective-permute-start(bf16[2,4,96,768]{3,2,1,0:T(8,128)(2,1)S(1)} %get-tuple-element.133.refs_7_.refs_4_.refs_9_), channel_id=1, source_target_pairs={{0,2},{1,3},{2,0},{3,1},{4,6},{5,7},{6,4},{7,5},{8,10},{9,11},{10,... | collective-permute-start | bytes 3538952 | tf_op jit(solution)/shard_map/ppermute | solution.py:752
  78.9 25.6 %collective-permute-start.8 = (bf16[224,768]{1,0:T(8,128)(2,1)S(1)}, bf16[224,768]{1,0:T(8,128)(2,1)S(1)}, u32[]{:S(2)}, u32[]{:S(2)}) collective-permute-start(bf16[224,768]{1,0:T(8,128)(2,1)S(1)} %pack_ab.1.refs_4_.refs_1_), channel_id=1, source_target_pairs={{0,16},{4,20},{8,24},{12,28},{16,0},{20,4},{24,8},{28,12},{1,17},{... | collective-permute-start | bytes 1032200 | tf_op jit(solution)/shard_map/ppermute | solution.py:743
  78.9 25.6 %collective-permute-start.7 = (bf16[224,768]{1,0:T(8,128)(2,1)S(1)}, bf16[224,768]{1,0:T(8,128)(2,1)S(1)}, u32[]{:S(2)}, u32[]{:S(2)}) collective-permute-start(bf16[224,768]{1,0:T(8,128)(2,1)S(1)} %pack_ab.1.refs_4_.refs_1_), channel_id=1, source_target_pairs={{0,8},{4,12},{8,16},{12,20},{16,24},{20,28},{24,0},{28,4},{1,9},{5... | collective-permute-start | bytes 1032200 | tf_op jit(solution)/shard_map/ppermute | solution.py:743
  130.1 28.5 %collective-permute-start.31 = (bf16[2,2,2,48,768]{4,3,2,1,0:T(8,128)(2,1)}, bf16[2,2,2,48,768]{4,3,2,1,0:T(8,128)(2,1)}, u32[]{:S(2)}, u32[]{:S(2)}) collective-permute-start(bf16[2,2,2,48,768]{4,3,2,1,0:T(8,128)(2,1)} %get-tuple-element.148.refs_1_), channel_id=1, source_target_pairs={{0,16},{4,20},{8,24},{12,28},{16,0},{20,4},{24,8},{28,12},{1,17},{... | collective-permute-start | bytes 1769480 | tf_op jit(solution)/shard_map/ppermute | solution.py:746
  130.8 27.9 %collective-permute-start.28 = (bf16[2,4,48,768]{3,2,1,0:T(8,128)(2,1)}, bf16[2,4,48,768]{3,2,1,0:T(8,128)(2,1)}, u32[]{:S(2)}, u32[]{:S(2)}) collective-permute-start(bf16[2,4,48,768]{3,2,1,0:T(8,128)(2,1)} %get-tuple-element.145.refs_2_.refs_7_.refs_12_), channel_id=1, source_target_pairs={{0,4},{4,0},{8,12},{12,8},{16,20},{20,16},{24,28},{28,24},{1,5},{5... | collective-permute-start | bytes 1769480 | tf_op jit(solution)/shard_map/ppermute | solution.py:749
  132.2 26.5 %collective-permute-start.27 = (bf16[2,4,48,768]{3,2,1,0:T(8,128)(2,1)}, bf16[2,4,48,768]{3,2,1,0:T(8,128)(2,1)}, u32[]{:S(2)}, u32[]{:S(2)}) collective-permute-start(bf16[2,4,48,768]{3,2,1,0:T(8,128)(2,1)} %get-tuple-element.141.refs_9_.refs_0_.refs_4_), channel_id=1, source_target_pairs={{0,2},{1,3},{2,0},{3,1},{4,6},{5,7},{6,4},{7,5},{8,10},{9,11},{10,... | collective-permute-start | bytes 1769480 | tf_op jit(solution)/shard_map/ppermute | solution.py:752
  133.0 26.2 %collective-permute-start.29 = (bf16[2,4,48,768]{3,2,1,0:T(8,128)(2,1)}, bf16[2,4,48,768]{3,2,1,0:T(8,128)(2,1)}, u32[]{:S(2)}, u32[]{:S(2)}) collective-permute-start(bf16[2,4,48,768]{3,2,1,0:T(8,128)(2,1)} %get-tuple-element.146.refs_0_.refs_5_.refs_9_.refs_4_), channel_id=1, source_target_pairs={{0,2},{1,3},{2,0},{3,1},{4,6},{5,7},{6,4},{7,5},{8,10},{9,11},{10,... | collective-permute-start | bytes 1769480 | tf_op jit(solution)/shard_map/ppermute | solution.py:752
  134.2 25.0 %collective-permute-start.30 = (bf16[2,4,48,768]{3,2,1,0:T(8,128)(2,1)}, bf16[2,4,48,768]{3,2,1,0:T(8,128)(2,1)}, u32[]{:S(2)}, u32[]{:S(2)}) collective-permute-start(bf16[2,4,48,768]{3,2,1,0:T(8,128)(2,1)} %get-tuple-element.147.refs_2_.refs_8_.refs_12_.refs_7_), channel_id=1, source_target_pairs={{0,4},{4,0},{8,12},{12,8},{16,20},{20,16},{24,28},{28,24},{1,5},{5... | collective-permute-start | bytes 1769480 | tf_op jit(solution)/shard_map/ppermute | solution.py:749
  165.8 29.1 %collective-permute-start.35 = (bf16[2,1,2,48,768]{4,3,2,1,0:T(8,128)(2,1)}, bf16[2,1,2,48,768]{4,3,2,1,0:T(8,128)(2,1)}, u32[]{:S(2)}, u32[]{:S(2)}) collective-permute-start(bf16[2,1,2,48,768]{4,3,2,1,0:T(8,128)(2,1)} %get-tuple-element.151.refs_1_), channel_id=1, source_target_pairs={{0,16},{4,20},{8,24},{12,28},{16,0},{20,4},{24,8},{28,12},{1,17},{... | collective-permute-start | bytes 884744 | tf_op jit(solution)/shard_map/ppermute | solution.py:746
  168.1 26.8 %collective-permute-start.36 = (bf16[2,1,2,48,768]{4,3,2,1,0:T(8,128)(2,1)}, bf16[2,1,2,48,768]{4,3,2,1,0:T(8,128)(2,1)}, u32[]{:S(2)}, u32[]{:S(2)}) collective-permute-start(bf16[2,1,2,48,768]{4,3,2,1,0:T(8,128)(2,1)} %get-tuple-element.152.refs_3_), channel_id=1, source_target_pairs={{0,16},{4,20},{8,24},{12,28},{16,0},{20,4},{24,8},{28,12},{1,17},{... | collective-permute-start | bytes 884744 | tf_op jit(solution)/shard_map/ppermute | solution.py:746
  194.3 22.2 %collective-permute-start.38 = (bf16[2,2,2,4,48,768]{5,4,3,2,1,0:T(8,128)(2,1)}, bf16[2,2,2,4,48,768]{5,4,3,2,1,0:T(8,128)(2,1)}, u32[]{:S(2)}, u32[]{:S(2)}) collective-permute-start(bf16[2,2,2,4,48,768]{5,4,3,2,1,0:T(8,128)(2,1)} %get-tuple-element.163), channel_id=1, source_target_pairs={{0,1},{1,0},{2,3},{3,2},{4,5},{5,4},{6,7},{7,6},{8,9},{9,8},{10,11... | collective-permute-start | bytes 7077896 | tf_op jit(solution)/shard_map/ppermute | solution.py:755
  222.0 29.0 %collective-permute-start.41 = (bf16[2,2,2,4,48,768]{5,4,3,2,1,0:T(8,128)(2,1)}, bf16[2,2,2,4,48,768]{5,4,3,2,1,0:T(8,128)(2,1)}, u32[]{:S(2)}, u32[]{:S(2)}) collective-permute-start(bf16[2,2,2,4,48,768]{5,4,3,2,1,0:T(8,128)(2,1)} %get-tuple-element.173), channel_id=1, source_target_pairs={{0,1},{1,0},{2,3},{3,2},{4,5},{5,4},{6,7},{7,6},{8,9},{9,8},{10,11... | collective-permute-start | bytes 7077896 | tf_op jit(solution)/shard_map/ppermute | solution.py:755
  256.7 30.0 %collective-permute-start.45 = (bf16[2,2,2,4,48,768]{5,4,3,2,1,0:T(8,128)(2,1)}, bf16[2,2,2,4,48,768]{5,4,3,2,1,0:T(8,128)(2,1)}, u32[]{:S(2)}, u32[]{:S(2)}) collective-permute-start(bf16[2,2,2,4,48,768]{5,4,3,2,1,0:T(8,128)(2,1)} %get-tuple-element.178), channel_id=1, source_target_pairs={{0,1},{1,0},{2,3},{3,2},{4,5},{5,4},{6,7},{7,6},{8,9},{9,8},{10,11... | collective-permute-start | bytes 7077896 | tf_op jit(solution)/shard_map/ppermute | solution.py:755
  256.8 28.7 %collective-permute-start.47 = (bf16[768,768]{1,0:T(8,128)(2,1)}, bf16[768,768]{1,0:T(8,128)(2,1)}, u32[]{:S(2)}, u32[]{:S(2)}) collective-permute-start(bf16[768,768]{1,0:T(8,128)(2,1)} %get-tuple-element.180), channel_id=1, source_target_pairs={{0,2},{1,3},{2,0},{3,1},{4,6},{5,7},{6,4},{7,5},{8,10},{9,11},{10,... | collective-permute-start | bytes 3538952 | tf_op jit(solution)/shard_map/ppermute | solution.py:752
  258.3 28.4 %collective-permute-start.46 = (bf16[768,768]{1,0:T(8,128)(2,1)}, bf16[768,768]{1,0:T(8,128)(2,1)}, u32[]{:S(2)}, u32[]{:S(2)}) collective-permute-start(bf16[768,768]{1,0:T(8,128)(2,1)} %get-tuple-element.179.refs_15_), channel_id=1, source_target_pairs={{0,4},{4,0},{8,12},{12,8},{16,20},{20,16},{24,28},{28,24},{1,5},{5... | collective-permute-start | bytes 3538952 | tf_op jit(solution)/shard_map/ppermute | solution.py:749
  291.4 29.1 %collective-permute-start.51 = (bf16[2,2,2,4,48,768]{5,4,3,2,1,0:T(8,128)(2,1)}, bf16[2,2,2,4,48,768]{5,4,3,2,1,0:T(8,128)(2,1)}, u32[]{:S(2)}, u32[]{:S(2)}) collective-permute-start(bf16[2,2,2,4,48,768]{5,4,3,2,1,0:T(8,128)(2,1)} %get-tuple-element.190), channel_id=1, source_target_pairs={{0,1},{1,0},{2,3},{3,2},{4,5},{5,4},{6,7},{7,6},{8,9},{9,8},{10,11... | collective-permute-start | bytes 7077896 | tf_op jit(solution)/shard_map/ppermute | solution.py:755
  291.5 20.5 %collective-permute-start.52 = (bf16[384,768]{1,0:T(8,128)(2,1)}, bf16[384,768]{1,0:T(8,128)(2,1)}, u32[]{:S(2)}, u32[]{:S(2)}) collective-permute-start(bf16[384,768]{1,0:T(8,128)(2,1)} %get-tuple-element.191), channel_id=1, source_target_pairs={{0,2},{1,3},{2,0},{3,1},{4,6},{5,7},{6,4},{7,5},{8,10},{9,11},{10,... | collective-permute-start | bytes 1769480 | tf_op jit(solution)/shard_map/ppermute | solution.py:752
  292.1 19.9 %collective-permute-start.53 = (bf16[384,768]{1,0:T(8,128)(2,1)}, bf16[384,768]{1,0:T(8,128)(2,1)}, u32[]{:S(2)}, u32[]{:S(2)}) collective-permute-start(bf16[384,768]{1,0:T(8,128)(2,1)} %get-tuple-element.192.refs_19_), channel_id=1, source_target_pairs={{0,4},{4,0},{8,12},{12,8},{16,20},{20,16},{24,28},{28,24},{1,5},{5... | collective-permute-start | bytes 1769480 | tf_op jit(solution)/shard_map/ppermute | solution.py:749
  293.3 27.2 %collective-permute-start.49 = (bf16[384,768]{1,0:T(8,128)(2,1)}, bf16[384,768]{1,0:T(8,128)(2,1)}, u32[]{:S(2)}, u32[]{:S(2)}) collective-permute-start(bf16[384,768]{1,0:T(8,128)(2,1)} %get-tuple-element.187), channel_id=1, source_target_pairs={{0,4},{4,0},{8,12},{12,8},{16,20},{20,16},{24,28},{28,24},{1,5},{5... | collective-permute-start | bytes 1769480 | tf_op jit(solution)/shard_map/ppermute | solution.py:749
  294.1 26.3 %collective-permute-start.50 = (bf16[384,768]{1,0:T(8,128)(2,1)}, bf16[384,768]{1,0:T(8,128)(2,1)}, u32[]{:S(2)}, u32[]{:S(2)}) collective-permute-start(bf16[384,768]{1,0:T(8,128)(2,1)} %get-tuple-element.188), channel_id=1, source_target_pairs={{0,2},{1,3},{2,0},{3,1},{4,6},{5,7},{6,4},{7,5},{8,10},{9,11},{10,... | collective-permute-start | bytes 1769480 | tf_op jit(solution)/shard_map/ppermute | solution.py:752
  324.3 31.3 %collective-permute-start.59 = (bf16[576,768]{1,0:T(8,128)(2,1)}, bf16[576,768]{1,0:T(8,128)(2,1)}, u32[]{:S(2)}, u32[]{:S(2)}) collective-permute-start(bf16[576,768]{1,0:T(8,128)(2,1)} %get-tuple-element.213), channel_id=1, source_target_pairs={{0,2},{1,3},{2,0},{3,1},{4,6},{5,7},{6,4},{7,5},{8,10},{9,11},{10,... | collective-permute-start | bytes 2654216 | tf_op jit(solution)/shard_map/ppermute | solution.py:752
  325.9 29.8 %collective-permute-start.58 = (bf16[576,768]{1,0:T(8,128)(2,1)}, bf16[576,768]{1,0:T(8,128)(2,1)}, u32[]{:S(2)}, u32[]{:S(2)}) collective-permute-start(bf16[576,768]{1,0:T(8,128)(2,1)} %get-tuple-element.206.refs_13_), channel_id=1, source_target_pairs={{0,4},{4,0},{8,12},{12,8},{16,20},{20,16},{24,28},{28,24},{1,5},{5... | collective-permute-start | bytes 2654216 | tf_op jit(solution)/shard_map/ppermute | solution.py:749
  326.7 29.0 %collective-permute-start.54 = (bf16[2,192,768]{2,1,0:T(8,128)(2,1)}, bf16[2,192,768]{2,1,0:T(8,128)(2,1)}, u32[]{:S(2)}, u32[]{:S(2)}) collective-permute-start(bf16[2,192,768]{2,1,0:T(8,128)(2,1)} %get-tuple-element.208), channel_id=1, source_target_pairs={{0,16},{4,20},{8,24},{12,28},{16,0},{20,4},{24,8},{28,12},{1,17},{... | collective-permute-start | bytes 1769480 | tf_op jit(solution)/shard_map/ppermute | solution.py:746
  339.3 36.3 %collective-permute-start.57 = (bf16[512,768]{1,0:T(8,128)(2,1)}, bf16[512,768]{1,0:T(8,128)(2,1)}, u32[]{:S(2)}, u32[]{:S(2)}) collective-permute-start(bf16[512,768]{1,0:T(8,128)(2,1)} %get-tuple-element.212), channel_id=1, source_target_pairs={{0,2},{1,3},{2,0},{3,1},{4,6},{5,7},{6,4},{7,5},{8,10},{9,11},{10,... | collective-permute-start | bytes 2359304 | tf_op jit(solution)/shard_map/ppermute | solution.py:752
  340.0 35.6 %collective-permute-start.56 = (bf16[512,768]{1,0:T(8,128)(2,1)}, bf16[512,768]{1,0:T(8,128)(2,1)}, u32[]{:S(2)}, u32[]{:S(2)}) collective-permute-start(bf16[512,768]{1,0:T(8,128)(2,1)} %get-tuple-element.211.refs_9_), channel_id=1, source_target_pairs={{0,4},{4,0},{8,12},{12,8},{16,20},{20,16},{24,28},{28,24},{1,5},{5... | collective-permute-start | bytes 2359304 | tf_op jit(solution)/shard_map/ppermute | solution.py:749
  380.6 22.0 %collective-permute-start.63 = (bf16[384,768]{1,0:T(8,128)(2,1)}, bf16[384,768]{1,0:T(8,128)(2,1)}, u32[]{:S(2)}, u32[]{:S(2)}) collective-permute-start(bf16[384,768]{1,0:T(8,128)(2,1)} %get-tuple-element.218), channel_id=1, source_target_pairs={{0,8},{4,12},{8,0},{12,4},{16,24},{20,28},{24,16},{28,20},{1,9},{5... | collective-permute-start | bytes 1769480 | tf_op jit(solution)/shard_map/ppermute | solution.py:746
  380.7 19.7 %collective-permute-start.65 = (bf16[256,768]{1,0:T(8,128)(2,1)}, bf16[256,768]{1,0:T(8,128)(2,1)}, u32[]{:S(2)}, u32[]{:S(2)}) collective-permute-start(bf16[256,768]{1,0:T(8,128)(2,1)} %get-tuple-element.221), channel_id=1, source_target_pairs={{0,2},{1,3},{2,0},{3,1},{4,6},{5,7},{6,4},{7,5},{8,10},{9,11},{10,... | collective-permute-start | bytes 1179656 | tf_op jit(solution)/shard_map/ppermute | solution.py:752
  406.4 19.0 %collective-permute-start.68 = (bf16[128,768]{1,0:T(8,128)(2,1)}, bf16[128,768]{1,0:T(8,128)(2,1)}, u32[]{:S(2)}, u32[]{:S(2)}) collective-permute-start(bf16[128,768]{1,0:T(8,128)(2,1)} %get-tuple-element.225), channel_id=1, source_target_pairs={{0,8},{4,12},{8,16},{12,20},{16,24},{20,28},{24,0},{28,4},{1,9},{5... | collective-permute-start | bytes 589832 | tf_op jit(solution)/shard_map/ppermute | solution.py:743
  (66 other events, 907.6 us)
